TPU v7x, 32 devices: a whole 2x2x4 slice. The times are simulated.
32 devices in a mesh: batch: 16 (over z, y, core), seq: 2 (over x).
Axes of the slice: x: 2, y: 2, z: 4, core: 2. Of those that a mesh axis runs over, the one named last changes fastest.
Arguments:
- tokens: bfloat16 [24576, 768], P(('batch', 'seq')), may hold values from -6 to 6
- lengths: int32 [16, 3], P('batch'), may hold values from 16 to 1504, as said below
- labels: int32 [48], replicated, may hold values from 0 to 47, as said below
- attention_gain: bfloat16 [768], P('batch'), may hold values from 0.5 to 1.5
- query_weight: bfloat16 [768, 768], P('batch'), may hold values from -0.02734375 to 0.02734375
- key_weight: bfloat16 [768, 768], P('batch'), may hold values from -0.21875 to 0.21875
- value_weight: bfloat16 [768, 768], P('batch'), may hold values from -0.21875 to 0.21875
- attention_out: bfloat16 [768, 768], P('batch'), may hold values from -0.875 to 0.875
- position_bias: bfloat16 [32, 12], P('batch'), may hold values from -4 to 4
- feed_gain: bfloat16 [768], P('batch'), may hold values from 0.5 to 1.5
- feed_inner: bfloat16 [768, 3072], P('batch'), may hold values from -0.21875 to 0.21875
- feed_outer: bfloat16 [3072, 768], P('batch'), may hold values from -0.109375 to 0.109375
- encoder_gain: bfloat16 [768], P('batch'), may hold values from 0.5 to 1.5
- start_token: bfloat16 [768], P('batch'), may hold values from -6 to 6
- self_gain: bfloat16 [768], P('batch'), may hold values from 0.5 to 1.5
- self_value: bfloat16 [768, 768], P('batch'), may hold values from -0.21875 to 0.21875
- self_out: bfloat16 [768, 768], P('batch'), may hold values from -0.21875 to 0.21875
- cross_gain: bfloat16 [768], P('batch'), may hold values from 0.5 to 1.5
- cross_query: bfloat16 [768, 768], P('batch'), may hold values from -0.02734375 to 0.02734375
- cross_key: bfloat16 [768, 768], P('batch'), may hold values from -0.21875 to 0.21875
- cross_value: bfloat16 [768, 768], P('batch'), may hold values from -0.21875 to 0.21875
- cross_out: bfloat16 [768, 768], P('batch'), may hold values from -0.875 to 0.875
- second_gain: bfloat16 [768], P('batch'), may hold values from 0.5 to 1.5
- second_inner: bfloat16 [768, 3072], P('batch'), may hold values from -0.21875 to 0.21875
- second_outer: bfloat16 [3072, 768], P('batch'), may hold values from -0.109375 to 0.109375
- final_gain: bfloat16 [768], P('batch'), may hold values from 0.5 to 1.5
- pooler_weight: bfloat16 [768, 768], P('batch'), may hold values from -0.21875 to 0.21875
Outputs:
- contrastive_loss: float32 [1], replicated
- embeddings: float32 [48, 768], P('batch')
- grad_tokens: float32 [24576, 768], P(('batch', 'seq'))
- grad_attention_gain: float32 [768], P('batch')
- grad_query_weight: float32 [768, 768], P('batch')
- grad_key_weight: float32 [768, 768], P('batch')
- grad_value_weight: float32 [768, 768], P('batch')
- grad_attention_out: float32 [768, 768], P('batch')
- grad_position_bias: float32 [32, 12], P('batch')
- grad_feed_gain: float32 [768], P('batch')
- grad_feed_inner: float32 [768, 3072], P('batch')
- grad_feed_outer: float32 [3072, 768], P('batch')
- grad_encoder_gain: float32 [768], P('batch')
- grad_start_token: float32 [768], P('batch')
- grad_self_gain: float32 [768], P('batch')
- grad_self_value: float32 [768, 768], P('batch')
- grad_self_out: float32 [768, 768], P('batch')
- grad_cross_gain: float32 [768], P('batch')
- grad_cross_query: float32 [768, 768], P('batch')
- grad_cross_key: float32 [768, 768], P('batch')
- grad_cross_value: float32 [768, 768], P('batch')
- grad_cross_out: float32 [768, 768], P('batch')
- grad_second_gain: float32 [768], P('batch')
- grad_second_inner: float32 [768, 3072], P('batch')
- grad_second_outer: float32 [3072, 768], P('batch')
- grad_final_gain: float32 [768], P('batch')
- grad_pooler_weight: float32 [768, 768], P('batch')
Inputs may be any that keep to these rules, and one draw needn't show every extreme that they name: `lengths`: each row lists the 3 sequences of one group in order: one query, one document, one query; each query has 16 to 128 tokens and every row sums to 1536. labels[i] is never i.
All inputs are finite; a program needn't handle non-finite values.
Results may differ from a plain program's by a relative error of at most 0.033.
Values may be sent and summed in bfloat16 or wider, within the bound.
A program may use at most 320 MiB of HBM per device.

v0:
```python
import functools
import math

import jax
import jax.numpy as jnp
from jax import lax
from jax.experimental import pallas as pl
from jax.experimental.pallas import tpu as pltpu
from jax.sharding import PartitionSpec as P

HEADS = 12
HEAD = 64
BUCKETS = 32
LANES = 128
far_apart = float(2**30)

eps_norm = 1e-06
masked_score = -1000000000.0
logit_scale = 20.0
bucket_limits = (12, 16, 23, 32, 46, 64, 91)
highest = lax.Precision.HIGHEST
low = jnp.bfloat16
wide = jnp.float32


def rms_norm(values, gain_vector):
    return (
        values
        * lax.rsqrt(jnp.mean(values * values, axis=-1, keepdims=True) + eps_norm)
        * gain_vector
    )


def unit_length(values):
    return values * lax.rsqrt(jnp.sum(values * values, axis=-1, keepdims=True) + eps_norm)


def bucket_of(offsets):
    upper_half = jnp.where(offsets > 0, 16, 0).astype(jnp.int32)
    distance = jnp.abs(offsets)
    far_bucket = 8 + sum(((distance >= threshold).astype(jnp.int32) for threshold in bucket_limits))
    return upper_half + jnp.where(distance < 8, distance, far_bucket)


def product(left_side, right_side):
    return jnp.dot(left_side, right_side, preferred_element_type=wide)


def back_product(left_side, right_side):
    return lax.dot_general(
        left_side, right_side, (((1,), (1,)), ((), ())), preferred_element_type=wide
    )


def weight_grad(left_side, right_side):
    return lax.dot_general(
        left_side, right_side, (((0,), (0,)), ((), ())), preferred_element_type=wide
    )


def norm_back(values, gain_vector, grad_rows):
    _, pullback = jax.vjp(rms_norm, values, gain_vector)
    return pullback(grad_rows)


def gelu_back(values, grad_rows):
    _, pullback = jax.vjp(jax.nn.gelu, values)
    return pullback(grad_rows)[0]


def segment_of(places, ends):
    return (places >= ends[0]).astype(jnp.int32) + (places >= ends[1]).astype(jnp.int32)


def block_rows(rows):
    return 256 if rows % 256 == 0 else rows


def table_sizes(size, pack):
    slack = LANES if size % LANES else 0
    reach = -(-(size + slack + 91) // LANES) * LANES
    lead = -(-(size + slack) // LANES) * LANES
    middle = -(-(pack - size) // LANES) * LANES
    return middle, reach, lead, middle + max(pack, reach)


def offset_biases(table, size, pack, shift):
    _, reach, lead, _ = table_sizes(size, pack)
    offsets = jnp.arange(lead + reach + LANES, dtype=jnp.int32) - (lead + LANES) - shift
    onehot = (
        bucket_of(offsets)[None, :] == jnp.arange(BUCKETS, dtype=jnp.int32)[:, None]
    ).astype(low)
    return weight_grad(table, onehot)[:, None, :]


def turned_biases(row, size, lead):
    spread = jnp.broadcast_to(row, (size, row.shape[1]))
    return pltpu.roll(spread, 0, 1, stride=1, stride_axis=0)[:, lead:]


def attend_kernel(
    place, q_ref, k_ref, v_ref, near_ref, attended_ref, total_ref, bias, key_side, value_side
):
    pair = pl.program_id(0)
    block = pl.program_id(1)
    pack = k_ref.shape[0]
    size = q_ref.shape[0]
    middle, reach, lead, width = table_sizes(size, pack)
    ends = (place[0], place[1])
    first = place[2] + block * size
    shift = place[3]

    @pl.when(block == 0)
    def _():
        places = lax.broadcasted_iota(jnp.int32, (pack, LANES), 0)
        lane = lax.broadcasted_iota(jnp.int32, (pack, LANES), 1)
        key_side[:, :LANES] = k_ref[...]
        key_side[:, LANES:] = (segment_of(places, ends) == lane).astype(wide).astype(low)
        value_side[:, :LANES] = v_ref[...]
        value_side[:, LANES:] = jnp.ones((pack, LANES), low)
        for half in range(2):
            row = near_ref[half]
            before = middle - LANES
            after = middle + reach
            bias[half, :, before:after] = turned_biases(row, size, lead)
            if before > 0:
                bias[half, :, :before] = jnp.broadcast_to(row[:, :1], (size, before))
            if after < width:
                bias[half, :, after:] = jnp.broadcast_to(row[:, -1:], (size, width - after))

    lane = lax.broadcasted_iota(jnp.int32, (size, LANES), 1)
    rows = first + lax.broadcasted_iota(jnp.int32, (size, LANES), 0)
    apart = jnp.where((segment_of(rows, ends) != lane) & (lane < 3), -far_apart, 0.0).astype(low)
    own = pl.ds(pl.multiple_of(block * size, 64), size)
    start = pl.multiple_of(middle - (first - shift), LANES)
    queries = q_ref[...]
    outputs = []
    totals = total_ref[own, :]
    for half in range(2):
        mine = (lane >= HEAD) if half else (lane < HEAD)
        query_side = jnp.concatenate(
            [jnp.where(mine, queries, jnp.zeros_like(queries)), apart], axis=1
        )
        scores = back_product(query_side, key_side[...]) + bias[half, :, pl.ds(start, pack)]
        top = jnp.max(scores, axis=1, keepdims=True)
        weights = jnp.exp(scores - top).astype(low)
        output = product(weights, value_side[...])
        total = output[:, LANES:]
        outputs.append(output[:, :LANES] / total)
        totals = jnp.where(lane == 2 * pair + half, top + jnp.log(total), totals)
    attended_ref[...] = jnp.where(lane < HEAD, outputs[0], outputs[1])
    total_ref[own, :] = totals


def attend(queries, all_keys, all_values, near, place):
    rows, width = queries.shape
    pack = all_keys.shape[0]
    size = block_rows(rows)
    _, _, _, columns = table_sizes(size, pack)
    pairs = width // LANES
    return pl.pallas_call(
        attend_kernel,
        name="attend",
        grid=(pairs, rows // size),
        in_specs=[
            pl.BlockSpec(memory_space=pltpu.SMEM),
            pl.BlockSpec((size, LANES), lambda p, i: (i, p)),
            pl.BlockSpec((pack, LANES), lambda p, i: (0, p)),
            pl.BlockSpec((pack, LANES), lambda p, i: (0, p)),
            pl.BlockSpec((2, 1, near.shape[2]), lambda p, i: (p, 0, 0)),
        ],
        out_specs=[
            pl.BlockSpec((size, LANES), lambda p, i: (i, p)),
            pl.BlockSpec((rows, LANES), lambda p, i: (0, 0)),
        ],
        out_shape=[
            jax.ShapeDtypeStruct((rows, width), wide),
            jax.ShapeDtypeStruct((rows, LANES), wide),
        ],
        scratch_shapes=[
            pltpu.VMEM((2, size, columns), wide),
            pltpu.VMEM((pack, 2 * LANES), low),
            pltpu.VMEM((pack, 2 * LANES), low),
        ],
        compiler_params=pltpu.CompilerParams(vmem_limit_bytes=48 * 2**20),
        cost_estimate=pl.CostEstimate(
            flops=8 * rows * pack * width * 2, bytes_accessed=16 * pack * width, transcendentals=0
        ),
    )(place, queries, all_keys, all_values, near)


def attend_back_kernel(
    place,
    q_ref,
    k_ref,
    v_ref,
    grad_ref,
    attended_ref,
    total_ref,
    near_ref,
    grad_q_ref,
    grad_k_ref,
    grad_v_ref,
    band_ref,
    far_ref,
    bias,
    key_side,
    value_side,
    keys_turned,
    grad_scores,
    grad_k_sum,
    grad_v_sum,
    band_sum,
):
    pair = pl.program_id(0)
    block = pl.program_id(1)
    blocks = pl.num_programs(1)
    pack = k_ref.shape[0]
    size = q_ref.shape[0]
    middle, reach, lead, width = table_sizes(size, pack)
    ends = (place[0], place[1])
    first = place[2] + block * size
    shift = place[3]

    @pl.when(block == 0)
    def _():
        places = lax.broadcasted_iota(jnp.int32, (pack, LANES), 0)
        lane = lax.broadcasted_iota(jnp.int32, (pack, LANES), 1)
        key_side[:, :LANES] = k_ref[...]
        ones = (segment_of(places, ends) == lane) | ((lane >= 3) & (lane < 9))
        key_side[:, LANES:] = ones.astype(wide).astype(low)
        value_side[:, :LANES] = v_ref[...]
        value_side[:, LANES:] = (lane < 6).astype(wide).astype(low)
        keys_turned[...] = k_ref[...].T
        for half in range(2):
            row = near_ref[half]
            before = middle - LANES
            after = middle + reach
            bias[half, before:after, :] = turned_biases(row, size, lead).T
            if before > 0:
                bias[half, :before, :] = jnp.broadcast_to(row[:, :1], (before, size))
            if after < width:
                bias[half, after:, :] = jnp.broadcast_to(row[:, -1:], (width - after, size))
        grad_scores[...] = jnp.zeros_like(grad_scores)
        grad_k_sum[...] = jnp.zeros_like(grad_k_sum)
        grad_v_sum[...] = jnp.zeros_like(grad_v_sum)
        band_sum[...] = jnp.zeros_like(band_sum)

    lane = lax.broadcasted_iota(jnp.int32, (size, LANES), 1)
    rows = first + lax.broadcasted_iota(jnp.int32, (size, LANES), 0)
    apart = jnp.where((segment_of(rows, ends) != lane) & (lane < 3), -far_apart, 0.0)
    start = pl.multiple_of(middle - (first - shift), LANES)
    near_rows = pl.ds(pl.multiple_of(first - shift, LANES), LANES + reach)
    queries = q_ref[...]
    grads = grad_ref[...]
    products = grads.astype(wide) * attended_ref[...]
    totals = total_ref[...]

    def in_parts(column, at):
        head = column.astype(low).astype(wide)
        body = (column - head).astype(low).astype(wide)
        tail = column - head - body
        return jnp.where(
            lane == at,
            head,
            jnp.where(lane == at + 1, body, jnp.where(lane == at + 2, tail, 0.0)),
        )

    query_grads = []
    for half in range(2):
        mine = (lane >= HEAD) if half else (lane < HEAD)
        row_term = jnp.sum(jnp.where(mine, products, 0.0), axis=1, keepdims=True)
        row_total = jnp.sum(
            jnp.where(lane == 2 * pair + half, totals, 0.0), axis=1, keepdims=True
        )
        query_part = jnp.where(mine, queries, jnp.zeros_like(queries))
        grad_part = jnp.where(mine, grads, jnp.zeros_like(grads))
        query_side = jnp.concatenate(
            [query_part, (apart - in_parts(row_total, 3 + 3 * half)).astype(low)], axis=1
        )
        grad_side = jnp.concatenate(
            [grad_part, (-in_parts(row_term, 3 * half)).astype(low)], axis=1
        )
        weights = jnp.exp(
            back_product(key_side[...], query_side) + bias[half, pl.ds(start, pack), :]
        )
        grad_block = (weights * back_product(value_side[...], grad_side)).astype(low)
        grad_scores[LANES : LANES + pack, :] = grad_block
        grad_v_sum[...] += product(weights.astype(low), grad_part)
        block_lane = jnp.where(lane == 8 * half + block, 1.0, 0.0).astype(low)
        grad_k_sum[...] += product(
            grad_block, jnp.concatenate([query_part, block_lane], axis=1)
        )
        query_grads.append(product(keys_turned[HEAD * half : HEAD * (half + 1), :], grad_block))
        band_sum[half] += grad_scores[near_rows, :].astype(wide)
    grad_q_ref[...] = jnp.concatenate(query_grads, axis=0).T.astype(grad_q_ref.dtype)

    @pl.when(block == blocks - 1)
    def _():
        grad_k_ref[...] = grad_k_sum[:, :LANES].astype(grad_k_ref.dtype)
        grad_v_ref[...] = grad_v_sum[...].astype(grad_v_ref.dtype)
        key = lax.broadcasted_iota(jnp.int32, (pack, LANES), 0)
        which = lax.broadcasted_iota(jnp.int32, (pack, LANES), 1) % 8
        begin = place[2] - shift + size * which
        sums = grad_k_sum[:, LANES:]
        below = jnp.sum(jnp.where(key < begin - LANES, sums, 0.0), axis=0, keepdims=True)
        above = jnp.sum(jnp.where(key >= begin + reach, sums, 0.0), axis=0, keepdims=True)
        far_ref[0] = jnp.concatenate([below, above, jnp.zeros((6, LANES), wide)], axis=0)
        columns = band_ref.shape[2]
        mirror = (
            lax.broadcasted_iota(jnp.int32, (size, columns), 0)
            + lax.broadcasted_iota(jnp.int32, (size, columns), 1)
            == size - 1
        ).astype(wide)
        for half in range(2):
            flipped = jnp.dot(
                band_sum[half], mirror, precision=highest, preferred_element_type=wide
            )
            turned = pltpu.roll(flipped, 0, 1, stride=1, stride_axis=0)
            band_ref[0, half : half + 1, :] = jnp.sum(turned, axis=0, keepdims=True)
        band_ref[0, 2:, :] = jnp.zeros((6, columns), wide)


def attend_back(queries, all_keys, all_values, grads, attended, totals, near, place):
    rows, width = queries.shape
    pack = all_keys.shape[0]
    size = block_rows(rows)
    _, reach, _, columns = table_sizes(size, pack)
    band = -(-(size + LANES + reach) // LANES) * LANES
    pairs = width // LANES

    def own(p, i):
        return (i, p)

    def every(p, i):
        return (0, p)

    grad_q, grad_k, grad_v, band_sums, far_sums = pl.pallas_call(
        attend_back_kernel,
        name="attend_back",
        grid=(pairs, rows // size),
        in_specs=[
            pl.BlockSpec(memory_space=pltpu.SMEM),
            pl.BlockSpec((size, LANES), own),
            pl.BlockSpec((pack, LANES), every),
            pl.BlockSpec((pack, LANES), every),
            pl.BlockSpec((size, LANES), own),
            pl.BlockSpec((size, LANES), own),
            pl.BlockSpec((size, LANES), lambda p, i: (i, 0)),
            pl.BlockSpec((2, 1, near.shape[2]), lambda p, i: (p, 0, 0)),
        ],
        out_specs=[
            pl.BlockSpec((size, LANES), own),
            pl.BlockSpec((pack, LANES), every),
            pl.BlockSpec((pack, LANES), every),
            pl.BlockSpec((1, 8, band), lambda p, i: (p, 0, 0)),
            pl.BlockSpec((1, 8, LANES), lambda p, i: (p, 0, 0)),
        ],
        out_shape=[
            jax.ShapeDtypeStruct((rows, width), low),
            jax.ShapeDtypeStruct((pack, width), low),
            jax.ShapeDtypeStruct((pack, width), low),
            jax.ShapeDtypeStruct((pairs, 8, band), wide),
            jax.ShapeDtypeStruct((pairs, 8, LANES), wide),
        ],
        scratch_shapes=[
            pltpu.VMEM((2, columns, size), wide),
            pltpu.VMEM((pack, 2 * LANES), low),
            pltpu.VMEM((pack, 2 * LANES), low),
            pltpu.VMEM((LANES, pack), low),
            pltpu.VMEM((LANES + pack + reach, size), low),
            pltpu.VMEM((pack, 2 * LANES), wide),
            pltpu.VMEM((pack, LANES), wide),
            pltpu.VMEM((2, LANES + reach, size), wide),
        ],
        compiler_params=pltpu.CompilerParams(vmem_limit_bytes=56 * 2**20),
        cost_estimate=pl.CostEstimate(
            flops=20 * rows * pack * width * 2, bytes_accessed=16 * pack * width, transcendentals=0
        ),
    )(place, queries, all_keys, all_values, grads, attended, totals, near)
    offsets = jnp.arange(band, dtype=jnp.int32) - (size - 1) - LANES - place[3]
    buckets = jnp.arange(BUCKETS, dtype=jnp.int32)
    onehot = (bucket_of(offsets)[:, None] == buckets[None, :]).astype(wide)
    near_grad = jnp.dot(
        band_sums[:, :2].reshape(HEADS, band), onehot, precision=highest, preferred_element_type=wide
    )
    far_grad = jnp.sum(far_sums[:, :2, :16].reshape(pairs, 2, 2, 8), axis=3)
    far_grad = jnp.transpose(far_grad, (0, 2, 1)).reshape(HEADS, 2)
    grad_table = near_grad + far_grad[:, :1] * (buckets == 15) + far_grad[:, 1:] * (buckets == 31)
    return grad_q, grad_k, grad_v, grad_table.T


SEQ_ROWS = 8
HEAD_ROWS = 16
MESH = pl.DeviceIdType.MESH


def rms_factor(values):
    return lax.rsqrt(jnp.mean(values * values, axis=-1, keepdims=True) + eps_norm)


def rms_back(values, gain_row, grad_rows):
    factor = rms_factor(values)
    scaled = gain_row * grad_rows
    inner = jnp.mean(scaled * values, axis=-1, keepdims=True)
    return (
        factor * scaled - values * (factor * factor * factor) * inner,
        jnp.sum(grad_rows * values * factor, axis=0, keepdims=True),
    )


gelu_scale = 0.7978845608028654


def gelu_value(values):
    return 0.5 * values * (
        1.0 + jnp.tanh(gelu_scale * (values + 0.044715 * values * values * values))
    )


def gelu_slope(values):
    square = values * values
    bent = jnp.tanh(gelu_scale * (values + 0.044715 * square * values))
    return 0.5 * (1.0 + bent) + 0.5 * values * (1.0 - bent * bent) * gelu_scale * (
        1.0 + 0.134145 * square
    )


def decoder_kernel(
    groups,
    members,
    seqs,
    place,
    context_ref,
    third_ref,
    gains_ref,
    target_ref,
    embedded_ref,
    loss_ref,
    grad_context_ref,
    pieces_ref,
    mixed_ref,
    starts_ref,
    totals_ref,
    weights,
    everyone,
    shared,
    similar_ref,
    weight_sem,
    every_send,
    every_recv,
    share_send,
    share_recv,
):
    rows, width = context_ref.shape
    count, _, _ = third_ref.shape
    unit = width // count
    blocks = 4 * unit
    group = lax.axis_index("batch")
    member = lax.axis_index("seq")
    seq_total = groups * seqs

    barrier = pltpu.get_barrier_semaphore()
    for step in range(1, groups):
        pl.semaphore_signal(
            barrier,
            inc=1,
            device_id={"batch": lax.rem(group + step, groups)},
            device_id_type=MESH,
        )
    for step in range(1, members):
        pl.semaphore_signal(
            barrier,
            inc=1,
            device_id={"seq": lax.rem(member + step, members)},
            device_id_type=MESH,
        )

    sizes = [unit] * 7 + [unit] * 4 + [blocks]
    firsts = [sum(sizes[:i]) for i in range(len(sizes))]
    copies = [
        pltpu.make_async_copy(
            third_ref.at[:, first : first + size, :],
            weights.at[:, first : first + size, :],
            weight_sem.at[i],
        )
        for i, (first, size) in enumerate(zip(firsts, sizes))
    ]
    for copy in copies:
        copy.start()

    def weight(i):
        return weights[:, firsts[i] : firsts[i] + unit, :].reshape(width, width)

    def outer_weight(j):
        per = count // 4
        return weights[per * j : per * (j + 1), firsts[11] : firsts[11] + blocks, :].reshape(
            width, width
        )

    gain = {
        name: gains_ref[i : i + 1, :]
        for i, name in enumerate(
            ("attention", "feed", "encoder", "start", "own", "cross", "second", "final")
        )
    }
    context = context_ref[...]

    start = jnp.broadcast_to(gain["start"], (SEQ_ROWS, width))
    self_in = (start * rms_factor(start) * gain["own"]).astype(low)
    copies[0].wait()
    self_vals = product(self_in, weight(0)).astype(low)
    copies[1].wait()
    after_self = start + product(self_vals, weight(1))
    cross_in = (after_self * rms_factor(after_self) * gain["cross"]).astype(low)
    copies[2].wait()
    cross_query = product(cross_in, weight(2))
    head_row = lax.broadcasted_iota(jnp.int32, (HEAD_ROWS, width), 0)
    head_mask = head_row == lax.broadcasted_iota(jnp.int32, (HEAD_ROWS, width), 1) // HEAD
    query_heads = jnp.where(
        head_mask, jnp.broadcast_to(cross_query[:1], (HEAD_ROWS, width)), 0.0
    ).astype(low)
    copies[3].wait()
    key_rows = back_product(query_heads, weight(3)).astype(low)

    many = seqs * HEAD_ROWS
    scores = back_product(key_rows, context)
    scores = jnp.concatenate([scores] * seqs, axis=0)
    places = member * rows + lax.broadcasted_iota(jnp.int32, (many, rows), 1)
    row_seq = lax.broadcasted_iota(jnp.int32, (many, rows), 0) // HEAD_ROWS
    inside = segment_of(places, (place[0], place[1])) == row_seq
    scores = jnp.where(inside, scores, masked_score)
    part_top = jnp.max(scores, axis=1, keepdims=True)
    part_weights = jnp.where(inside, jnp.exp(scores - part_top), 0.0).astype(low)
    part_total = jnp.sum(part_weights.astype(wide), axis=1, keepdims=True)
    lane = lax.broadcasted_iota(jnp.int32, (many, LANES), 1)
    shared[0, :, :width] = product(part_weights, context)
    shared[0, :, width:] = jnp.where(lane == 0, part_top, part_total)

    pl.semaphore_wait(barrier, groups - 1 + members - 1)
    for step in range(1, members):
        pltpu.make_async_remote_copy(
            src_ref=shared.at[0],
            dst_ref=shared.at[step],
            send_sem=share_send.at[step - 1],
            recv_sem=share_recv.at[step - 1],
            device_id={"seq": lax.rem(member + step, members)},
            device_id_type=MESH,
        ).start()
    for step in range(1, members):
        pltpu.make_async_remote_copy(
            src_ref=shared.at[0],
            dst_ref=shared.at[step],
            send_sem=share_send.at[step - 1],
            recv_sem=share_recv.at[step - 1],
            device_id={"seq": lax.rem(member + step, members)},
            device_id_type=MESH,
        ).wait()
    top = shared[0, :, width : width + 1]
    for step in range(1, members):
        top = jnp.maximum(top, shared[step, :, width : width + 1])
    total = jnp.zeros((many, 1), wide)
    mixed = jnp.zeros((many, width), wide)
    for step in range(members):
        scale = jnp.exp(shared[step, :, width : width + 1] - top)
        total = total + shared[step, :, width + 1 : width + 2] * scale
        mixed = mixed + shared[step, :, :width] * scale
    mixed = (mixed / total).astype(low)
    mixed_ref[...] = mixed
    log_total = top + jnp.log(total)

    def by_seq(parts):
        row = lax.broadcasted_iota(jnp.int32, (SEQ_ROWS, width), 0)
        joined = jnp.zeros((SEQ_ROWS, width), wide)
        for i, part in enumerate(parts):
            joined = jnp.where(row == i, part, joined)
        return joined

    copies[4].wait()
    spread = product(mixed, weight(4))
    cross_attended = by_seq(
        [
            jnp.sum(
                jnp.where(head_mask, spread[HEAD_ROWS * i : HEAD_ROWS * (i + 1)], 0.0),
                axis=0,
                keepdims=True,
            )
            for i in range(seqs)
        ]
    )
    cross_low = cross_attended.astype(low)
    copies[5].wait()
    after_cross = after_self + product(cross_low, weight(5))
    second_in = (after_cross * rms_factor(after_cross) * gain["second"]).astype(low)
    for i in range(7, 12):
        copies[i].wait()
    second_pre = [product(second_in, weight(7 + j)) for j in range(4)]
    second_act = [gelu_value(second_pre[j]).astype(low) for j in range(4)]
    decoded = after_cross
    for j in range(4):
        decoded = decoded + product(second_act[j], outer_weight(j))
    pooled_in = (decoded * rms_factor(decoded) * gain["final"]).astype(low)
    copies[6].wait()
    pooled = product(pooled_in, weight(6))
    size = lax.rsqrt(jnp.sum(pooled * pooled, axis=-1, keepdims=True) + eps_norm)
    embedded = pooled * size
    embedded_ref[...] = embedded

    everyone[0] = embedded
    sends = []
    for step in range(1, groups):
        sends.append(
            pltpu.make_async_remote_copy(
                src_ref=everyone.at[0],
                dst_ref=everyone.at[step],
                send_sem=every_send,
                recv_sem=every_recv,
                device_id={"batch": lax.rem(group + step, groups)},
                device_id_type=MESH,
            )
        )
        sends[-1].start()
    arrival = pltpu.make_async_remote_copy(
        src_ref=everyone.at[pl.ds(1, groups - 1)],
        dst_ref=everyone.at[pl.ds(1, groups - 1)],
        send_sem=every_send,
        recv_sem=every_recv,
        device_id={"batch": lax.rem(group + 1, groups)},
        device_id_type=MESH,
    )
    arrival.wait_recv()
    arrival.wait_send()
    all_rows = everyone[...].reshape(groups * SEQ_ROWS, width)
    number = groups * SEQ_ROWS
    row = lax.broadcasted_iota(jnp.int32, (number, number), 0)
    column = lax.broadcasted_iota(jnp.int32, (number, number), 1)
    row_valid = row % SEQ_ROWS < seqs
    valid = row_valid & (column % SEQ_ROWS < seqs)
    similar = logit_scale * lax.dot_general(
        all_rows,
        all_rows,
        (((1,), (1,)), ((), ())),
        precision=highest,
        preferred_element_type=wide,
    )
    similar = jnp.where(valid & (row != column), similar, masked_score)
    best = jnp.max(similar, axis=1, keepdims=True)
    log_norm = best + jnp.log(jnp.sum(jnp.exp(similar - best), axis=1, keepdims=True))
    row_group = lax.rem(group - row // SEQ_ROWS + groups, groups)
    column_group = lax.rem(group - column // SEQ_ROWS + groups, groups)
    row_number = row_group * seqs + row % SEQ_ROWS
    column_number = column_group * seqs + column % SEQ_ROWS
    label = jnp.max(
        jnp.where(
            lax.broadcasted_iota(jnp.int32, (number, target_ref.shape[1]), 1)
            == row_number[:, : target_ref.shape[1]],
            target_ref[:1, :],
            -1.0,
        ),
        axis=1,
        keepdims=True,
    )
    target = (column_number.astype(wide) == label) & valid
    picked = jnp.sum(jnp.where(target, similar, 0.0), axis=1, keepdims=True)
    losses = jnp.where(row_valid[:, :1], log_norm - picked, 0.0)
    loss_ref[...] = jnp.broadcast_to(
        jnp.sum(losses, axis=0, keepdims=True) / seq_total, loss_ref.shape
    )
    grad_similar = jnp.where(
        valid, (jnp.exp(similar - log_norm) - target.astype(wide)) / seq_total, 0.0
    )
    similar_ref[...] = grad_similar + grad_similar.T
    grad_embedded = logit_scale * jnp.dot(
        similar_ref[:SEQ_ROWS, :], all_rows, precision=highest, preferred_element_type=wide
    )

    grad_pooled = (
        size
        * (grad_embedded - embedded * jnp.sum(embedded * grad_embedded, axis=-1, keepdims=True))
    ).astype(low)
    grad_decoded, grad_final_gain = rms_back(
        decoded, gain["final"], back_product(grad_pooled, weight(6))
    )
    grad_second_out = grad_decoded.astype(low)
    grad_second_pre = [
        (gelu_slope(second_pre[j]) * back_product(grad_second_out, outer_weight(j))).astype(low)
        for j in range(4)
    ]
    grad_second_in = back_product(grad_second_pre[0], weight(7))
    for j in range(1, 4):
        grad_second_in = grad_second_in + back_product(grad_second_pre[j], weight(7 + j))
    grad_after_cross, grad_second_gain = rms_back(after_cross, gain["second"], grad_second_in)
    grad_after_cross = grad_after_cross + grad_decoded
    grad_cross_branch = grad_after_cross.astype(low)
    grad_cross_att = back_product(grad_cross_branch, weight(5)).astype(low)
    grad_cross_wide = grad_cross_att.astype(wide)
    grad_heads = jnp.concatenate(
        [
            jnp.where(
                head_mask,
                jnp.broadcast_to(grad_cross_wide[i : i + 1], (HEAD_ROWS, width)),
                0.0,
            )
            for i in range(seqs)
        ],
        axis=0,
    )
    attended_heads = jnp.concatenate(
        [
            jnp.broadcast_to(cross_attended[i : i + 1], (HEAD_ROWS, width))
            for i in range(seqs)
        ],
        axis=0,
    )
    row_terms = jnp.sum(grad_heads * attended_heads, axis=1, keepdims=True)
    value_rows = back_product(grad_heads.astype(low), weight(4)).astype(low)
    probs = jnp.where(inside, jnp.exp(scores - log_total), 0.0)
    grad_scores = (probs * (back_product(value_rows, context) - row_terms)).astype(low)
    grad_context_ref[...] = weight_grad(
        jnp.concatenate([grad_scores, probs.astype(low)], axis=0),
        jnp.concatenate([key_rows] * seqs + [value_rows], axis=0),
    )
    key_sums = product(grad_scores, context)
    sums = key_sums[:HEAD_ROWS]
    for i in range(1, seqs):
        sums = sums + key_sums[HEAD_ROWS * i : HEAD_ROWS * (i + 1)]
    first_member = jnp.where(member == 0, 1.0, 0.0)
    totals_ref[:HEAD_ROWS, :] = sums
    totals_ref[HEAD_ROWS:, :] = first_member * by_seq(
        [jnp.sum(grad_after_cross, axis=0, keepdims=True), grad_final_gain, grad_second_gain]
    )
    for i, piece in enumerate(
        [cross_low, second_in]
        + second_act
        + [pooled_in, grad_cross_branch]
        + grad_second_pre
        + [grad_second_out, grad_pooled, grad_cross_att]
    ):
        pieces_ref[i] = piece.astype(wide)
    for i, piece in enumerate([start, self_in, self_vals, after_self, cross_in, cross_query]):
        starts_ref[i : i + 1, :] = piece[:1].astype(wide)
    starts_ref[6:, :] = jnp.zeros((2, width), wide)


def decoder_step(context, third, gains, labels, place, groups, members, seqs):
    rows, width = context.shape
    everything = pl.BlockSpec(memory_space=pltpu.VMEM)
    labels = jnp.pad(labels.astype(wide)[None], ((0, 7), (0, LANES - labels.shape[0])))
    number = groups * SEQ_ROWS
    return pl.pallas_call(
        functools.partial(decoder_kernel, groups, members, seqs),
        name="decoder",
        in_specs=[
            pl.BlockSpec(memory_space=pltpu.SMEM),
            everything,
            pl.BlockSpec(memory_space=pl.ANY),
            everything,
            everything,
        ],
        out_specs=[everything] * 7,
        out_shape=[
            jax.ShapeDtypeStruct((SEQ_ROWS, width), wide),
            jax.ShapeDtypeStruct((8, LANES), wide),
            jax.ShapeDtypeStruct((rows, width), wide),
            jax.ShapeDtypeStruct((15, SEQ_ROWS, width), wide),
            jax.ShapeDtypeStruct((seqs * HEAD_ROWS, width), low),
            jax.ShapeDtypeStruct((8, width), wide),
            jax.ShapeDtypeStruct((HEAD_ROWS + SEQ_ROWS, width), wide),
        ],
        scratch_shapes=[
            pltpu.VMEM(third.shape, low),
            pltpu.VMEM((groups, SEQ_ROWS, width), wide),
            pltpu.VMEM((members, seqs * HEAD_ROWS, width + LANES), wide),
            pltpu.VMEM((number, number), wide),
            pltpu.SemaphoreType.DMA((12,)),
            pltpu.SemaphoreType.DMA,
            pltpu.SemaphoreType.DMA,
            pltpu.SemaphoreType.DMA((max(members - 1, 1),)),
            pltpu.SemaphoreType.DMA((max(members - 1, 1),)),
        ],
        compiler_params=pltpu.CompilerParams(
            collective_id=0, has_side_effects=True, vmem_limit_bytes=56 * 2**20
        ),
        cost_estimate=pl.CostEstimate(
            flops=2 * rows * width * 300, bytes_accessed=2 * third.size, transcendentals=0
        ),
    )(place, context, third, gains, labels)


def seq_exchange(value):
    count = lax.axis_size("seq")
    return [value] + [
        lax.ppermute(value, "seq", [(i, (i - step) % count) for i in range(count)])
        for step in range(1, count)
    ]


def in_place_order(pieces):
    count = len(pieces)
    me = lax.axis_index("seq")
    ordered = []
    for place in range(count):
        chosen = pieces[0]
        for step in range(1, count):
            chosen = jnp.where((place - me) % count == step, pieces[step], chosen)
        ordered.append(chosen)
    return jnp.concatenate(ordered, axis=0)


def seq_sum(value):
    count = lax.axis_size("seq")
    total = value.astype(wide)
    for step in range(1, count):
        total = total + lax.ppermute(
            value, "seq", [(i, (i - step) % count) for i in range(count)]
        ).astype(wide)
    return total


def seq_scatter(value, rows):
    count = lax.axis_size("seq")
    me = lax.axis_index("seq")
    total = lax.dynamic_slice_in_dim(value, me * rows, rows)
    for step in range(1, count):
        other = lax.dynamic_slice_in_dim(value, (me + step) % count * rows, rows)
        total = total + lax.ppermute(
            other.astype(low), "seq", [(i, (i + step) % count) for i in range(count)]
        ).astype(wide)
    return total


def in_blocks(gathered, sizes):
    count, _, width = gathered.shape
    join = 16 // math.gcd(16, sizes[0])
    if join == 1:
        return gathered
    pieces, at = [], 0
    for size in sizes:
        piece = gathered[:, at : at + size].reshape(count // join, join * size, width)
        pieces.append(piece)
        at += size
    return jnp.concatenate(pieces, axis=1)


def column_blocks(weight, model_width):
    rows, columns = weight.shape
    blocks = columns // model_width
    return jnp.transpose(weight.reshape(rows, blocks, model_width), (1, 0, 2)).reshape(
        blocks * rows, model_width
    )


def shards(
    tokens,
    lengths,
    labels,
    attention_gain,
    query_weight,
    key_weight,
    value_weight,
    attention_out,
    position_bias,
    feed_gain,
    feed_inner,
    feed_outer,
    encoder_gain,
    start_token,
    self_gain,
    self_value,
    self_out,
    cross_gain,
    cross_query,
    cross_key,
    cross_value,
    cross_out,
    second_gain,
    second_inner,
    second_outer,
    final_gain,
    pooler_weight,
):
    rows, width = tokens.shape
    part = query_weight.shape[0]
    share = feed_outer.shape[0]
    groups = lax.axis_size("batch")
    members = lax.axis_size("seq")
    blocks = feed_inner.shape[1] // width
    pack = rows * members
    seqs = lengths.shape[1]
    group = lax.axis_index("batch")
    member = lax.axis_index("seq")
    own_first = member * rows
    ends = jnp.cumsum(lengths[0])
    place = jnp.stack(
        [ends[0], ends[1], own_first, own_first % LANES]
    ).astype(jnp.int32)

    vectors = jnp.stack(
        [
            attention_gain,
            feed_gain,
            encoder_gain,
            start_token,
            self_gain,
            cross_gain,
            second_gain,
            final_gain,
        ],
        axis=1,
    )
    bias_row = jnp.pad(position_bias.reshape(1, -1), ((0, part - 1), (0, 0)))
    extra = jnp.concatenate([vectors, bias_row], axis=1)
    extra = jnp.pad(extra, ((0, 0), (0, LANES - extra.shape[1])))
    first_part = jnp.concatenate([query_weight, key_weight, value_weight, extra], axis=1)
    first = lax.all_gather(first_part, "batch", axis=0, tiled=True)
    second_part = jnp.concatenate(
        [attention_out, column_blocks(feed_inner, width), feed_outer], axis=0
    )
    second = lax.all_gather(second_part, "batch", axis=0, tiled=False)
    third_part = jnp.concatenate(
        [
            self_value,
            self_out,
            cross_query,
            cross_key,
            cross_value,
            cross_out,
            pooler_weight,
            column_blocks(second_inner, width),
            second_outer,
        ],
        axis=0,
    )
    third = lax.all_gather(third_part, "batch", axis=0, tiled=False)

    def square(gathered, at):
        return gathered[:, at : at + part].reshape(groups * part, width)

    def tall(gathered, at):
        return gathered[:, at : at + share].reshape(groups * share, width)

    gains = first[:, 3 * width : 3 * width + 8].astype(wide).T
    (
        attention_gain_full,
        feed_gain_full,
        encoder_gain_full,
        start_full,
        self_gain_full,
        cross_gain_full,
        second_gain_full,
        final_gain_full,
    ) = [gains[i] for i in range(8)]
    table = first.reshape(groups, part, -1)[
        :, 0, 3 * width + 8 : 3 * width + 8 + position_bias.size
    ].reshape(BUCKETS, HEADS)
    query_full = first[:, :width]
    key_value_full = first[:, width : 3 * width]

    all_tokens = in_place_order(seq_exchange(tokens))
    inputs = tokens.astype(wide)
    normed_all = rms_norm(all_tokens.astype(wide), attention_gain_full).astype(low)
    normed = rms_norm(inputs, attention_gain_full).astype(low)
    queries = product(normed, query_full).astype(low)
    keys_values = product(normed_all, key_value_full).astype(low)
    all_keys = keys_values[:, :width]
    all_values = keys_values[:, width:]
    near = offset_biases(table, block_rows(rows), pack, place[3])
    attended, totals = attend(queries, all_keys, all_values, near, place)
    attended_low = attended.astype(low)
    out_full = square(second, 0)
    hidden = inputs + product(attended_low, out_full)

    inner_in = rms_norm(hidden, feed_gain_full).astype(low)
    inner_full = [square(second, part * (1 + j)) for j in range(blocks)]
    outer_full = tall(second, part * (1 + blocks)).reshape(blocks, -1, width)
    inner_pre = [product(inner_in, inner_full[j]) for j in range(blocks)]
    inner_act = [jax.nn.gelu(inner_pre[j]).astype(low) for j in range(blocks)]
    encoded = hidden
    for j in range(blocks):
        encoded = encoded + product(inner_act[j], outer_full[j])
    context = rms_norm(encoded, encoder_gain_full).astype(low)

    third_sizes = [part] * (7 + blocks) + [share]
    (
        embedded,
        loss,
        grad_context,
        pieces,
        mixed,
        starts,
        decoder_totals,
    ) = decoder_step(
        context, in_blocks(third, third_sizes), gains, labels, place, groups, members, seqs
    )
    contrastive_loss = loss[0, :1]
    embedded = embedded[:seqs]
    decoder_rows = jnp.concatenate(
        [
            pieces[:, :seqs].astype(low).reshape(-1, width),
            mixed.reshape(seqs, HEAD_ROWS, width)[:, :HEADS].reshape(-1, width),
        ],
        axis=0,
    )
    start_row, self_in, self_vals, after_self, cross_in, cross_query_row = [
        starts[i : i + 1] for i in range(6)
    ]
    head_of = jnp.arange(width, dtype=jnp.int32) // HEAD
    head_mask = head_of[None, :] == jnp.arange(HEADS, dtype=jnp.int32)[:, None]

    count = decoder_rows.shape[0]
    decoder_rows = jnp.pad(decoder_rows, ((0, -count % 16), (0, 0)))

    grad_encoded, grad_encoder_gain = norm_back(encoded, encoder_gain_full, grad_context)
    grad_feed_branch = grad_encoded.astype(low)
    grad_inner_pre = [
        gelu_back(inner_pre[j], back_product(grad_feed_branch, outer_full[j])).astype(low)
        for j in range(blocks)
    ]
    grad_inner_in = sum(back_product(grad_inner_pre[j], inner_full[j]) for j in range(blocks))
    grad_hidden, grad_feed_gain = norm_back(hidden, feed_gain_full, grad_inner_in)
    grad_hidden = grad_hidden + grad_encoded
    grad_attn_branch = grad_hidden.astype(low)
    second_grads = jnp.concatenate(
        [weight_grad(attended_low, grad_attn_branch).astype(low).reshape(groups, part, width)]
        + [
            weight_grad(inner_in, grad_inner_pre[j]).astype(low).reshape(groups, part, width)
            for j in range(blocks)
        ]
        + [
            jnp.concatenate(
                [weight_grad(inner_act[j], grad_feed_branch).astype(low) for j in range(blocks)],
                axis=0,
            ).reshape(groups, share, width)
        ],
        axis=1,
    )

    sums = lax.psum(
        jnp.concatenate(
            [decoder_totals[:HEADS], decoder_totals[HEAD_ROWS : HEAD_ROWS + 3], grad_encoder_gain[None]],
            axis=0,
        ),
        ("batch", "seq"),
    )

    grad_attended = back_product(grad_attn_branch, out_full).astype(low)
    grad_attended, second_grads = lax.optimization_barrier((grad_attended, second_grads))
    second_sums = lax.psum_scatter(second_grads, "batch", scatter_dimension=0, tiled=False)
    grad_query_low, grad_key_low, grad_value_low, grad_table = attend_back(
        queries, all_keys, all_values, grad_attended, attended, totals, near, place
    )
    first_grads = jnp.concatenate(
        [
            weight_grad(normed, grad_query_low).astype(low).reshape(groups, part, width),
            weight_grad(normed_all, grad_key_low).astype(low).reshape(groups, part, width),
            weight_grad(normed_all, grad_value_low).astype(low).reshape(groups, part, width),
        ],
        axis=1,
    )
    decoder_rows, grad_query_low = lax.optimization_barrier((decoder_rows, grad_query_low))
    decoder_rows = lax.all_gather(decoder_rows, "batch", axis=0, tiled=False)
    first_sums = lax.psum_scatter(first_grads, "batch", scatter_dimension=0, tiled=False)
    grad_normed_all = back_product(grad_key_low, key_value_full[:, :width]) + back_product(
        grad_value_low, key_value_full[:, width:]
    )
    grad_normed = seq_scatter(grad_normed_all, rows) + back_product(grad_query_low, query_full)
    grad_inputs, grad_attention_gain = norm_back(inputs, attention_gain_full, grad_normed)
    grad_inputs = grad_inputs + grad_hidden
    table_row = jnp.pad(grad_table.reshape(1, -1), ((0, 0), (0, width - grad_table.size)))
    last_sums = lax.psum(
        jnp.concatenate([grad_attention_gain[None], grad_feed_gain[None], table_row], axis=0),
        ("batch", "seq"),
    )

    self_value_full = square(third, 0)
    self_out_full = square(third, part)
    cross_query_full = square(third, 2 * part)
    cross_key_full = square(third, 3 * part)
    grad_cross_query_row = jnp.sum(
        jnp.where(head_mask, product(sums[:HEADS].astype(low), cross_key_full), 0.0),
        axis=0,
        keepdims=True,
    ).astype(low)
    grad_after_self, grad_cross_gain = norm_back(
        after_self, cross_gain_full, back_product(grad_cross_query_row, cross_query_full)
    )
    grad_after_self = grad_after_self + sums[HEADS : HEADS + 1]
    grad_self_branch = grad_after_self.astype(low)
    grad_self_vals = back_product(grad_self_branch, self_out_full).astype(low)
    grad_start, grad_self_gain = norm_back(
        start_row, self_gain_full, back_product(grad_self_vals, self_value_full)
    )
    grad_start = (grad_start + grad_after_self)[0]

    def mine(values, size=part):
        return lax.dynamic_slice_in_dim(values, group * size, size, values.ndim - 1)

    def outer(left_side, right_side):
        return mine(left_side).astype(wide).T * right_side.astype(wide)

    def every_row(at, size=seqs):
        return decoder_rows[:, at : at + size].reshape(groups * size, width)

    at = 0
    cross_rows = every_row(0)
    second_in_rows = every_row(seqs)
    act_rows = decoder_rows[:, 2 * seqs : (2 + blocks) * seqs].reshape(
        groups, blocks, seqs, width
    )
    act_rows = jnp.transpose(act_rows, (0, 2, 1, 3)).reshape(groups * seqs, blocks * width)
    at = (2 + blocks) * seqs
    pooled_rows = every_row(at)
    branch_rows = every_row(at + seqs)
    pre_rows = decoder_rows[:, at + 2 * seqs : at + (2 + blocks) * seqs].reshape(
        groups, blocks, seqs, width
    )
    pre_rows = jnp.transpose(pre_rows, (0, 2, 1, 3)).reshape(groups * seqs, blocks * width)
    at = at + (2 + blocks) * seqs
    out_rows = every_row(at)
    grad_pooled_rows = every_row(at + seqs)
    att_rows = every_row(at + 2 * seqs)
    context_rows = every_row(at + 3 * seqs, seqs * HEADS)
    att_heads = jnp.where(
        head_mask[None], att_rows[:, None, :], jnp.zeros((), low)
    ).reshape(-1, width)

    second_sums = seq_sum(second_sums)
    first_sums = seq_sum(first_sums)
    inner_sums = jnp.transpose(
        second_sums[part : part * (1 + blocks)].reshape(blocks, part, width), (1, 0, 2)
    ).reshape(part, blocks * width)
    key_totals = mine(sums[:HEADS])
    return (
        contrastive_loss,
        embedded,
        grad_inputs,
        mine(last_sums[0]),
        first_sums[:part],
        first_sums[part : 2 * part],
        first_sums[2 * part :],
        second_sums[:part],
        mine(last_sums[2, : BUCKETS * HEADS], BUCKETS * HEADS // groups).reshape(-1, HEADS),
        mine(last_sums[1]),
        inner_sums,
        second_sums[part * (1 + blocks) :],
        mine(sums[HEADS + 3]),
        mine(grad_start),
        mine(grad_self_gain),
        outer(self_in, grad_self_vals),
        outer(self_vals, grad_self_branch),
        mine(grad_cross_gain),
        outer(cross_in, grad_cross_query_row),
        jnp.repeat(key_totals.T, HEAD, axis=1) * cross_query_row.astype(wide),
        weight_grad(mine(context_rows), att_heads),
        weight_grad(mine(cross_rows), branch_rows),
        mine(sums[HEADS + 2]),
        weight_grad(mine(second_in_rows), pre_rows),
        weight_grad(mine(act_rows, share), out_rows),
        mine(sums[HEADS + 1]),
        weight_grad(mine(pooled_rows), grad_pooled_rows),
    )


def solution(mesh):
    placed = (
        P(("batch", "seq"), None),
        P("batch", None),
        P(),
        P("batch"),
        P("batch", None),
        P("batch", None),
        P("batch", None),
        P("batch", None),
        P("batch", None),
        P("batch"),
        P("batch", None),
        P("batch", None),
        P("batch"),
        P("batch"),
        P("batch"),
        P("batch", None),
        P("batch", None),
        P("batch"),
        P("batch", None),
        P("batch", None),
        P("batch", None),
        P("batch", None),
        P("batch"),
        P("batch", None),
        P("batch", None),
        P("batch"),
        P("batch", None),
    )
    return jax.shard_map(
        shards,
        mesh=mesh,
        in_specs=placed,
        out_specs=(
            P(),
            P("batch", None),
            P(("batch", "seq"), None),
            P("batch"),
            P("batch", None),
            P("batch", None),
            P("batch", None),
            P("batch", None),
            P("batch", None),
            P("batch"),
            P("batch", None),
            P("batch", None),
            P("batch"),
            P("batch"),
            P("batch"),
            P("batch", None),
            P("batch", None),
            P("batch"),
            P("batch", None),
            P("batch", None),
            P("batch", None),
            P("batch", None),
            P("batch"),
            P("batch", None),
            P("batch", None),
            P("batch"),
            P("batch", None),
        ),
        check_vma=False,
    )
```

profile of v0, /device:TPU:0, one launch (start us, length us, event | category | flops | bytes accessed | tf_op | source)
XLA Modules:
  0.0 681.1 jit_solution(2348188423039287633)
XLA Ops:
  20.5 3.0 collective-permute-start
  27.8 21.7 %collective-permute-done = bf16[768,768]{1,0:T(8,128)(2,1)S(1)} collective-permute-done((bf16[768,768]{1,0:T(8,128)(2,1)S(1)}, bf16[768,768]{1,0:T(8,128)(2,1)S(1)}, u32[]{:S(2)}, u32[]{:S(2)}) %collective-permute-start) | collective-permute-done | bytes 1179680 | tf_op jit(solution)/shard_map/ppermute | solution.py:793
  51.2 15.6 %all-gather.8.cloned.1.call-done = bf16[768,2432]{1,0:T(8,128)(2,1)} async-done(((bf16[48,2432]{1,0:T(8,128)(2,1)}), bf16[768,2432]{1,0:T(8,128)(2,1)}) %all-gather.8.cloned.1.call-update) | async-done | bytes 3735568 | tf_op jit(solution)/shard_map/all_gather | solution.py:915
  69.6 2.6 convolution_convert_fusion.12.q_ref
  72.4 5.6 convolution_convert_fusion
  78.0 2.5 fusion.138
  80.5 40.8 %attend.1 = (f32[768,768]{1,0:T(8,128)S(1)}, f32[768,128]{1,0:T(8,128)S(1)}) custom-call(s32[4]{0:T(128)S(1)} %pad_add_fusion.place, bf16[768,768]{1,0:T(8,128)(2,1)S(1)} %convolution_convert_fusion.12.q_ref, bf16[1536,768]{1,0:T(8,128)(2,1)} %get-tuple-element.96.k_ref, bf16[1536,768]{1,0:T(8,128)(2,1)} %get-tuple-element.95.v_ref, ...), custom_call_target="tpu_custom_call" | custom-call | flops 14495514624 | bytes 18874368 | tf_op jit(solution)/shard_map/attend/pallas_call | solution.py:161
  122.1 34.7 %all-gather.10.cloned.1.call-done = bf16[6912,768]{1,0:T(8,128)(2,1)} async-done(((bf16[432,768]{1,0:T(8,128)(2,1)}), bf16[6912,768]{1,0:T(8,128)(2,1)}) %all-gather.10.cloned.1.call-update) | async-done | bytes 10616848 | tf_op jit(solution)/shard_map/all_gather | solution.py:919
  156.8 3.2 fusion.136
  166.0 3.4 fusion.137
  178.9 71.1 %all-gather.12.cloned.1.call-done = bf16[11520,768]{1,0:T(8,128)(2,1)} async-done(((bf16[720,768]{1,0:T(8,128)(2,1)}), bf16[11520,768]{1,0:T(8,128)(2,1)}) %all-gather.12.cloned.1.call-update) | async-done | bytes 17694736 | tf_op jit(solution)/shard_map/all_gather | solution.py:934
  250.0 32.1 %decoder.1 = (f32[8,768]{1,0:T(8,128)}, f32[8,128]{1,0:T(8,128)}, f32[768,768]{1,0:T(8,128)}, f32[15,8,768]{2,1,0:T(8,128)}, bf16[48,768]{1,0:T(8,128)(2,1)}, /*index=5*/f32[8,768]{1,0:T(8,128)}, f32[24,768]{1,0:T(8,128)}) custom-call(s32[4]{0:T(128)} %copy-done.2, bf16[768,768]{1,0:T(8,128)(2,1)} %multiply_convert_fusion.context_ref, ...), custom_call_target="tpu_custom_call" | custom-call | flops 353894400 | bytes 17694720 | tf_op jit(solution)/shard_map/decoder/pallas_call | solution.py:750
  282.1 3.0 multiply_reduce_fusion
  289.4 2.4 convolution_convert_fusion.2
  294.2 2.4 convolution_convert_fusion.4
  298.8 2.4 convolution_convert_fusion.5
  303.5 2.4 convolution_convert_fusion.3
  312.4 2.6 convolution_convert_fusion.8
  329.2 2.5 constant_dynamic-update-slice_fusion.14
  337.8 2.6 constant_dynamic-update-slice_fusion.9
  341.0 76.7 %attend_back.1 = (bf16[768,768]{1,0:T(8,128)(2,1)}, bf16[1536,768]{1,0:T(8,128)(2,1)}, bf16[1536,768]{1,0:T(8,128)(2,1)}, f32[6,8,768]{2,1,0:T(8,128)}, f32[6,8,128]{2,1,0:T(8,128)}) custom-call(s32[4]{0:T(128)} %copy-done.2, bf16[768,768]{1,0:T(8,128)(2,1)} %copy-done.3, bf16[1536,768]{1,0:T(8,128)(2,1)} %get-tuple-element.96.k_ref, ...), custom_call_target="tpu_custom_call" | custom-call | flops 36238786560 | bytes 18874368 | tf_op jit(solution)/shard_map/attend_back/pallas_call | solution.py:338
  418.0 2.7 convolution_convert_fusion.1
  429.0 3.5 fusion.41
  432.5 3.3 convolution_add_fusion
  445.9 4.5 fusion.135
  450.4 17.6 %collective-permute-done.1 = bf16[768,768]{1,0:T(8,128)(2,1)} collective-permute-done((bf16[768,768]{1,0:T(8,128)(2,1)}, bf16[768,768]{1,0:T(8,128)(2,1)}, u32[]{:S(2)}, u32[]{:S(2)}) %collective-permute-start.1) | collective-permute-done | bytes 1179680 | tf_op jit(solution)/shard_map/ppermute | solution.py:826
  468.0 5.3 fusion.6
  474.0 42.8 %all-reduce.5 = (f32[3,768]{1,0:T(4,128)}, f32[16,768]{1,0:T(8,128)}) all-reduce(f32[3,768]{1,0:T(4,128)} %select_maximum_fusion, f32[16,768]{1,0:T(8,128)} %pad_maximum_fusion.4), channel_id=1, replica_groups=mesh['batch'=16,'seq'=2] {'batch','seq'}, use_global_device_ids=true, to_apply=%region_11.12 | all-reduce | flops 14592 | bytes 116736 | tf_op jit(solution)/shard_map/psum | solution.py:1070
  518.5 2.5 slice_reduce_fusion.4
  558.8 3.7 fusion.36
  581.6 73.2 %reduce-scatter.5.cloned.1.call-done = bf16[1,432,768]{2,1,0:T(8,128)(2,1)} async-done(((bf16[16,432,768]{2,1,0:T(8,128)(2,1)}), bf16[1,432,768]{2,1,0:T(8,128)(2,1)}) %reduce-scatter.5.cloned.1.call-update) | async-done | bytes 663568 | tf_op jit(solution)/shard_map/reduce_scatter | solution.py:1048
  659.6 11.8 %collective-permute-done.3 = bf16[432,768]{1,0:T(8,128)(2,1)S(1)} collective-permute-done((bf16[432,768]{1,0:T(8,128)(2,1)}, bf16[432,768]{1,0:T(8,128)(2,1)S(1)}, u32[]{:S(2)}, u32[]{:S(2)}) %collective-permute-start.3) | collective-permute-done | bytes 663584 | tf_op jit(solution)/shard_map/ppermute | solution.py:814
  (400 shorter events, 158.4 us)
Async XLA Ops:
  7.2 12.0 %copy-start.61 = (bf16[48,768]{1,0:T(8,128)(2,1)S(1)}, bf16[48,768]{1,0:T(8,128)(2,1)}, u32[]{:S(2)}) copy-start(bf16[48,768]{1,0:T(8,128)(2,1)} %param.46) | copy-start | bytes 221188
  7.3 59.5 %all-gather.8.cloned.1.call-start = ((), (), s32[]{:S(2)}) async-start(), calls=%async_computation.2 | async-start | bytes 3969024 | tf_op jit(solution)/shard_map/all_gather | solution.py:915
  16.1 140.7 %all-gather.10.cloned.1.call-start = ((), (), s32[]{:S(2)}) async-start(), calls=%async_computation.5 | async-start | bytes 11280384 | tf_op jit(solution)/shard_map/all_gather | solution.py:919
  19.1 230.9 %all-gather.12.cloned.1.call-start = ((), (), s32[]{:S(2)}) async-start(), calls=%async_computation.6 | async-start | bytes 18800640 | tf_op jit(solution)/shard_map/all_gather | solution.py:934
  20.4 542.0 %all-gather.14.cloned.1.call-start = ((), (), s32[]{:S(2)}) async-start(), calls=%async_computation.7 | async-start | bytes 2506752 | tf_op jit(solution)/shard_map/all_gather | solution.py:1061
  20.5 29.0 %collective-permute-start = (bf16[768,768]{1,0:T(8,128)(2,1)S(1)}, bf16[768,768]{1,0:T(8,128)(2,1)S(1)}, u32[]{:S(2)}, u32[]{:S(2)}) collective-permute-start(bf16[768,768]{1,0:T(8,128)(2,1)S(1)} %copy-done.12), channel_id=1, source_target_pairs={{0,1},{1,0},{2,3},{3,2},{4,5},{5,4},{6,7},{7,6},{8,9},{9,8},{10,11... | collective-permute-start | bytes 3538952 | tf_op jit(solution)/shard_map/ppermute | solution.py:793
  26.2 54.2 %copy-start.2 = (s32[4]{0:T(128)}, s32[4]{0:T(128)S(1)}, u32[]{:S(2)}) copy-start(s32[4]{0:T(128)S(1)} %pad_add_fusion.place) | copy-start | bytes 52
  27.8 41.9 %copy-start.73 = (f32[768]{0:T(1024)}, f32[768]{0:T(1024)S(1)}, u32[]{:S(2)}) copy-start(f32[768]{0:T(1024)S(1)} %fusion.103) | copy-start | bytes 9220
  49.6 22.6 %copy-start.20 = (bf16[768,768]{1,0:T(8,128)(2,1)}, bf16[768,768]{1,0:T(8,128)(2,1)S(1)}, u32[]{:S(2)}) copy-start(bf16[768,768]{1,0:T(8,128)(2,1)S(1)} %get-tuple-element.106) | copy-start | bytes 3538948
  51.2 21.0 %copy-start.84 = (f32[1536]{0:T(1024)}, f32[1536]{0:T(1024)S(1)}, u32[]{:S(2)}) copy-start(f32[1536]{0:T(1024)S(1)} %add_rsqrt_fusion) | copy-start | bytes 18436
  67.9 12.5 %copy-start.1 = (f32[12,1,768]{2,1,0:T(1,128)}, f32[12,1,768]{2,1,0:T(1,128)S(1)}, u32[]{:S(2)}) copy-start(f32[12,1,768]{2,1,0:T(1,128)S(1)} %broadcast_in_dim.87.near_ref) | copy-start | bytes 110596
  122.1 201.6 %copy-start = (f32[768,768]{1,0:T(8,128)}, f32[768,768]{1,0:T(8,128)S(1)}, u32[]{:S(2)}) copy-start(f32[768,768]{1,0:T(8,128)S(1)} %get-tuple-element.45.attended_ref) | copy-start | bytes 7077892
  161.3 12.9 %copy-start.7 = (f32[768,768]{1,0:T(8,128)}, f32[768,768]{1,0:T(8,128)S(1)}, u32[]{:S(2)}) copy-start(f32[768,768]{1,0:T(8,128)S(1)} %get-tuple-element.130) | copy-start | bytes 7077892
  250.0 32.1 %copy-start.6 = (f32[768,768]{1,0:T(8,128)S(1)}, f32[768,768]{1,0:T(8,128)}, u32[]{:S(2)}) copy-start(f32[768,768]{1,0:T(8,128)} %copy-done.5) | copy-start | bytes 7077892
  341.0 76.9 %copy-start.74 = (f32[768]{0:T(1024)S(1)}, f32[768]{0:T(1024)}, u32[]{:S(2)}) copy-start(f32[768]{0:T(1024)} %copy-done.73) | copy-start | bytes 9220
  341.0 77.0 %copy-start.77 = (f32[768]{0:T(1024)S(1)}, f32[768]{0:T(1024)}, u32[]{:S(2)}) copy-start(f32[768]{0:T(1024)} %copy-done.76) | copy-start | bytes 9220
  417.8 161.6 %reduce-scatter.3.cloned.1.call-start = ((), (), s32[]{:S(2)}) async-start(), calls=%async_computation.3 | async-start | bytes 3760128 | tf_op jit(solution)/shard_map/reduce_scatter | solution.py:1062
  427.4 227.4 %reduce-scatter.5.cloned.1.call-start = ((), (), s32[]{:S(2)}) async-start(), calls=%async_computation.4 | async-start | bytes 11280384 | tf_op jit(solution)/shard_map/reduce_scatter | solution.py:1048
  439.1 28.9 %collective-permute-start.1 = (bf16[768,768]{1,0:T(8,128)(2,1)}, bf16[768,768]{1,0:T(8,128)(2,1)}, u32[]{:S(2)}, u32[]{:S(2)}) collective-permute-start(bf16[768,768]{1,0:T(8,128)(2,1)} %dynamic-slice_convert_fusion), channel_id=1, source_target_pairs={{0,1},{1,0},{2,3},{3,2},{4,5},{5,4},{6,7},{7,6},{8,9},{9,8},{10,11... | collective-permute-start | bytes 3538952 | tf_op jit(solution)/shard_map/ppermute | solution.py:826
  445.3 22.7 %slice-start = ((s8[4718592]{0:T(1024)(128)(4,1)}), s8[4194304]{0:T(1024)(128)(4,1)S(1)}, s32[]{:S(2)}) async-start(s8[4718592]{0:T(1024)(128)(4,1)} %bitcast.234), calls=%async_computation.8 | async-start | bytes 8388608
  445.9 22.1 %slice-start.1 = ((s8[4718592]{0:T(1024)(128)(4,1)}), s8[524288]{0:T(1024)(128)(4,1)S(1)}, s32[]{:S(2)}) async-start(s8[4718592]{0:T(1024)(128)(4,1)} %bitcast.234), calls=%async_computation.9 | async-start | bytes 1048576
  445.9 22.1 %copy-start.75 = (f32[768]{0:T(1024)S(1)}, f32[768]{0:T(1024)}, u32[]{:S(2)}) copy-start(f32[768]{0:T(1024)} %copy-done.73) | copy-start | bytes 9220
  445.9 22.1 %copy-start.78 = (f32[768]{0:T(1024)S(1)}, f32[768]{0:T(1024)}, u32[]{:S(2)}) copy-start(f32[768]{0:T(1024)} %copy-done.76) | copy-start | bytes 9220
  445.9 22.1 %copy-start.99 = (bf16[768,768]{1,0:T(8,128)(2,1)S(1)}, bf16[768,768]{1,0:T(8,128)(2,1)}, u32[]{:S(2)}) copy-start(bf16[768,768]{1,0:T(8,128)(2,1)} %get-tuple-element.56) | copy-start | bytes 3538948
  450.4 22.9 %copy-start.82 = (f32[1,768]{1,0:T(1,128)S(1)}, f32[1,768]{1,0:T(1,128)}, u32[]{:S(2)}) copy-start(f32[1,768]{1,0:T(1,128)} %reshape.481) | copy-start | bytes 9220
  450.4 22.9 %copy-start.86 = (f32[1,384]{1,0:T(1,128)S(1)}, f32[1,384]{1,0:T(1,128)}, u32[]{:S(2)}) copy-start(f32[1,384]{1,0:T(1,128)} %reshape.485) | copy-start | bytes 4612
  518.5 33.6 %copy-start.67 = (f32[768]{0:T(1024)S(1)}, f32[768]{0:T(1024)}, u32[]{:S(2)}) copy-start(f32[768]{0:T(1024)} %copy-done.66) | copy-start | bytes 9220
  521.0 37.8 %copy-start.11 = (f32[768,768]{1,0:T(8,128)S(1)}, f32[768,768]{1,0:T(8,128)}, u32[]{:S(2)}) copy-start(f32[768,768]{1,0:T(8,128)} %copy-done.10) | copy-start | bytes 7077892
  572.5 83.7 %copy-start.55 = (bf16[48,768]{1,0:T(8,128)(2,1)S(1)}, bf16[48,768]{1,0:T(8,128)(2,1)}, u32[]{:S(2)}) copy-start(bf16[48,768]{1,0:T(8,128)(2,1)} %reshape.503) | copy-start | bytes 221188
  579.3 78.5 %collective-permute-start.2 = (bf16[144,768]{1,0:T(8,128)(2,1)}, bf16[144,768]{1,0:T(8,128)(2,1)S(1)}, u32[]{:S(2)}, u32[]{:S(2)}) collective-permute-start(bf16[144,768]{1,0:T(8,128)(2,1)} %bitcast.238), channel_id=1, source_target_pairs={{0,1},{1,0},{2,3},{3,2},{4,5},{5,4},{6,7},{7,6},{8,9},{9,8},{10,11... | collective-permute-start | bytes 663560 | tf_op jit(solution)/shard_map/ppermute | solution.py:814
  654.7 16.7 %copy-start.50 = (bf16[1,432,768]{2,1,0:T(8,128)(2,1)S(1)}, bf16[1,432,768]{2,1,0:T(8,128)(2,1)}, u32[]{:S(2)}) copy-start(bf16[1,432,768]{2,1,0:T(8,128)(2,1)} %reduce-scatter.5.cloned.1.call-done) | copy-start | bytes 1990660
  654.7 16.7 %collective-permute-start.3 = (bf16[432,768]{1,0:T(8,128)(2,1)}, bf16[432,768]{1,0:T(8,128)(2,1)S(1)}, u32[]{:S(2)}, u32[]{:S(2)}) collective-permute-start(bf16[432,768]{1,0:T(8,128)(2,1)} %bitcast.231), channel_id=1, source_target_pairs={{0,1},{1,0},{2,3},{3,2},{4,5},{5,4},{6,7},{7,6},{8,9},{9,8},{10,11... | collective-permute-start | bytes 1990664 | tf_op jit(solution)/shard_map/ppermute | solution.py:814
  (82 other events, 282.8 us)
Sparse Core Ops, SparseCore 0:
  16.2 50.5 all-gather.7
  69.0 87.7 all-gather.9
  158.4 91.5 all-gather.11
  417.8 43.0 all-gather.13
  464.6 66.9 reduce-scatter.2
  535.6 119.1 reduce-scatter.4
where the time goes:
time: 690 us; the launch traced here: 681 us
  waiting for transfers between devices  246 us (36%)
  Pallas kernels  150 us (22%)
  matrix products  92.9 us (13%)
  local copies, waits for them, and re-layouts  85.5 us (12%)
  blocking collectives  42.8 us (6%)
  other arithmetic  37.6 us (5%)
  between operations  18.8 us (3%)
  starting transfers between devices  7.73 us (1%)
    pallas_call x1, Pallas kernels, attend_back(): pl.pallas_call(attend_back_kernel, name='attend_back', grid=(pairs, rows...  76.7 us
    reduce_scatter x1, waiting for transfers between devices, shards(): lax.psum_scatter(second_grads, 'batch', scatter_dimension=0, tiled=False)  73.2 us
    all_gather x1, waiting for transfers between devices, shards(): third = lax.all_gather(third_part, 'batch', axis=0, tiled=False)  71.1 us
    psum x1, blocking collectives, shards(): lax.psum(jnp.concatenate([grad_attention_gain[None], grad_feed_gain[None]...  42.8 us
    pallas_call x1, Pallas kernels, attend(): pl.pallas_call(attend_kernel, name='attend', grid=(pairs, rows // size),...  40.8 us
    dot_general x18, matrix products, weight_grad(): lax.dot_general(left_side, right_side, (((0,), (0,)), ((), ())), preferre...  36.8 us
    all_gather x1, waiting for transfers between devices, shards(): second = lax.all_gather(second_part, 'batch', axis=0, tiled=False)  34.7 us
    dot_general x15, matrix products, back_product(): lax.dot_general(left_side, right_side, (((1,), (1,)), ((), ())), preferre...  34.5 us
  transfers between devices with their start and end apart: 10, of which 7 were waited for; matrix products, arithmetic and copies ran while one was open for 20% of the time, Pallas kernels for 6%

commit v1 on v0

--- a/solution.py
+++ b/solution.py
@@ -187,207 +187,6 @@
             flops=8 * rows * pack * width * 2, bytes_accessed=16 * pack * width, transcendentals=0
         ),
     )(place, queries, all_keys, all_values, near)
-
-
-def attend_back_kernel(
-    place,
-    q_ref,
-    k_ref,
-    v_ref,
-    grad_ref,
-    attended_ref,
-    total_ref,
-    near_ref,
-    grad_q_ref,
-    grad_k_ref,
-    grad_v_ref,
-    band_ref,
-    far_ref,
-    bias,
-    key_side,
-    value_side,
-    keys_turned,
-    grad_scores,
-    grad_k_sum,
-    grad_v_sum,
-    band_sum,
-):
-    pair = pl.program_id(0)
-    block = pl.program_id(1)
-    blocks = pl.num_programs(1)
-    pack = k_ref.shape[0]
-    size = q_ref.shape[0]
-    middle, reach, lead, width = table_sizes(size, pack)
-    ends = (place[0], place[1])
-    first = place[2] + block * size
-    shift = place[3]
-
-    @pl.when(block == 0)
-    def _():
-        places = lax.broadcasted_iota(jnp.int32, (pack, LANES), 0)
-        lane = lax.broadcasted_iota(jnp.int32, (pack, LANES), 1)
-        key_side[:, :LANES] = k_ref[...]
-        ones = (segment_of(places, ends) == lane) | ((lane >= 3) & (lane < 9))
-        key_side[:, LANES:] = ones.astype(wide).astype(low)
-        value_side[:, :LANES] = v_ref[...]
-        value_side[:, LANES:] = (lane < 6).astype(wide).astype(low)
-        keys_turned[...] = k_ref[...].T
-        for half in range(2):
-            row = near_ref[half]
-            before = middle - LANES
-            after = middle + reach
-            bias[half, before:after, :] = turned_biases(row, size, lead).T
-            if before > 0:
-                bias[half, :before, :] = jnp.broadcast_to(row[:, :1], (before, size))
-            if after < width:
-                bias[half, after:, :] = jnp.broadcast_to(row[:, -1:], (width - after, size))
-        grad_scores[...] = jnp.zeros_like(grad_scores)
-        grad_k_sum[...] = jnp.zeros_like(grad_k_sum)
-        grad_v_sum[...] = jnp.zeros_like(grad_v_sum)
-        band_sum[...] = jnp.zeros_like(band_sum)
-
-    lane = lax.broadcasted_iota(jnp.int32, (size, LANES), 1)
-    rows = first + lax.broadcasted_iota(jnp.int32, (size, LANES), 0)
-    apart = jnp.where((segment_of(rows, ends) != lane) & (lane < 3), -far_apart, 0.0)
-    start = pl.multiple_of(middle - (first - shift), LANES)
-    near_rows = pl.ds(pl.multiple_of(first - shift, LANES), LANES + reach)
-    queries = q_ref[...]
-    grads = grad_ref[...]
-    products = grads.astype(wide) * attended_ref[...]
-    totals = total_ref[...]
-
-    def in_parts(column, at):
-        head = column.astype(low).astype(wide)
-        body = (column - head).astype(low).astype(wide)
-        tail = column - head - body
-        return jnp.where(
-            lane == at,
-            head,
-            jnp.where(lane == at + 1, body, jnp.where(lane == at + 2, tail, 0.0)),
-        )
-
-    query_grads = []
-    for half in range(2):
-        mine = (lane >= HEAD) if half else (lane < HEAD)
-        row_term = jnp.sum(jnp.where(mine, products, 0.0), axis=1, keepdims=True)
-        row_total = jnp.sum(
-            jnp.where(lane == 2 * pair + half, totals, 0.0), axis=1, keepdims=True
-        )
-        query_part = jnp.where(mine, queries, jnp.zeros_like(queries))
-        grad_part = jnp.where(mine, grads, jnp.zeros_like(grads))
-        query_side = jnp.concatenate(
-            [query_part, (apart - in_parts(row_total, 3 + 3 * half)).astype(low)], axis=1
-        )
-        grad_side = jnp.concatenate(
-            [grad_part, (-in_parts(row_term, 3 * half)).astype(low)], axis=1
-        )
-        weights = jnp.exp(
-            back_product(key_side[...], query_side) + bias[half, pl.ds(start, pack), :]
-        )
-        grad_block = (weights * back_product(value_side[...], grad_side)).astype(low)
-        grad_scores[LANES : LANES + pack, :] = grad_block
-        grad_v_sum[...] += product(weights.astype(low), grad_part)
-        block_lane = jnp.where(lane == 8 * half + block, 1.0, 0.0).astype(low)
-        grad_k_sum[...] += product(
-            grad_block, jnp.concatenate([query_part, block_lane], axis=1)
-        )
-        query_grads.append(product(keys_turned[HEAD * half : HEAD * (half + 1), :], grad_block))
-        band_sum[half] += grad_scores[near_rows, :].astype(wide)
-    grad_q_ref[...] = jnp.concatenate(query_grads, axis=0).T.astype(grad_q_ref.dtype)
-
-    @pl.when(block == blocks - 1)
-    def _():
-        grad_k_ref[...] = grad_k_sum[:, :LANES].astype(grad_k_ref.dtype)
-        grad_v_ref[...] = grad_v_sum[...].astype(grad_v_ref.dtype)
-        key = lax.broadcasted_iota(jnp.int32, (pack, LANES), 0)
-        which = lax.broadcasted_iota(jnp.int32, (pack, LANES), 1) % 8
-        begin = place[2] - shift + size * which
-        sums = grad_k_sum[:, LANES:]
-        below = jnp.sum(jnp.where(key < begin - LANES, sums, 0.0), axis=0, keepdims=True)
-        above = jnp.sum(jnp.where(key >= begin + reach, sums, 0.0), axis=0, keepdims=True)
-        far_ref[0] = jnp.concatenate([below, above, jnp.zeros((6, LANES), wide)], axis=0)
-        columns = band_ref.shape[2]
-        mirror = (
-            lax.broadcasted_iota(jnp.int32, (size, columns), 0)
-            + lax.broadcasted_iota(jnp.int32, (size, columns), 1)
-            == size - 1
-        ).astype(wide)
-        for half in range(2):
-            flipped = jnp.dot(
-                band_sum[half], mirror, precision=highest, preferred_element_type=wide
-            )
-            turned = pltpu.roll(flipped, 0, 1, stride=1, stride_axis=0)
-            band_ref[0, half : half + 1, :] = jnp.sum(turned, axis=0, keepdims=True)
-        band_ref[0, 2:, :] = jnp.zeros((6, columns), wide)
-
-
-def attend_back(queries, all_keys, all_values, grads, attended, totals, near, place):
-    rows, width = queries.shape
-    pack = all_keys.shape[0]
-    size = block_rows(rows)
-    _, reach, _, columns = table_sizes(size, pack)
-    band = -(-(size + LANES + reach) // LANES) * LANES
-    pairs = width // LANES
-
-    def own(p, i):
-        return (i, p)
-
-    def every(p, i):
-        return (0, p)
-
-    grad_q, grad_k, grad_v, band_sums, far_sums = pl.pallas_call(
-        attend_back_kernel,
-        name="attend_back",
-        grid=(pairs, rows // size),
-        in_specs=[
-            pl.BlockSpec(memory_space=pltpu.SMEM),
-            pl.BlockSpec((size, LANES), own),
-            pl.BlockSpec((pack, LANES), every),
-            pl.BlockSpec((pack, LANES), every),
-            pl.BlockSpec((size, LANES), own),
-            pl.BlockSpec((size, LANES), own),
-            pl.BlockSpec((size, LANES), lambda p, i: (i, 0)),
-            pl.BlockSpec((2, 1, near.shape[2]), lambda p, i: (p, 0, 0)),
-        ],
-        out_specs=[
-            pl.BlockSpec((size, LANES), own),
-            pl.BlockSpec((pack, LANES), every),
-            pl.BlockSpec((pack, LANES), every),
-            pl.BlockSpec((1, 8, band), lambda p, i: (p, 0, 0)),
-            pl.BlockSpec((1, 8, LANES), lambda p, i: (p, 0, 0)),
-        ],
-        out_shape=[
-            jax.ShapeDtypeStruct((rows, width), low),
-            jax.ShapeDtypeStruct((pack, width), low),
-            jax.ShapeDtypeStruct((pack, width), low),
-            jax.ShapeDtypeStruct((pairs, 8, band), wide),
-            jax.ShapeDtypeStruct((pairs, 8, LANES), wide),
-        ],
-        scratch_shapes=[
-            pltpu.VMEM((2, columns, size), wide),
-            pltpu.VMEM((pack, 2 * LANES), low),
-            pltpu.VMEM((pack, 2 * LANES), low),
-            pltpu.VMEM((LANES, pack), low),
-            pltpu.VMEM((LANES + pack + reach, size), low),
-            pltpu.VMEM((pack, 2 * LANES), wide),
-            pltpu.VMEM((pack, LANES), wide),
-            pltpu.VMEM((2, LANES + reach, size), wide),
-        ],
-        compiler_params=pltpu.CompilerParams(vmem_limit_bytes=56 * 2**20),
-        cost_estimate=pl.CostEstimate(
-            flops=20 * rows * pack * width * 2, bytes_accessed=16 * pack * width, transcendentals=0
-        ),
-    )(place, queries, all_keys, all_values, grads, attended, totals, near)
-    offsets = jnp.arange(band, dtype=jnp.int32) - (size - 1) - LANES - place[3]
-    buckets = jnp.arange(BUCKETS, dtype=jnp.int32)
-    onehot = (bucket_of(offsets)[:, None] == buckets[None, :]).astype(wide)
-    near_grad = jnp.dot(
-        band_sums[:, :2].reshape(HEADS, band), onehot, precision=highest, preferred_element_type=wide
-    )
-    far_grad = jnp.sum(far_sums[:, :2, :16].reshape(pairs, 2, 2, 8), axis=3)
-    far_grad = jnp.transpose(far_grad, (0, 2, 1)).reshape(HEADS, 2)
-    grad_table = near_grad + far_grad[:, :1] * (buckets == 15) + far_grad[:, 1:] * (buckets == 31)
-    return grad_q, grad_k, grad_v, grad_table.T
 
 
 SEQ_ROWS = 8
@@ -787,6 +586,680 @@
     )(place, context, third, gains, labels)
 
 
+class Summing:
+    def __init__(self, groups, members, buffers):
+        self.groups = groups
+        self.members = members
+        self.lines = groups // 4
+        self.group = lax.axis_index("batch")
+        self.member = lax.axis_index("seq")
+        self.z = self.group // 4
+        self.y = lax.rem(self.group // 2, 2)
+        self.core = lax.rem(self.group, 2)
+        (
+            self.chip,
+            self.pairs,
+            self.line,
+            self.shares,
+            self.chip_send,
+            self.chip_recv,
+            self.pair_send,
+            self.pair_recv,
+            self.line_send,
+            self.line_recv,
+            self.share_send,
+            self.share_recv,
+        ) = buffers
+        self.stages = 3 + self.lines
+
+    def batch_id(self, offset):
+        return {"batch": self.group + offset}
+
+    def neighbours(self):
+        found = [
+            (None, self.batch_id(1 - 2 * self.core)),
+            (None, self.batch_id(2 - 4 * self.y)),
+            (self.z > 0, self.batch_id(-4)),
+            (self.z < self.lines - 1, self.batch_id(4)),
+        ]
+        for step in range(1, self.members):
+            found.append((None, {"seq": lax.rem(self.member + step, self.members)}))
+        return found
+
+    def greet(self, barrier):
+        for condition, device in self.neighbours():
+            if condition is None:
+                pl.semaphore_signal(barrier, inc=1, device_id=device, device_id_type=MESH)
+            else:
+
+                @pl.when(condition)
+                def _():
+                    pl.semaphore_signal(barrier, inc=1, device_id=device, device_id_type=MESH)
+
+    def greeted(self, barrier):
+        ends = (self.z > 0).astype(jnp.int32) + (self.z < self.lines - 1).astype(jnp.int32)
+        pl.semaphore_wait(barrier, 2 + self.members - 1 + ends)
+
+    def copy(self, source, target, send, recv, device):
+        return pltpu.make_async_remote_copy(
+            src_ref=source,
+            dst_ref=target,
+            send_sem=send,
+            recv_sem=recv,
+            device_id=device,
+            device_id_type=MESH,
+        )
+
+    def chip_copy(self, chunk, source):
+        return self.copy(
+            source,
+            self.chip.at[chunk],
+            self.chip_send.at[chunk],
+            self.chip_recv.at[chunk],
+            self.batch_id(1 - 2 * self.core),
+        )
+
+    def pair_copy(self, chunk):
+        return self.copy(
+            self.chip.at[chunk, :, 1 - self.y],
+            self.pairs.at[chunk],
+            self.pair_send.at[chunk],
+            self.pair_recv.at[chunk],
+            self.batch_id(2 - 4 * self.y),
+        )
+
+    def line_copy(self, chunk, way, first, last, source):
+        return self.copy(
+            source.at[chunk, pl.ds(first, last - first)]
+            if source is self.pairs
+            else source.at[chunk, way, pl.ds(first, last - first)],
+            self.line.at[chunk, way, pl.ds(first, last - first)],
+            self.line_send.at[chunk, way],
+            self.line_recv.at[chunk, way],
+            self.batch_id(-4 if way else 4),
+        )
+
+    def share_copy(self, chunk, step):
+        return self.copy(
+            self.shares.at[chunk, self.member],
+            self.shares.at[chunk, self.member],
+            self.share_send.at[chunk, step - 1],
+            self.share_recv.at[chunk, step - 1],
+            {"seq": lax.rem(self.member + step, self.members)},
+        )
+
+    def start(self, chunk, source):
+        self.chip_copy(chunk, source).start()
+
+    def to_pair(self, chunk, source, own):
+        self.chip_copy(chunk, source).wait()
+        self.chip[chunk] = (self.chip[chunk].astype(wide) + own.astype(wide)).astype(low)
+        self.pair_copy(chunk).start()
+
+    def to_line(self, chunk, step):
+        lines = self.lines
+        if step == 0:
+            self.pair_copy(chunk).wait()
+            self.pairs[chunk] = (
+                self.pairs[chunk].astype(wide) + self.chip[chunk, :, self.y].astype(wide)
+            ).astype(low)
+        for way in range(2):
+            at = lines - 1 - step if way else step
+            first, last = (0, at) if way else (at + 1, lines)
+
+            @pl.when(self.z == at)
+            def _():
+                if step > 0:
+                    kept = (0, at + 1) if way else (at, lines)
+                    self.line_copy(chunk, way, kept[0], kept[1], self.line).wait_recv()
+                    span = pl.ds(first, last - first)
+                    self.line[chunk, way, span] = (
+                        self.line[chunk, way, span].astype(wide)
+                        + self.pairs[chunk, span].astype(wide)
+                    ).astype(low)
+                self.line_copy(
+                    chunk, way, first, last, self.line if step > 0 else self.pairs
+                ).start()
+
+    def to_members(self, chunk, held):
+        lines = self.lines
+        for way in range(2):
+            end = 0 if way else lines - 1
+
+            @pl.when(self.z == end)
+            def _():
+                kept = (0, 1) if way else (lines - 1, lines)
+                self.line_copy(chunk, way, kept[0], kept[1], self.line).wait_recv()
+
+            for step in range(lines - 1):
+                at = lines - 1 - step if way else step
+                first, last = (0, at) if way else (at + 1, lines)
+
+                @pl.when(self.z == at)
+                def _():
+                    self.line_copy(chunk, way, first, last, self.line).wait_send()
+
+        held[...] = self.pairs[chunk, self.z].astype(wide)
+
+        @pl.when(self.z > 0)
+        def _():
+            held[...] += self.line[chunk, 0, self.z].astype(wide)
+
+        @pl.when(self.z < lines - 1)
+        def _():
+            held[...] += self.line[chunk, 1, self.z].astype(wide)
+
+        self.shares[chunk, self.member] = held[...].astype(low)
+        for step in range(1, self.members):
+            self.share_copy(chunk, step).start()
+
+    def result(self, chunk):
+        for step in range(1, self.members):
+            self.share_copy(chunk, step).wait()
+        total = self.shares[chunk, 0].astype(wide)
+        for member in range(1, self.members):
+            total = total + self.shares[chunk, member].astype(wide)
+        return total
+
+
+def summing_scratch(groups, members, chunks, rows, columns):
+    lines = groups // 4
+    return [
+        pltpu.VMEM((chunks, lines, 2, rows, columns), low),
+        pltpu.VMEM((chunks, lines, rows, columns), low),
+        pltpu.VMEM((chunks, 2, lines, rows, columns), low),
+        pltpu.VMEM((chunks, members, rows, columns), low),
+        pltpu.SemaphoreType.DMA((chunks,)),
+        pltpu.SemaphoreType.DMA((chunks,)),
+        pltpu.SemaphoreType.DMA((chunks,)),
+        pltpu.SemaphoreType.DMA((chunks,)),
+        pltpu.SemaphoreType.DMA((chunks, 2)),
+        pltpu.SemaphoreType.DMA((chunks, 2)),
+        pltpu.SemaphoreType.DMA((chunks, max(members - 1, 1))),
+        pltpu.SemaphoreType.DMA((chunks, max(members - 1, 1))),
+    ]
+
+
+def stage_delays(lines):
+    return [1, 3] + [4 + step for step in range(lines - 2)] + [lines + 2, lines + 3]
+
+
+def attend_back_kernel(
+    groups,
+    members,
+    place,
+    q_ref,
+    k_ref,
+    v_ref,
+    grad_ref,
+    attended_ref,
+    total_ref,
+    near_ref,
+    own_turned_ref,
+    all_turned_ref,
+    parts_ref,
+    grad_q_ref,
+    grad_k_ref,
+    grad_v_ref,
+    band_ref,
+    far_ref,
+    feed_sums_ref,
+    pair_sums_ref,
+    bias,
+    key_side,
+    value_side,
+    keys_turned,
+    grad_scores,
+    grad_k_sum,
+    grad_v_sum,
+    band_sum,
+    grad_q_sum,
+    pair_grads,
+    fetched,
+    held,
+    fetch_sem,
+    *buffers,
+):
+    pair = pl.program_id(0)
+    block = pl.program_id(1)
+    blocks = pl.num_programs(1)
+    pairs = pl.num_programs(0)
+    now = pair * blocks + block
+    pack = k_ref.shape[0]
+    size = q_ref.shape[0]
+    middle, reach, lead, width = table_sizes(size, pack)
+    ends = (place[0], place[1])
+    rows_here = size * blocks
+    summing = Summing(groups, members, buffers)
+    first = summing.member * rows_here + block * size
+    shift = lax.rem(summing.member * rows_here, LANES) if size % LANES else 0
+    barrier = pltpu.get_barrier_semaphore()
+    feed_chunks = 2 * parts_ref.shape[3]
+    half_width = fetched.shape[-1]
+    part = fetched.shape[-2]
+    lines = groups // 4
+    delays = stage_delays(lines)
+
+    @pl.when(now == 0)
+    def _():
+        summing.greet(barrier)
+        summing.greeted(barrier)
+
+    def feed_part(chunk, core):
+        return parts_ref.at[
+            :, :, core, chunk // 2, :, pl.ds(pl.multiple_of(lax.rem(chunk, 2) * half_width, LANES), half_width)
+        ]
+
+    def fetch(chunk):
+        slot = lax.rem(chunk, 4)
+        return pltpu.make_async_copy(
+            feed_part(chunk, summing.core), fetched.at[slot], fetch_sem.at[slot]
+        )
+
+    def feed_stage(stage, chunk):
+        if stage == 0:
+            summing.start(chunk, feed_part(chunk, 1 - summing.core))
+            fetch(chunk).start()
+        elif stage == 1:
+            fetch(chunk).wait()
+            summing.to_pair(
+                chunk, feed_part(chunk, 1 - summing.core), fetched[lax.rem(chunk, 4)]
+            )
+        elif stage <= lines:
+            summing.to_line(chunk, stage - 2)
+        elif stage == lines + 1:
+            summing.to_members(chunk, held)
+        else:
+            total = summing.result(chunk)
+            column = pl.multiple_of(lax.rem(chunk, 2) * half_width, LANES)
+            feed_sums_ref[chunk // 2, :, pl.ds(column, half_width)] = total
+
+    def pair_stage(stage, which):
+        chunk = feed_chunks + which
+        if stage == 0:
+            summing.start(chunk, pair_grads.at[which, :, :, 1 - summing.core])
+        elif stage == 1:
+            summing.to_pair(
+                chunk,
+                pair_grads.at[which, :, :, 1 - summing.core],
+                pair_grads[which, :, :, summing.core],
+            )
+        elif stage <= lines:
+            summing.to_line(chunk, stage - 2)
+        elif stage == lines + 1:
+            summing.to_members(chunk, held)
+        else:
+            pair_sums_ref[which] = summing.result(chunk)
+
+    stages = 3 + lines
+    starts = [0] + delays
+    total_steps = pairs * blocks
+
+    def run_stages(step):
+        for stage in reversed(range(stages)):
+            chunk = step - starts[stage]
+
+            @pl.when((chunk >= 0) & (chunk < feed_chunks))
+            def _():
+                feed_stage(stage, chunk)
+
+            late = step - (blocks - 1) - starts[stage]
+
+            @pl.when((late >= 0) & (lax.rem(late + 64 * blocks, blocks) == 0) & (late < total_steps))
+            def _():
+                pair_stage(stage, late // blocks)
+
+    @pl.when(block == 0)
+    def _():
+        places = lax.broadcasted_iota(jnp.int32, (pack, LANES), 0)
+        lane = lax.broadcasted_iota(jnp.int32, (pack, LANES), 1)
+        key_side[:, :LANES] = k_ref[...]
+        ones = (segment_of(places, ends) == lane) | ((lane >= 3) & (lane < 9))
+        key_side[:, LANES:] = ones.astype(wide).astype(low)
+        value_side[:, :LANES] = v_ref[...]
+        value_side[:, LANES:] = (lane < 6).astype(wide).astype(low)
+        keys_turned[...] = k_ref[...].T
+        for half in range(2):
+            row = near_ref[half]
+            before = middle - LANES
+            after = middle + reach
+            bias[half, before:after, :] = turned_biases(row, size, lead).T
+            if before > 0:
+                bias[half, :before, :] = jnp.broadcast_to(row[:, :1], (before, size))
+            if after < width:
+                bias[half, after:, :] = jnp.broadcast_to(row[:, -1:], (width - after, size))
+        grad_scores[...] = jnp.zeros_like(grad_scores)
+        grad_k_sum[...] = jnp.zeros_like(grad_k_sum)
+        grad_v_sum[...] = jnp.zeros_like(grad_v_sum)
+        band_sum[...] = jnp.zeros_like(band_sum)
+
+    lane = lax.broadcasted_iota(jnp.int32, (size, LANES), 1)
+    rows = first + lax.broadcasted_iota(jnp.int32, (size, LANES), 0)
+    apart = jnp.where((segment_of(rows, ends) != lane) & (lane < 3), -far_apart, 0.0)
+    start = pl.multiple_of(middle - (first - shift), LANES)
+    near_rows = pl.ds(pl.multiple_of(first - shift, LANES), LANES + reach)
+    queries = q_ref[...]
+    grads = grad_ref[...]
+    products = grads.astype(wide) * attended_ref[...]
+    totals = total_ref[...]
+
+    def in_parts(column, at):
+        head = column.astype(low).astype(wide)
+        body = (column - head).astype(low).astype(wide)
+        tail = column - head - body
+        return jnp.where(
+            lane == at,
+            head,
+            jnp.where(lane == at + 1, body, jnp.where(lane == at + 2, tail, 0.0)),
+        )
+
+    query_grads = []
+    for half in range(2):
+        mine = (lane >= HEAD) if half else (lane < HEAD)
+        row_term = jnp.sum(jnp.where(mine, products, 0.0), axis=1, keepdims=True)
+        row_total = jnp.sum(
+            jnp.where(lane == 2 * pair + half, totals, 0.0), axis=1, keepdims=True
+        )
+        query_part = jnp.where(mine, queries, jnp.zeros_like(queries))
+        grad_part = jnp.where(mine, grads, jnp.zeros_like(grads))
+        query_side = jnp.concatenate(
+            [query_part, (apart - in_parts(row_total, 3 + 3 * half)).astype(low)], axis=1
+        )
+        grad_side = jnp.concatenate(
+            [grad_part, (-in_parts(row_term, 3 * half)).astype(low)], axis=1
+        )
+        weights = jnp.exp(
+            back_product(key_side[...], query_side) + bias[half, pl.ds(start, pack), :]
+        )
+        grad_block = (weights * back_product(value_side[...], grad_side)).astype(low)
+        grad_scores[LANES : LANES + pack, :] = grad_block
+        grad_v_sum[...] += product(weights.astype(low), grad_part)
+        block_lane = jnp.where(lane == 8 * half + block, 1.0, 0.0).astype(low)
+        grad_k_sum[...] += product(
+            grad_block, jnp.concatenate([query_part, block_lane], axis=1)
+        )
+        query_grads.append(product(keys_turned[HEAD * half : HEAD * (half + 1), :], grad_block))
+        band_sum[half] += grad_scores[near_rows, :].astype(wide)
+    grad_query = jnp.concatenate(query_grads, axis=0).T.astype(low)
+    grad_q_ref[...] = grad_query
+    grad_q_sum[pl.ds(pl.multiple_of(block * size, 64), size), :] = grad_query
+
+    @pl.when(block == blocks - 1)
+    def _():
+        grad_key = grad_k_sum[:, :LANES].astype(low)
+        grad_value = grad_v_sum[...].astype(low)
+        grad_k_ref[...] = grad_key
+        grad_v_ref[...] = grad_value
+        for i, gradient in enumerate(
+            (
+                product(own_turned_ref[...], grad_q_sum[...]),
+                product(all_turned_ref[...], grad_key),
+                product(all_turned_ref[...], grad_value),
+            )
+        ):
+            pair_grads[pair, :, :, :, :, LANES * i : LANES * (i + 1)] = gradient.reshape(
+                lines, 2, 2, part, LANES
+            ).astype(low)
+        key = lax.broadcasted_iota(jnp.int32, (pack, LANES), 0)
+        which = lax.broadcasted_iota(jnp.int32, (pack, LANES), 1) % 8
+        begin = summing.member * rows_here - shift + size * which
+        sums = grad_k_sum[:, LANES:]
+        below = jnp.sum(jnp.where(key < begin - LANES, sums, 0.0), axis=0, keepdims=True)
+        above = jnp.sum(jnp.where(key >= begin + reach, sums, 0.0), axis=0, keepdims=True)
+        far_ref[0] = jnp.concatenate([below, above, jnp.zeros((6, LANES), wide)], axis=0)
+        columns = band_ref.shape[2]
+        mirror = (
+            lax.broadcasted_iota(jnp.int32, (size, columns), 0)
+            + lax.broadcasted_iota(jnp.int32, (size, columns), 1)
+            == size - 1
+        ).astype(wide)
+        for half in range(2):
+            flipped = jnp.dot(
+                band_sum[half], mirror, precision=highest, preferred_element_type=wide
+            )
+            turned = pltpu.roll(flipped, 0, 1, stride=1, stride_axis=0)
+            band_ref[0, half : half + 1, :] = jnp.sum(turned, axis=0, keepdims=True)
+        band_ref[0, 2:, :] = jnp.zeros((6, columns), wide)
+
+    run_stages(now)
+
+    @pl.when(now == total_steps - 1)
+    def _():
+        def drain(step, carry):
+            run_stages(step)
+            return carry
+
+        lax.fori_loop(total_steps, total_steps + starts[-1] + 1, drain, 0)
+
+
+def attend_back(
+    queries, all_keys, all_values, grads, attended, totals, near, place, own_turned, all_turned, parts
+):
+    rows, width = queries.shape
+    pack = all_keys.shape[0]
+    size = block_rows(rows)
+    _, reach, _, columns = table_sizes(size, pack)
+    band = -(-(size + LANES + reach) // LANES) * LANES
+    pairs = width // LANES
+    members = pack // rows
+    pieces = parts.shape[3]
+    part = parts.shape[4]
+    groups = 4 * parts.shape[0]
+    half_width = width // 2
+    chunks = 2 * pieces + pairs
+
+    def own(p, i):
+        return (i, p)
+
+    def every(p, i):
+        return (0, p)
+
+    whole = pl.BlockSpec(memory_space=pltpu.VMEM)
+    grad_q, grad_k, grad_v, band_sums, far_sums, feed_sums, pair_sums = pl.pallas_call(
+        functools.partial(attend_back_kernel, groups, members),
+        name="attend_back",
+        grid=(pairs, rows // size),
+        in_specs=[
+            pl.BlockSpec(memory_space=pltpu.SMEM),
+            pl.BlockSpec((size, LANES), own),
+            pl.BlockSpec((pack, LANES), every),
+            pl.BlockSpec((pack, LANES), every),
+            pl.BlockSpec((size, LANES), own),
+            pl.BlockSpec((size, LANES), own),
+            pl.BlockSpec((size, LANES), lambda p, i: (i, 0)),
+            pl.BlockSpec((2, 1, near.shape[2]), lambda p, i: (p, 0, 0)),
+            whole,
+            whole,
+            pl.BlockSpec(memory_space=pl.ANY),
+        ],
+        out_specs=[
+            pl.BlockSpec((size, LANES), own),
+            pl.BlockSpec((pack, LANES), every),
+            pl.BlockSpec((pack, LANES), every),
+            pl.BlockSpec((1, 8, band), lambda p, i: (p, 0, 0)),
+            pl.BlockSpec((1, 8, LANES), lambda p, i: (p, 0, 0)),
+            whole,
+            whole,
+        ],
+        out_shape=[
+            jax.ShapeDtypeStruct((rows, width), low),
+            jax.ShapeDtypeStruct((pack, width), low),
+            jax.ShapeDtypeStruct((pack, width), low),
+            jax.ShapeDtypeStruct((pairs, 8, band), wide),
+            jax.ShapeDtypeStruct((pairs, 8, LANES), wide),
+            jax.ShapeDtypeStruct((pieces, part, width), wide),
+            jax.ShapeDtypeStruct((pairs, part, half_width), wide),
+        ],
+        scratch_shapes=[
+            pltpu.VMEM((2, columns, size), wide),
+            pltpu.VMEM((pack, 2 * LANES), low),
+            pltpu.VMEM((pack, 2 * LANES), low),
+            pltpu.VMEM((LANES, pack), low),
+            pltpu.VMEM((LANES + pack + reach, size), low),
+            pltpu.VMEM((pack, 2 * LANES), wide),
+            pltpu.VMEM((pack, LANES), wide),
+            pltpu.VMEM((2, LANES + reach, size), wide),
+            pltpu.VMEM((rows, LANES), low),
+            pltpu.VMEM((pairs, groups // 4, 2, 2, part, half_width), low),
+            pltpu.VMEM((4, groups // 4, 2, part, half_width), low),
+            pltpu.VMEM((part, half_width), wide),
+            pltpu.SemaphoreType.DMA((4,)),
+        ]
+        + summing_scratch(groups, members, chunks, part, half_width),
+        compiler_params=pltpu.CompilerParams(
+            collective_id=1, has_side_effects=True, vmem_limit_bytes=62 * 2**20
+        ),
+        cost_estimate=pl.CostEstimate(
+            flops=20 * rows * pack * width * 2, bytes_accessed=16 * pack * width, transcendentals=0
+        ),
+    )(
+        place,
+        queries,
+        all_keys,
+        all_values,
+        grads,
+        attended,
+        totals,
+        near,
+        own_turned,
+        all_turned,
+        parts,
+    )
+    offsets = jnp.arange(band, dtype=jnp.int32) - (size - 1) - LANES - place[3]
+    buckets = jnp.arange(BUCKETS, dtype=jnp.int32)
+    onehot = (bucket_of(offsets)[:, None] == buckets[None, :]).astype(wide)
+    near_grad = jnp.dot(
+        band_sums[:, :2].reshape(HEADS, band), onehot, precision=highest, preferred_element_type=wide
+    )
+    far_grad = jnp.sum(far_sums[:, :2, :16].reshape(pairs, 2, 2, 8), axis=3)
+    far_grad = jnp.transpose(far_grad, (0, 2, 1)).reshape(HEADS, 2)
+    grad_table = near_grad + far_grad[:, :1] * (buckets == 15) + far_grad[:, 1:] * (buckets == 31)
+    return grad_q, grad_k, grad_v, grad_table.T, feed_sums, pair_sums
+
+
+def finish_kernel(
+    groups,
+    members,
+    rows_ref,
+    third_ref,
+    starts_ref,
+    gains_ref,
+    sums_ref,
+    backs_ref,
+    weights,
+    parts,
+    weight_sem,
+    send_sem,
+    recv_sem,
+):
+    count, _, width = third_ref.shape
+    unit = width // count
+    group = lax.axis_index("batch")
+    member = lax.axis_index("seq")
+    partners = []
+    for axis, place, number in (("batch", group, groups), ("seq", member, members)):
+        span = 1
+        while span < number:
+            bit = lax.rem(place // span, 2)
+            partners.append({axis: place + span * (1 - 2 * bit)})
+            span *= 2
+    barrier = pltpu.get_barrier_semaphore()
+    for partner in partners:
+        pl.semaphore_signal(barrier, inc=1, device_id=partner, device_id_type=MESH)
+    copies = [
+        pltpu.make_async_copy(
+            third_ref.at[:, unit * i : unit * (i + 1), :], weights.at[i], weight_sem.at[i]
+        )
+        for i in range(4)
+    ]
+    for copy in copies:
+        copy.start()
+    parts[0] = rows_ref[...]
+    pl.semaphore_wait(barrier, len(partners))
+    for i, partner in enumerate(partners):
+        copy = pltpu.make_async_remote_copy(
+            src_ref=parts.at[2 * i],
+            dst_ref=parts.at[2 * i + 1],
+            send_sem=send_sem.at[i],
+            recv_sem=recv_sem.at[i],
+            device_id=partner,
+            device_id_type=MESH,
+        )
+        copy.start()
+        copy.wait()
+        parts[2 * i + 2] = parts[2 * i] + parts[2 * i + 1]
+    sums = parts[2 * len(partners)]
+    sums_ref[...] = sums
+    for copy in copies:
+        copy.wait()
+
+    def weight(i):
+        return weights[i].reshape(width, width)
+
+    head_row = lax.broadcasted_iota(jnp.int32, (HEAD_ROWS, width), 0)
+    head_mask = head_row == lax.broadcasted_iota(jnp.int32, (HEAD_ROWS, width), 1) // HEAD
+    spread = product(sums[:HEAD_ROWS].astype(low), weight(3))
+    grad_cross_query = jnp.sum(jnp.where(head_mask, spread, 0.0), axis=0, keepdims=True)
+    grad_cross_query = grad_cross_query.astype(low)
+
+    def widened(row):
+        return jnp.broadcast_to(row.astype(wide), (SEQ_ROWS, width))
+
+    start = widened(starts_ref[0:1, :])
+    after_self = widened(starts_ref[3:4, :])
+    grad_rows = back_product(widened(grad_cross_query).astype(low), weight(2))
+    grad_after_self, _ = rms_back(after_self, gains_ref[5:6, :], grad_rows)
+    cross_gain = grad_rows * after_self * rms_factor(after_self)
+    grad_after_self = grad_after_self + widened(sums[HEAD_ROWS : HEAD_ROWS + 1])
+    grad_branch = grad_after_self.astype(low)
+    grad_self_vals = back_product(grad_branch, weight(1)).astype(low)
+    grad_rows = back_product(grad_self_vals, weight(0))
+    grad_start, _ = rms_back(start, gains_ref[4:5, :], grad_rows)
+    self_gain = grad_rows * start * rms_factor(start)
+    for i, row in enumerate(
+        (
+            grad_start + grad_after_self,
+            self_gain,
+            cross_gain,
+            grad_cross_query,
+            grad_branch,
+            grad_self_vals,
+        )
+    ):
+        backs_ref[i : i + 1, :] = row[:1].astype(wide)
+    backs_ref[6:, :] = jnp.zeros((2, width), wide)
+
+
+def finish(rows, third, starts, gains, groups, members):
+    many, width = rows.shape
+    partners = (groups.bit_length() - 1) + (members.bit_length() - 1)
+    count = third.shape[0]
+    whole = pl.BlockSpec(memory_space=pltpu.VMEM)
+    return pl.pallas_call(
+        functools.partial(finish_kernel, groups, members),
+        name="finish",
+        in_specs=[whole, pl.BlockSpec(memory_space=pl.ANY), whole, whole],
+        out_specs=[whole, whole],
+        out_shape=[
+            jax.ShapeDtypeStruct((many, width), wide),
+            jax.ShapeDtypeStruct((8, width), wide),
+        ],
+        scratch_shapes=[
+            pltpu.VMEM((4, count, width // count, width), low),
+            pltpu.VMEM((2 * partners + 1, many, width), wide),
+            pltpu.SemaphoreType.DMA((4,)),
+            pltpu.SemaphoreType.DMA((partners,)),
+            pltpu.SemaphoreType.DMA((partners,)),
+        ],
+        compiler_params=pltpu.CompilerParams(
+            collective_id=2, has_side_effects=True, vmem_limit_bytes=32 * 2**20
+        ),
+        cost_estimate=pl.CostEstimate(
+            flops=2**30, bytes_accessed=8 * width * width, transcendentals=0
+        ),
+    )(rows, third, starts, gains)
+
+
 def seq_exchange(value):
     count = lax.axis_size("seq")
     return [value] + [
@@ -805,16 +1278,6 @@
             chosen = jnp.where((place - me) % count == step, pieces[step], chosen)
         ordered.append(chosen)
     return jnp.concatenate(ordered, axis=0)
-
-
-def seq_sum(value):
-    count = lax.axis_size("seq")
-    total = value.astype(wide)
-    for step in range(1, count):
-        total = total + lax.ppermute(
-            value, "seq", [(i, (i - step) % count) for i in range(count)]
-        ).astype(wide)
-    return total
 
 
 def seq_scatter(value, rows):
@@ -980,7 +1443,7 @@
         encoded = encoded + product(inner_act[j], outer_full[j])
     context = rms_norm(encoded, encoder_gain_full).astype(low)
 
-    third_sizes = [part] * (7 + blocks) + [share]
+    third_blocks = in_blocks(third, [part] * (7 + blocks) + [share])
     (
         embedded,
         loss,
@@ -990,7 +1453,7 @@
         starts,
         decoder_totals,
     ) = decoder_step(
-        context, in_blocks(third, third_sizes), gains, labels, place, groups, members, seqs
+        context, third_blocks, gains, labels, place, groups, members, seqs
     )
     contrastive_loss = loss[0, :1]
     embedded = embedded[:seqs]
@@ -1009,6 +1472,7 @@
 
     count = decoder_rows.shape[0]
     decoder_rows = jnp.pad(decoder_rows, ((0, -count % 16), (0, 0)))
+    decoder_rows = lax.all_gather(decoder_rows, "batch", axis=0, tiled=False)
 
     grad_encoded, grad_encoder_gain = norm_back(encoded, encoder_gain_full, grad_context)
     grad_feed_branch = grad_encoded.astype(low)
@@ -1021,76 +1485,67 @@
     grad_hidden = grad_hidden + grad_encoded
     grad_attn_branch = grad_hidden.astype(low)
     second_grads = jnp.concatenate(
-        [weight_grad(attended_low, grad_attn_branch).astype(low).reshape(groups, part, width)]
+        [weight_grad(attended_low, grad_attn_branch).astype(low).reshape(groups, 1, part, width)]
         + [
-            weight_grad(inner_in, grad_inner_pre[j]).astype(low).reshape(groups, part, width)
+            weight_grad(inner_in, grad_inner_pre[j]).astype(low).reshape(groups, 1, part, width)
             for j in range(blocks)
         ]
         + [
             jnp.concatenate(
                 [weight_grad(inner_act[j], grad_feed_branch).astype(low) for j in range(blocks)],
                 axis=0,
-            ).reshape(groups, share, width)
+            ).reshape(groups, blocks, part, width)
         ],
         axis=1,
-    )
-
-    sums = lax.psum(
-        jnp.concatenate(
-            [decoder_totals[:HEADS], decoder_totals[HEAD_ROWS : HEAD_ROWS + 3], grad_encoder_gain[None]],
-            axis=0,
-        ),
-        ("batch", "seq"),
-    )
+    ).reshape(groups // 4, 2, 2, 1 + 2 * blocks, part, width)
 
     grad_attended = back_product(grad_attn_branch, out_full).astype(low)
-    grad_attended, second_grads = lax.optimization_barrier((grad_attended, second_grads))
-    second_sums = lax.psum_scatter(second_grads, "batch", scatter_dimension=0, tiled=False)
-    grad_query_low, grad_key_low, grad_value_low, grad_table = attend_back(
-        queries, all_keys, all_values, grad_attended, attended, totals, near, place
-    )
-    first_grads = jnp.concatenate(
-        [
-            weight_grad(normed, grad_query_low).astype(low).reshape(groups, part, width),
-            weight_grad(normed_all, grad_key_low).astype(low).reshape(groups, part, width),
-            weight_grad(normed_all, grad_value_low).astype(low).reshape(groups, part, width),
-        ],
-        axis=1,
-    )
-    decoder_rows, grad_query_low = lax.optimization_barrier((decoder_rows, grad_query_low))
-    decoder_rows = lax.all_gather(decoder_rows, "batch", axis=0, tiled=False)
-    first_sums = lax.psum_scatter(first_grads, "batch", scatter_dimension=0, tiled=False)
+    grad_query_low, grad_key_low, grad_value_low, grad_table, second_sums, first_sums = attend_back(
+        queries,
+        all_keys,
+        all_values,
+        grad_attended,
+        attended,
+        totals,
+        near,
+        place,
+        normed.T,
+        normed_all.T,
+        second_grads,
+    )
     grad_normed_all = back_product(grad_key_low, key_value_full[:, :width]) + back_product(
         grad_value_low, key_value_full[:, width:]
     )
-    grad_normed = seq_scatter(grad_normed_all, rows) + back_product(grad_query_low, query_full)
-    grad_inputs, grad_attention_gain = norm_back(inputs, attention_gain_full, grad_normed)
+    grad_normed_own = back_product(grad_query_low, query_full)
+    all_inputs = all_tokens.astype(wide)
+    grad_attention_gain = jnp.sum(
+        grad_normed_all * (all_inputs * rms_factor(all_inputs)), axis=0
+    ) + jnp.sum(grad_normed_own * (inputs * rms_factor(inputs)), axis=0)
+    grad_normed = seq_scatter(grad_normed_all, rows) + grad_normed_own
+    grad_inputs, _ = norm_back(inputs, attention_gain_full, grad_normed)
     grad_inputs = grad_inputs + grad_hidden
+
     table_row = jnp.pad(grad_table.reshape(1, -1), ((0, 0), (0, width - grad_table.size)))
-    last_sums = lax.psum(
-        jnp.concatenate([grad_attention_gain[None], grad_feed_gain[None], table_row], axis=0),
-        ("batch", "seq"),
-    )
-
-    self_value_full = square(third, 0)
-    self_out_full = square(third, part)
-    cross_query_full = square(third, 2 * part)
-    cross_key_full = square(third, 3 * part)
-    grad_cross_query_row = jnp.sum(
-        jnp.where(head_mask, product(sums[:HEADS].astype(low), cross_key_full), 0.0),
+    last_rows = jnp.concatenate(
+        [
+            decoder_totals[: HEAD_ROWS + 3],
+            grad_encoder_gain[None],
+            grad_feed_gain[None],
+            grad_attention_gain[None],
+            table_row,
+        ],
         axis=0,
-        keepdims=True,
-    ).astype(low)
-    grad_after_self, grad_cross_gain = norm_back(
-        after_self, cross_gain_full, back_product(grad_cross_query_row, cross_query_full)
-    )
-    grad_after_self = grad_after_self + sums[HEADS : HEADS + 1]
-    grad_self_branch = grad_after_self.astype(low)
-    grad_self_vals = back_product(grad_self_branch, self_out_full).astype(low)
-    grad_start, grad_self_gain = norm_back(
-        start_row, self_gain_full, back_product(grad_self_vals, self_value_full)
-    )
-    grad_start = (grad_start + grad_after_self)[0]
+    )
+    last_rows = jnp.pad(last_rows, ((0, -last_rows.shape[0] % 8), (0, 0)))
+    sums, backs = finish(last_rows, third_blocks, starts, gains, groups, members)
+    (
+        grad_start,
+        grad_self_gain,
+        grad_cross_gain,
+        grad_cross_query_row,
+        grad_self_branch,
+        grad_self_vals,
+    ) = [backs[i] for i in range(6)]
 
     def mine(values, size=part):
         return lax.dynamic_slice_in_dim(values, group * size, size, values.ndim - 1)
@@ -1124,39 +1579,42 @@
         head_mask[None], att_rows[:, None, :], jnp.zeros((), low)
     ).reshape(-1, width)
 
-    second_sums = seq_sum(second_sums)
-    first_sums = seq_sum(first_sums)
-    inner_sums = jnp.transpose(
-        second_sums[part : part * (1 + blocks)].reshape(blocks, part, width), (1, 0, 2)
-    ).reshape(part, blocks * width)
+    inner_sums = jnp.transpose(second_sums[1 : 1 + blocks], (1, 0, 2)).reshape(
+        part, blocks * width
+    )
+    query_sums, key_sums, value_sums = [
+        jnp.transpose(first_sums[:, :, LANES * i : LANES * (i + 1)], (1, 0, 2)).reshape(part, width)
+        for i in range(3)
+    ]
     key_totals = mine(sums[:HEADS])
+    other_sums = sums[HEAD_ROWS:]
     return (
         contrastive_loss,
         embedded,
         grad_inputs,
-        mine(last_sums[0]),
-        first_sums[:part],
-        first_sums[part : 2 * part],
-        first_sums[2 * part :],
-        second_sums[:part],
-        mine(last_sums[2, : BUCKETS * HEADS], BUCKETS * HEADS // groups).reshape(-1, HEADS),
-        mine(last_sums[1]),
+        mine(other_sums[5]),
+        query_sums,
+        key_sums,
+        value_sums,
+        second_sums[0],
+        mine(other_sums[6, : BUCKETS * HEADS], BUCKETS * HEADS // groups).reshape(-1, HEADS),
+        mine(other_sums[4]),
         inner_sums,
-        second_sums[part * (1 + blocks) :],
-        mine(sums[HEADS + 3]),
+        second_sums[1 + blocks :].reshape(share, width),
+        mine(other_sums[3]),
         mine(grad_start),
         mine(grad_self_gain),
-        outer(self_in, grad_self_vals),
-        outer(self_vals, grad_self_branch),
+        outer(self_in, grad_self_vals[None]),
+        outer(self_vals, grad_self_branch[None]),
         mine(grad_cross_gain),
-        outer(cross_in, grad_cross_query_row),
-        jnp.repeat(key_totals.T, HEAD, axis=1) * cross_query_row.astype(wide),
+        outer(cross_in, grad_cross_query_row[None]),
+        jnp.repeat(key_totals.T, HEAD, axis=1) * cross_query_row.astype(low).astype(wide),
         weight_grad(mine(context_rows), att_heads),
         weight_grad(mine(cross_rows), branch_rows),
-        mine(sums[HEADS + 2]),
+        mine(other_sums[2]),
         weight_grad(mine(second_in_rows), pre_rows),
         weight_grad(mine(act_rows, share), out_rows),
-        mine(sums[HEADS + 1]),
+        mine(other_sums[1]),
         weight_grad(mine(pooled_rows), grad_pooled_rows),
     )
 

time: 690 us -> 588 us (0.85)
  waiting for transfers between devices: 246 us -> 152 us
  Pallas kernels: 150 us -> 228 us
  blocking collectives: 42.8 us -> 0 us
  matrix products: 92.9 us -> 75.6 us
  other arithmetic: 37.6 us -> 24.7 us
    pallas_call x1 -> x2, Pallas kernels: 76.7 us -> 155 us  [the longest x1 136 us: attend_back(): pl.pallas_call(functools.partial(attend_back_kernel, groups, members), na...]
    reduce_scatter x2 -> x0, waiting for transfers between devices: 73.2 us -> none  [the longest x1 73.2 us: shards(): lax.psum_scatter(second_grads, 'batch', scatter_dimension=0, tiled=False)]
    psum x1 -> x0, blocking collectives: 42.8 us -> none  [shards(): lax.psum(jnp.concatenate([grad_attention_gain[None], grad_feed_gain[None]...]
    ppermute x2 -> x0, waiting for transfers between devices: 11.8 us -> none  [seq_sum(): lax.ppermute(value, 'seq', [(i, (i - step) % count) for i in range(count)])]
    dot_general x18 -> x15, matrix products: 36.8 us -> 29.1 us  [weight_grad(): lax.dot_general(left_side, right_side, (((0,), (0,)), ((), ())), preferre...]
    dot_general x15 -> x12, matrix products: 34.5 us -> 26.9 us  [back_product(): lax.dot_general(left_side, right_side, (((1,), (1,)), ((), ())), preferre...]
    unnamed x226 -> x229, local copies, waits for them, and re-layouts: 19.7 us -> 27.2 us
    dot_general x12 -> x11, matrix products: 21.3 us -> 19.3 us  [product(): return jnp.dot(left_side, right_side, preferred_element_type=wide)]
  transfers between devices with their start and end apart: 10 -> 6, of which waited for: 7 -> 5; matrix products, arithmetic and copies ran while one was open for 20% -> 14% of each run, Pallas kernels for 6% -> 34%
where the time goes in v1:
time: 588 us; the launch traced here: 579 us
  Pallas kernels  228 us (39%)
  waiting for transfers between devices  152 us (26%)
  local copies, waits for them, and re-layouts  80.5 us (14%)
  matrix products  75.6 us (13%)
  other arithmetic  24.7 us (4%)
  between operations  15.7 us (3%)
    pallas_call x1, Pallas kernels, attend_back(): pl.pallas_call(functools.partial(attend_back_kernel, groups, members), na...  136 us
    all_gather x1, waiting for transfers between devices, shards(): third = lax.all_gather(third_part, 'batch', axis=0, tiled=False)  68.6 us
    pallas_call x1, Pallas kernels, attend(): pl.pallas_call(attend_kernel, name='attend', grid=(pairs, rows // size),...  41.1 us
    pallas_call x1, Pallas kernels, decoder_step(): pl.pallas_call(functools.partial(decoder_kernel, groups, members, seqs),...  31.5 us
    all_gather x1, waiting for transfers between devices, shards(): second = lax.all_gather(second_part, 'batch', axis=0, tiled=False)  31.4 us
    dot_general x15, matrix products, weight_grad(): lax.dot_general(left_side, right_side, (((0,), (0,)), ((), ())), preferre...  29.1 us
    unnamed x229, local copies, waits for them, and re-layouts  27.2 us
    dot_general x12, matrix products, back_product(): lax.dot_general(left_side, right_side, (((1,), (1,)), ((), ())), preferre...  26.9 us
  transfers between devices with their start and end apart: 6, of which 5 were waited for; matrix products, arithmetic and copies ran while one was open for 14% of the time, Pallas kernels for 34%

profile of v1, /device:TPU:0, one launch (start us, length us, event | category | flops | bytes accessed | tf_op | source)
XLA Modules:
  0.0 579.3 jit_solution(11991684611448488213)
XLA Ops:
  21.2 3.0 collective-permute-start
  29.0 21.2 %collective-permute-done = bf16[768,768]{0,1:T(8,128)(2,1)S(1)} collective-permute-done((bf16[768,768]{0,1:T(8,128)(2,1)S(1)}, bf16[768,768]{0,1:T(8,128)(2,1)S(1)}, u32[]{:S(2)}, u32[]{:S(2)}) %collective-permute-start) | collective-permute-done | bytes 1179680 | tf_op jit(solution)/shard_map/ppermute | solution.py:1266
  51.9 15.0 %all-gather.8.cloned.1.call-done = bf16[768,2432]{1,0:T(8,128)(2,1)} async-done(((bf16[48,2432]{1,0:T(8,128)(2,1)}), bf16[768,2432]{1,0:T(8,128)(2,1)}) %all-gather.8.cloned.1.call-update) | async-done | bytes 3735568 | tf_op jit(solution)/shard_map/all_gather | solution.py:1378
  70.5 2.7 convolution_convert_fusion.11.q_ref
  76.8 4.4 convolution_convert_fusion
  81.2 2.5 fusion.126
  83.7 41.1 %attend.1 = (f32[768,768]{1,0:T(8,128)S(1)}, f32[768,128]{1,0:T(8,128)S(1)}) custom-call(s32[4]{0:T(128)S(1)} %pad_add_fusion.place, bf16[768,768]{1,0:T(8,128)(2,1)S(1)} %convolution_convert_fusion.11.q_ref, bf16[1536,768]{1,0:T(8,128)(2,1)} %get-tuple-element.166.k_ref, bf16[1536,768]{1,0:T(8,128)(2,1)} %get-tuple-element.165.v_ref, ...), custom_call_target="tpu_custom_call" | custom-call | flops 14495514624 | bytes 18874368 | tf_op jit(solution)/shard_map/attend/pallas_call | solution.py:161
  125.5 31.4 %all-gather.10.cloned.1.call-done = bf16[6912,768]{1,0:T(8,128)(2,1)} async-done(((bf16[432,768]{1,0:T(8,128)(2,1)}), bf16[6912,768]{1,0:T(8,128)(2,1)}) %all-gather.10.cloned.1.call-update) | async-done | bytes 10616848 | tf_op jit(solution)/shard_map/all_gather | solution.py:1382
  156.9 3.2 fusion.124
  166.3 3.4 fusion.125
  179.1 2.4 copy.126.context_ref
  181.5 68.6 %all-gather.12.cloned.1.call-done = bf16[11520,768]{1,0:T(8,128)(2,1)} async-done(((bf16[720,768]{1,0:T(8,128)(2,1)}), bf16[11520,768]{1,0:T(8,128)(2,1)}) %all-gather.12.cloned.1.call-update) | async-done | bytes 17694736 | tf_op jit(solution)/shard_map/all_gather | solution.py:1397
  250.1 31.5 %decoder.1 = (f32[8,768]{1,0:T(8,128)}, f32[8,128]{1,0:T(8,128)}, f32[768,768]{1,0:T(8,128)}, f32[15,8,768]{2,1,0:T(8,128)}, bf16[48,768]{1,0:T(8,128)(2,1)}, /*index=5*/f32[8,768]{1,0:T(8,128)}, f32[24,768]{1,0:T(8,128)}) custom-call(s32[4]{0:T(128)} %copy-done.6, bf16[768,768]{1,0:T(8,128)(2,1)} %copy.126.context_ref, bf16[16,720,768]{2,1,0:T(8,128)(2,1)} %bitcast.178, ...), custom_call_target="tpu_custom_call" | custom-call | flops 353894400 | bytes 17694720 | tf_op jit(solution)/shard_map/decoder/pallas_call | solution.py:549
  281.7 3.3 copy.127
  285.0 3.7 multiply_reduce_fusion.1
  290.5 2.4 fusion.36
  292.8 2.8 convolution_convert_fusion.1
  295.6 2.4 fusion.22
  298.0 2.7 convolution_convert_fusion.3
  303.1 3.2 convolution_convert_fusion.4
  306.4 2.3 fusion.29
  308.7 2.8 convolution_convert_fusion.2
  323.4 2.4 multiply_reduce_fusion
  340.1 3.9 copy-done.64
  344.0 136.3 %attend_back.1 = (bf16[768,768]{1,0:T(8,128)(2,1)}, bf16[1536,768]{1,0:T(8,128)(2,1)}, bf16[1536,768]{1,0:T(8,128)(2,1)}, f32[6,8,768]{2,1,0:T(8,128)}, f32[6,8,...) custom-call(s32[4]{0:T(128)} %copy-done.6, bf16[768,768]{1,0:T(8,128)(2,1)} %copy-done.7, ...), custom_call_target="tpu_custom_call" | custom-call | flops 36238786560 | bytes 18874368 | tf_op jit(solution)/shard_map/attend_back/pallas_call | solution.py:1058
  482.9 4.2 fusion.43
  487.5 2.4 fusion.3
  496.0 15.4 %collective-permute-done.1 = bf16[768,768]{0,1:T(8,128)(2,1)S(1)} collective-permute-done((bf16[768,768]{0,1:T(8,128)(2,1)S(1)}, bf16[768,768]{0,1:T(8,128)(2,1)S(1)}, u32[]{:S(2)}, u32[]{:S(2)}) %collective-permute-start.1) | collective-permute-done | bytes 1179680 | tf_op jit(solution)/shard_map/ppermute | solution.py:1289
  511.4 3.0 fusion.8
  514.5 6.0 %copy-done = bf16[11520,768]{1,0:T(8,128)(2,1)S(1)} copy-done((bf16[11520,768]{1,0:T(8,128)(2,1)S(1)}, bf16[11520,768]{1,0:T(8,128)(2,1)}, u32[]{:S(2)}) %copy-start) | copy-done | bytes 17694744
  520.6 19.0 %finish.1 = (f32[24,768]{1,0:T(8,128)S(1)}, f32[8,768]{1,0:T(8,128)S(1)}) custom-call(f32[24,768]{1,0:T(8,128)S(1)} %pad.28.rows_ref, bf16[16,720,768]{2,1,0:T(8,128)(2,1)S(1)} %bitcast.179, f32[8,768]{1,0:T(8,128)S(1)} %copy-done.4, f32[8,768]{1,0:T(8,128)S(1)} %copy-done.3), custom_call_target="tpu_custom_call" | custom-call | flops 1073741824 | bytes 4718592 | tf_op jit(solution)/shard_map/finish/pallas_call | solution.py:1238
  541.9 3.0 copy.148
  (383 shorter events, 112.1 us)
Async XLA Ops:
  7.2 11.9 %copy-start.62 = (bf16[48,3072]{1,0:T(8,128)(2,1)S(1)}, bf16[48,3072]{1,0:T(8,128)(2,1)}, u32[]{:S(2)}) copy-start(bf16[48,3072]{1,0:T(8,128)(2,1)} %param.50) | copy-start | bytes 884740
  7.2 11.9 %copy-start.66 = (bf16[48,768]{1,0:T(8,128)(2,1)S(1)}, bf16[48,768]{1,0:T(8,128)(2,1)}, u32[]{:S(2)}) copy-start(bf16[48,768]{1,0:T(8,128)(2,1)} %param.42) | copy-start | bytes 221188
  7.2 12.0 %copy-start.67 = (bf16[48,768]{1,0:T(8,128)(2,1)S(1)}, bf16[48,768]{1,0:T(8,128)(2,1)}, u32[]{:S(2)}) copy-start(bf16[48,768]{1,0:T(8,128)(2,1)} %param.43) | copy-start | bytes 221188
  7.2 12.0 %copy-start.68 = (bf16[48,768]{1,0:T(8,128)(2,1)S(1)}, bf16[48,768]{1,0:T(8,128)(2,1)}, u32[]{:S(2)}) copy-start(bf16[48,768]{1,0:T(8,128)(2,1)} %param.45) | copy-start | bytes 221188
  7.2 12.0 %copy-start.69 = (bf16[48,768]{1,0:T(8,128)(2,1)S(1)}, bf16[48,768]{1,0:T(8,128)(2,1)}, u32[]{:S(2)}) copy-start(bf16[48,768]{1,0:T(8,128)(2,1)} %param.46) | copy-start | bytes 221188
  7.3 59.6 %all-gather.8.cloned.1.call-start = ((), (), s32[]{:S(2)}) async-start(), calls=%async_computation | async-start | bytes 3969024 | tf_op jit(solution)/shard_map/all_gather | solution.py:1378
  16.1 140.8 %all-gather.10.cloned.1.call-start = ((), (), s32[]{:S(2)}) async-start(), calls=%async_computation.1 | async-start | bytes 11280384 | tf_op jit(solution)/shard_map/all_gather | solution.py:1382
  19.1 231.0 %all-gather.12.cloned.1.call-start = ((), (), s32[]{:S(2)}) async-start(), calls=%async_computation.2 | async-start | bytes 18800640 | tf_op jit(solution)/shard_map/all_gather | solution.py:1397
  20.5 533.3 %all-gather.14.cloned.1.call-start = ((), (), s32[]{:S(2)}) async-start(), calls=%async_computation.3 | async-start | bytes 2506752 | tf_op jit(solution)/shard_map/all_gather | solution.py:1475
  21.2 49.4 %copy-start.13 = (bf16[768,768]{0,1:T(8,128)(2,1)}, bf16[768,768]{0,1:T(8,128)(2,1)S(1)}, u32[]{:S(2)}) copy-start(bf16[768,768]{0,1:T(8,128)(2,1)S(1)} %copy.111) | copy-start | bytes 3538948
  21.2 29.0 %collective-permute-start = (bf16[768,768]{0,1:T(8,128)(2,1)S(1)}, bf16[768,768]{0,1:T(8,128)(2,1)S(1)}, u32[]{:S(2)}, u32[]{:S(2)}) collective-permute-start(bf16[768,768]{0,1:T(8,128)(2,1)S(1)} %copy.111), channel_id=1, source_target_pairs={{0,1},{1,0},{2,3},{3,2},{4,5},{5,4},{6,7},{7,6},{8,9},{9,8},{10,11... | collective-permute-start | bytes 3538952 | tf_op jit(solution)/shard_map/ppermute | solution.py:1266
  26.9 56.7 %copy-start.6 = (s32[4]{0:T(128)}, s32[4]{0:T(128)S(1)}, u32[]{:S(2)}) copy-start(s32[4]{0:T(128)S(1)} %pad_add_fusion.place) | copy-start | bytes 52
  28.3 22.0 %copy-start.78 = (f32[768]{0:T(1024)}, f32[768]{0:T(1024)S(1)}, u32[]{:S(2)}) copy-start(f32[768]{0:T(1024)S(1)} %fusion.39) | copy-start | bytes 9220
  28.4 42.2 %copy-start.76 = (f32[768]{0:T(1024)}, f32[768]{0:T(1024)S(1)}, u32[]{:S(2)}) copy-start(f32[768]{0:T(1024)S(1)} %fusion.101) | copy-start | bytes 9220
  50.3 18.7 %copy-start.19 = (bf16[768,768]{0,1:T(8,128)(2,1)}, bf16[768,768]{0,1:T(8,128)(2,1)S(1)}, u32[]{:S(2)}) copy-start(bf16[768,768]{0,1:T(8,128)(2,1)S(1)} %get-tuple-element.176) | copy-start | bytes 3538948
  51.9 23.4 %copy-start.84 = (f32[1536]{0:T(1024)}, f32[1536]{0:T(1024)S(1)}, u32[]{:S(2)}) copy-start(f32[1536]{0:T(1024)S(1)} %add_rsqrt_fusion) | copy-start | bytes 18436
  68.0 15.6 %copy-start.5 = (f32[12,1,768]{2,1,0:T(1,128)}, f32[12,1,768]{2,1,0:T(1,128)S(1)}, u32[]{:S(2)}) copy-start(f32[12,1,768]{2,1,0:T(1,128)S(1)} %broadcast_in_dim.36.near_ref) | copy-start | bytes 110596
  125.5 203.7 %copy-start.1 = (f32[768,768]{1,0:T(8,128)}, f32[768,768]{1,0:T(8,128)S(1)}, u32[]{:S(2)}) copy-start(f32[768,768]{1,0:T(8,128)S(1)} %get-tuple-element.45.attended_ref) | copy-start | bytes 7077892
  161.4 12.8 %copy-start.11 = (f32[768,768]{0,1:T(8,128)}, f32[768,768]{0,1:T(8,128)S(1)}, u32[]{:S(2)}) copy-start(f32[768,768]{0,1:T(8,128)S(1)} %get-tuple-element.200) | copy-start | bytes 7077892
  344.0 138.3 %copy-start.91 = (s32[768]{0:T(1024)S(1)}, s32[768]{0:T(1024)}, u32[]{:S(2)}) copy-start(s32[768]{0:T(1024)} %fusion.81) | copy-start | bytes 9220
  344.0 138.3 %copy-start.94 = (f32[32]{0:T(128)S(1)}, f32[32]{0:T(128)}, u32[]{:S(2)}) copy-start(f32[32]{0:T(128)} %get-tuple-element.209) | copy-start | bytes 388
  344.0 138.3 %copy-start.95 = (f32[32]{0:T(128)S(1)}, f32[32]{0:T(128)}, u32[]{:S(2)}) copy-start(f32[32]{0:T(128)} %get-tuple-element.210) | copy-start | bytes 388
  489.8 21.5 %copy-start.29 = (f32[1536,768]{0,1:T(8,128)}, f32[1536,768]{0,1:T(8,128)S(1)}, u32[]{:S(2)}) copy-start(f32[1536,768]{0,1:T(8,128)S(1)} %get-tuple-element.205) | copy-start | bytes 14155780
  490.0 21.3 %collective-permute-start.1 = (bf16[768,768]{0,1:T(8,128)(2,1)S(1)}, bf16[768,768]{0,1:T(8,128)(2,1)S(1)}, u32[]{:S(2)}, u32[]{:S(2)}) collective-permute-start(bf16[768,768]{0,1:T(8,128)(2,1)S(1)} %dynamic-slice_convert_fusion), channel_id=1, source_target_pairs={{0,1},{1,0},{2,3},{3,2},{4,5},{5,4},{6,7},{7,6},{8,9},{9,8},{10,11... | collective-permute-start | bytes 3538952 | tf_op jit(solution)/shard_map/ppermute | solution.py:1289
  491.2 20.2 %copy-start.15 = (bf16[768,768]{0,1:T(8,128)(2,1)S(1)}, bf16[768,768]{0,1:T(8,128)(2,1)}, u32[]{:S(2)}) copy-start(bf16[768,768]{0,1:T(8,128)(2,1)} %copy-done.13) | copy-start | bytes 3538948
  491.2 20.1 %copy-start.74 = (f32[768]{0:T(1024)S(1)}, f32[768]{0:T(1024)}, u32[]{:S(2)}) copy-start(f32[768]{0:T(1024)} %copy-done.73) | copy-start | bytes 9220
  491.2 20.1 %copy-start.77 = (f32[768]{0:T(1024)S(1)}, f32[768]{0:T(1024)}, u32[]{:S(2)}) copy-start(f32[768]{0:T(1024)} %copy-done.76) | copy-start | bytes 9220
  491.2 20.1 %copy-start.102 = (bf16[768,768]{1,0:T(8,128)(2,1)S(1)}, bf16[768,768]{1,0:T(8,128)(2,1)}, u32[]{:S(2)}) copy-start(bf16[768,768]{1,0:T(8,128)(2,1)} %get-tuple-element.52) | copy-start | bytes 3538948
  520.5 19.1 %copy-start.79 = (f32[768]{0:T(1024)S(1)}, f32[768]{0:T(1024)}, u32[]{:S(2)}) copy-start(f32[768]{0:T(1024)} %copy-done.78) | copy-start | bytes 9220
  520.5 19.1 %copy-start.18 = (f32[768,768]{0,1:T(8,128)S(1)}, f32[768,768]{0,1:T(8,128)}, u32[]{:S(2)}) copy-start(f32[768,768]{0,1:T(8,128)} %copy-done.17) | copy-start | bytes 7077892
  520.5 19.1 %copy-start.30 = (f32[1536,768]{0,1:T(8,128)S(1)}, f32[1536,768]{0,1:T(8,128)}, u32[]{:S(2)}) copy-start(f32[1536,768]{0,1:T(8,128)} %copy-done.29) | copy-start | bytes 14155780
  520.5 19.1 %copy-start.33 = (f32[768,768]{0,1:T(8,128)S(1)}, f32[768,768]{0,1:T(8,128)}, u32[]{:S(2)}) copy-start(f32[768,768]{0,1:T(8,128)} %get-tuple-element.206) | copy-start | bytes 7077892
  (78 other events, 262.8 us)
Sparse Core Ops, SparseCore 0:
  16.2 50.6 all-gather.7
  69.1 87.7 all-gather.9
  158.5 91.5 all-gather.11
  335.2 46.8 all-gather.13

commit v2 on v1

--- a/solution.py
+++ b/solution.py
@@ -21,6 +21,11 @@
 highest = lax.Precision.HIGHEST
 low = jnp.bfloat16
 wide = jnp.float32
+MESH = pl.DeviceIdType.MESH
+
+
+def rms_factor(values):
+    return lax.rsqrt(jnp.mean(values * values, axis=-1, keepdims=True) + eps_norm)
 
 
 def rms_norm(values, gain_vector):
@@ -96,6 +101,294 @@
 def turned_biases(row, size, lead):
     spread = jnp.broadcast_to(row, (size, row.shape[1]))
     return pltpu.roll(spread, 0, 1, stride=1, stride_axis=0)[:, lead:]
+
+
+class Gathering:
+    def __init__(self, groups, members, sems):
+        self.groups = groups
+        self.members = members
+        self.lines = groups // 4
+        self.group = lax.axis_index("batch")
+        self.member = lax.axis_index("seq")
+        self.z = self.group // 4
+        self.y = lax.rem(self.group // 2, 2)
+        self.core = lax.rem(self.group, 2)
+        self.line_send, self.line_recv, self.pair_sems, self.chip_sems, self.share_sems = sems
+
+    def batch_id(self, offset):
+        return {"batch": self.group + offset}
+
+    def neighbours(self):
+        found = [
+            (None, self.batch_id(1 - 2 * self.core)),
+            (None, self.batch_id(2 - 4 * self.y)),
+            (self.z > 0, self.batch_id(-4)),
+            (self.z < self.lines - 1, self.batch_id(4)),
+        ]
+        for step in range(1, self.members):
+            found.append((None, {"seq": lax.rem(self.member + step, self.members)}))
+        return found
+
+    def greet(self, barrier):
+        for condition, device in self.neighbours():
+            if condition is None:
+                pl.semaphore_signal(barrier, inc=1, device_id=device, device_id_type=MESH)
+            else:
+
+                @pl.when(condition)
+                def _():
+                    pl.semaphore_signal(barrier, inc=1, device_id=device, device_id_type=MESH)
+
+    def greeted(self, barrier):
+        ends = (self.z > 0).astype(jnp.int32) + (self.z < self.lines - 1).astype(jnp.int32)
+        pl.semaphore_wait(barrier, 2 + self.members - 1 + ends)
+
+    def copy(self, source, target, send, recv, device):
+        return pltpu.make_async_remote_copy(
+            src_ref=source,
+            dst_ref=target,
+            send_sem=send,
+            recv_sem=recv,
+            device_id=device,
+            device_id_type=MESH,
+        )
+
+    def line_copy(self, item, source, full, way, step):
+        place = self.z + step if way else self.z - step
+        block = full.at[place, self.y, self.core]
+        return self.copy(
+            source if step == 0 else block,
+            block,
+            self.line_send.at[item, way, step],
+            self.line_recv.at[item, way, step],
+            self.batch_id(-4 if way else 4),
+        )
+
+    def line_sends(self, way, step):
+        if way:
+            return (self.z > 0) & (self.z + step < self.lines)
+        return (self.z < self.lines - 1) & (self.z - step >= 0)
+
+    def line_arrives(self, way, step):
+        return self.z + step < self.lines if way else self.z - step >= 0
+
+    def send_line(self, item, source, full, step):
+        for way in range(2):
+
+            @pl.when(self.line_sends(way, step))
+            def _():
+                self.line_copy(item, source, full, way, step).start()
+
+    def pair_copy(self, item, full):
+        span = full.at[:, self.y, self.core]
+        return self.copy(
+            span,
+            span,
+            self.pair_sems.at[item, 0],
+            self.pair_sems.at[item, 1],
+            self.batch_id(2 - 4 * self.y),
+        )
+
+    def share_copy(self, item, full):
+        span = full.at[:, :, self.core]
+        return self.copy(
+            span,
+            span,
+            self.share_sems.at[item, 0],
+            self.share_sems.at[item, 1],
+            {"seq": 1 - self.member},
+        )
+
+    def chip_copy(self, item, which, full):
+        span = full.at[:, :, self.core]
+        return self.copy(
+            span,
+            span,
+            self.chip_sems.at[item, which, 0],
+            self.chip_sems.at[item, which, 1],
+            self.batch_id(1 - 2 * self.core),
+        )
+
+    def stages(self, split):
+        return self.lines + (3 if split else 2)
+
+    def stage(self, number, item, source, full, other=None):
+        lines = self.lines
+        if number == 0:
+            own = pltpu.make_async_copy(
+                source, full.at[self.z, self.y, self.core], self.chip_sems.at[item, 0, 0]
+            )
+            own.start()
+            self.send_line(item, source, full, 0)
+            own.wait()
+        elif number < lines:
+            for way in range(2):
+
+                @pl.when(self.line_arrives(way, number))
+                def _():
+                    self.line_copy(item, source, full, way, number - 1).wait_recv()
+
+            if number < lines - 1:
+                self.send_line(item, source, full, number)
+            else:
+                self.pair_copy(item, full).start()
+        elif number == lines:
+            self.pair_copy(item, full).wait()
+            if other is not None:
+                self.share_copy(item, full).start()
+            self.chip_copy(item, 0, full).start()
+        elif number == lines + 1 and other is not None:
+            self.share_copy(item, full).wait()
+            self.chip_copy(item, 1, other).start()
+        else:
+            self.chip_copy(item, 0, full).wait()
+            if other is not None:
+                self.chip_copy(item, 1, other).wait()
+            for way in range(2):
+                for step in range(lines - 1):
+
+                    @pl.when(self.line_sends(way, step))
+                    def _():
+                        self.line_copy(item, source, full, way, step).wait_send()
+
+
+def gathering_sems(groups, items):
+    lines = groups // 4
+    return [
+        pltpu.SemaphoreType.DMA((items, 2, lines)),
+        pltpu.SemaphoreType.DMA((items, 2, lines)),
+        pltpu.SemaphoreType.DMA((items, 2)),
+        pltpu.SemaphoreType.DMA((items, 2, 2)),
+        pltpu.SemaphoreType.DMA((items, 2)),
+    ]
+
+
+def joined_rows(blocks):
+    size, width = blocks.shape[-2:]
+    rows = size * math.prod(blocks.shape[:-2])
+    if size % 16:
+        return blocks.astype(wide).reshape(rows, width).astype(low)
+    return blocks.reshape(rows, width)
+
+
+def first_kernel(
+    groups,
+    members,
+    tokens_ref,
+    extra_ref,
+    query_ref,
+    key_ref,
+    value_ref,
+    queries_ref,
+    keys_ref,
+    values_ref,
+    normed_ref,
+    gains_ref,
+    weights_ref,
+    all_tokens,
+    all_extra,
+    all_query,
+    all_key,
+    all_value,
+    token_send,
+    token_recv,
+    *sems,
+):
+    parts = (extra_ref, query_ref, key_ref, value_ref)
+    fulls = (all_extra, all_query, all_key, all_value)
+    gathering = Gathering(groups, members, sems)
+    member = gathering.member
+    rows, width = tokens_ref.shape
+    barrier = pltpu.get_barrier_semaphore()
+    gathering.greet(barrier)
+    gathering.greeted(barrier)
+    copies = []
+    for step in range(1, members):
+        copies.append(
+            pltpu.make_async_remote_copy(
+                src_ref=tokens_ref,
+                dst_ref=all_tokens.at[member],
+                send_sem=token_send.at[step - 1],
+                recv_sem=token_recv.at[step - 1],
+                device_id={"seq": lax.rem(member + step, members)},
+                device_id_type=MESH,
+            )
+        )
+        copies[-1].start()
+    all_tokens[member] = tokens_ref[...]
+
+    def normed(values):
+        values = values.astype(wide)
+        return (values * rms_factor(values) * gains_ref[:1, :]).astype(low)
+
+    def finished(item):
+        if item == 0:
+            total = jnp.zeros((16, width), wide)
+            for z in range(groups // 4):
+                for y in range(2):
+                    for core in range(2):
+                        total = total + all_extra[z, y, core].astype(wide)
+            gains_ref[...] = total
+        elif item == 1:
+            weights_ref[0] = joined_rows(all_query[...])
+            queries_ref[...] = product(normed(tokens_ref[...]), weights_ref[0]).astype(low)
+        elif item == 2:
+            for copy in copies:
+                copy.wait()
+            weights_ref[1] = joined_rows(all_key[...])
+            for part in range(members):
+                span = slice(rows * part, rows * (part + 1))
+                normed_ref[span, :] = normed(all_tokens[part])
+                keys_ref[span, :] = product(normed_ref[span, :], weights_ref[1]).astype(low)
+        else:
+            weights_ref[2] = joined_rows(all_value[...])
+            for part in range(members):
+                span = slice(rows * part, rows * (part + 1))
+                values_ref[span, :] = product(normed_ref[span, :], weights_ref[2]).astype(low)
+
+    stages = gathering.stages(False)
+    for step in range(len(parts) + stages - 1):
+        for stage in reversed(range(stages)):
+            if 0 <= step - stage < len(parts):
+                item = step - stage
+                gathering.stage(stage, item, parts[item], fulls[item])
+        if step - (stages - 1) >= 0:
+            finished(step - (stages - 1))
+
+
+def project(tokens, extra, parts, groups, members):
+    rows, width = tokens.shape
+    whole = pl.BlockSpec(memory_space=pltpu.VMEM)
+    lines = groups // 4
+    items = [extra] + list(parts)
+    pack = members * rows
+    return pl.pallas_call(
+        functools.partial(first_kernel, groups, members),
+        name="project",
+        in_specs=[whole] * 5,
+        out_specs=[whole] * 6,
+        out_shape=[
+            jax.ShapeDtypeStruct((rows, width), low),
+            jax.ShapeDtypeStruct((pack, width), low),
+            jax.ShapeDtypeStruct((pack, width), low),
+            jax.ShapeDtypeStruct((pack, width), low),
+            jax.ShapeDtypeStruct((16, width), wide),
+            jax.ShapeDtypeStruct((3, width, width), low),
+        ],
+        scratch_shapes=[pltpu.VMEM((members,) + tokens.shape, low)]
+        + [pltpu.VMEM((lines, 2, 2) + item.shape, low) for item in items]
+        + [
+            pltpu.SemaphoreType.DMA((max(members - 1, 1),)),
+            pltpu.SemaphoreType.DMA((max(members - 1, 1),)),
+        ]
+        + gathering_sems(groups, len(items)),
+        compiler_params=pltpu.CompilerParams(
+            collective_id=3, has_side_effects=True, vmem_limit_bytes=48 * 2**20
+        ),
+        cost_estimate=pl.CostEstimate(
+            flops=2**31, bytes_accessed=32 * pack * width, transcendentals=0
+        ),
+    )(tokens, extra, *parts)
 
 
 def attend_kernel(
@@ -191,11 +484,6 @@
 
 SEQ_ROWS = 8
 HEAD_ROWS = 16
-MESH = pl.DeviceIdType.MESH
-
-
-def rms_factor(values):
-    return lax.rsqrt(jnp.mean(values * values, axis=-1, keepdims=True) + eps_norm)
 
 
 def rms_back(values, gain_row, grad_rows):
@@ -226,6 +514,7 @@
 
 
 def decoder_kernel(
+    base,
     groups,
     members,
     seqs,
@@ -245,16 +534,22 @@
     everyone,
     shared,
     similar_ref,
+    halves_sent,
+    halves_got,
     weight_sem,
     every_send,
     every_recv,
     share_send,
     share_recv,
+    half_send,
+    half_recv,
 ):
     rows, width = context_ref.shape
     count, _, _ = third_ref.shape
     unit = width // count
-    blocks = 4 * unit
+    halves = 2 if members == 2 else 1
+    feeds = 4 // halves
+    blocks = feeds * unit
     group = lax.axis_index("batch")
     member = lax.axis_index("seq")
     seq_total = groups * seqs
@@ -275,11 +570,11 @@
             device_id_type=MESH,
         )
 
-    sizes = [unit] * 7 + [unit] * 4 + [blocks]
+    sizes = [unit] * 7 + [unit] * feeds + [blocks]
     firsts = [sum(sizes[:i]) for i in range(len(sizes))]
     copies = [
         pltpu.make_async_copy(
-            third_ref.at[:, first : first + size, :],
+            third_ref.at[:, base + first : base + first + size, :],
             weights.at[:, first : first + size, :],
             weight_sem.at[i],
         )
@@ -292,10 +587,30 @@
         return weights[:, firsts[i] : firsts[i] + unit, :].reshape(width, width)
 
     def outer_weight(j):
-        per = count // 4
-        return weights[per * j : per * (j + 1), firsts[11] : firsts[11] + blocks, :].reshape(
+        per = count // feeds
+        return weights[per * j : per * (j + 1), firsts[-1] : firsts[-1] + blocks, :].reshape(
             width, width
         )
+
+    def half_copy(which, first, number):
+        span = pl.ds(first, number)
+        return pltpu.make_async_remote_copy(
+            src_ref=halves_sent.at[span],
+            dst_ref=halves_got.at[span],
+            send_sem=half_send.at[which],
+            recv_sem=half_recv.at[which],
+            device_id={"seq": 1 - member},
+            device_id_type=MESH,
+        )
+
+    def joined(which, part):
+        if halves == 1:
+            return part
+        halves_sent[which] = part
+        copy = half_copy(which, which, 1)
+        copy.start()
+        copy.wait()
+        return part + halves_got[which]
 
     gain = {
         name: gains_ref[i : i + 1, :]
@@ -391,13 +706,14 @@
     copies[5].wait()
     after_cross = after_self + product(cross_low, weight(5))
     second_in = (after_cross * rms_factor(after_cross) * gain["second"]).astype(low)
-    for i in range(7, 12):
-        copies[i].wait()
-    second_pre = [product(second_in, weight(7 + j)) for j in range(4)]
-    second_act = [gelu_value(second_pre[j]).astype(low) for j in range(4)]
-    decoded = after_cross
-    for j in range(4):
-        decoded = decoded + product(second_act[j], outer_weight(j))
+    for copy in copies[7:]:
+        copy.wait()
+    second_pre = [product(second_in, weight(7 + j)) for j in range(feeds)]
+    second_act = [gelu_value(second_pre[j]).astype(low) for j in range(feeds)]
+    second_out = product(second_act[0], outer_weight(0))
+    for j in range(1, feeds):
+        second_out = second_out + product(second_act[j], outer_weight(j))
+    decoded = after_cross + joined(0, second_out)
     pooled_in = (decoded * rms_factor(decoded) * gain["final"]).astype(low)
     copies[6].wait()
     pooled = product(pooled_in, weight(6))
@@ -483,11 +799,17 @@
     grad_second_out = grad_decoded.astype(low)
     grad_second_pre = [
         (gelu_slope(second_pre[j]) * back_product(grad_second_out, outer_weight(j))).astype(low)
-        for j in range(4)
+        for j in range(feeds)
     ]
+    if halves == 2:
+        for j in range(feeds):
+            halves_sent[2 + j] = second_act[j].astype(wide)
+            halves_sent[2 + feeds + j] = grad_second_pre[j].astype(wide)
+        half_copy(2, 2, 2 * feeds).start()
     grad_second_in = back_product(grad_second_pre[0], weight(7))
-    for j in range(1, 4):
+    for j in range(1, feeds):
         grad_second_in = grad_second_in + back_product(grad_second_pre[j], weight(7 + j))
+    grad_second_in = joined(1, grad_second_in)
     grad_after_cross, grad_second_gain = rms_back(after_cross, gain["second"], grad_second_in)
     grad_after_cross = grad_after_cross + grad_decoded
     grad_cross_branch = grad_after_cross.astype(low)
@@ -528,26 +850,40 @@
     totals_ref[HEAD_ROWS:, :] = first_member * by_seq(
         [jnp.sum(grad_after_cross, axis=0, keepdims=True), grad_final_gain, grad_second_gain]
     )
-    for i, piece in enumerate(
-        [cross_low, second_in]
-        + second_act
-        + [pooled_in, grad_cross_branch]
-        + grad_second_pre
-        + [grad_second_out, grad_pooled, grad_cross_att]
+    for i, piece in zip(
+        (0, 1, 6, 7, 12, 13, 14),
+        (
+            cross_low,
+            second_in,
+            pooled_in,
+            grad_cross_branch,
+            grad_second_out,
+            grad_pooled,
+            grad_cross_att,
+        ),
     ):
         pieces_ref[i] = piece.astype(wide)
+    if halves == 2:
+        half_copy(2, 2, 2 * feeds).wait()
+    for first, values, got in ((2, second_act, 2), (8, grad_second_pre, 2 + feeds)):
+        for j in range(feeds):
+            if halves == 1:
+                pieces_ref[first + j] = values[j].astype(wide)
+            else:
+                pieces_ref[first + feeds * member + j] = values[j].astype(wide)
+                pieces_ref[first + feeds * (1 - member) + j] = halves_got[got + j]
     for i, piece in enumerate([start, self_in, self_vals, after_self, cross_in, cross_query]):
         starts_ref[i : i + 1, :] = piece[:1].astype(wide)
     starts_ref[6:, :] = jnp.zeros((2, width), wide)
 
 
-def decoder_step(context, third, gains, labels, place, groups, members, seqs):
+def decoder_step(context, third, base, gains, labels, place, groups, members, seqs):
     rows, width = context.shape
     everything = pl.BlockSpec(memory_space=pltpu.VMEM)
     labels = jnp.pad(labels.astype(wide)[None], ((0, 7), (0, LANES - labels.shape[0])))
     number = groups * SEQ_ROWS
     return pl.pallas_call(
-        functools.partial(decoder_kernel, groups, members, seqs),
+        functools.partial(decoder_kernel, base, groups, members, seqs),
         name="decoder",
         in_specs=[
             pl.BlockSpec(memory_space=pltpu.SMEM),
@@ -567,15 +903,19 @@
             jax.ShapeDtypeStruct((HEAD_ROWS + SEQ_ROWS, width), wide),
         ],
         scratch_shapes=[
-            pltpu.VMEM(third.shape, low),
+            pltpu.VMEM((third.shape[0], third.shape[1] - base, width), low),
             pltpu.VMEM((groups, SEQ_ROWS, width), wide),
             pltpu.VMEM((members, seqs * HEAD_ROWS, width + LANES), wide),
             pltpu.VMEM((number, number), wide),
+            pltpu.VMEM((10, SEQ_ROWS, width), wide),
+            pltpu.VMEM((10, SEQ_ROWS, width), wide),
             pltpu.SemaphoreType.DMA((12,)),
             pltpu.SemaphoreType.DMA,
             pltpu.SemaphoreType.DMA,
             pltpu.SemaphoreType.DMA((max(members - 1, 1),)),
             pltpu.SemaphoreType.DMA((max(members - 1, 1),)),
+            pltpu.SemaphoreType.DMA((3,)),
+            pltpu.SemaphoreType.DMA((3,)),
         ],
         compiler_params=pltpu.CompilerParams(
             collective_id=0, has_side_effects=True, vmem_limit_bytes=56 * 2**20
@@ -1138,6 +1478,7 @@
 
 
 def finish_kernel(
+    base,
     groups,
     members,
     rows_ref,
@@ -1168,7 +1509,7 @@
         pl.semaphore_signal(barrier, inc=1, device_id=partner, device_id_type=MESH)
     copies = [
         pltpu.make_async_copy(
-            third_ref.at[:, unit * i : unit * (i + 1), :], weights.at[i], weight_sem.at[i]
+            third_ref.at[:, base + unit * i : base + unit * (i + 1), :], weights.at[i], weight_sem.at[i]
         )
         for i in range(4)
     ]
@@ -1230,13 +1571,13 @@
     backs_ref[6:, :] = jnp.zeros((2, width), wide)
 
 
-def finish(rows, third, starts, gains, groups, members):
+def finish(rows, third, base, starts, gains, groups, members):
     many, width = rows.shape
     partners = (groups.bit_length() - 1) + (members.bit_length() - 1)
     count = third.shape[0]
     whole = pl.BlockSpec(memory_space=pltpu.VMEM)
     return pl.pallas_call(
-        functools.partial(finish_kernel, groups, members),
+        functools.partial(finish_kernel, base, groups, members),
         name="finish",
         in_specs=[whole, pl.BlockSpec(memory_space=pl.ANY), whole, whole],
         out_specs=[whole, whole],
@@ -1258,26 +1599,6 @@
             flops=2**30, bytes_accessed=8 * width * width, transcendentals=0
         ),
     )(rows, third, starts, gains)
-
-
-def seq_exchange(value):
-    count = lax.axis_size("seq")
-    return [value] + [
-        lax.ppermute(value, "seq", [(i, (i - step) % count) for i in range(count)])
-        for step in range(1, count)
-    ]
-
-
-def in_place_order(pieces):
-    count = len(pieces)
-    me = lax.axis_index("seq")
-    ordered = []
-    for place in range(count):
-        chosen = pieces[0]
-        for step in range(1, count):
-            chosen = jnp.where((place - me) % count == step, pieces[step], chosen)
-        ordered.append(chosen)
-    return jnp.concatenate(ordered, axis=0)
 
 
 def seq_scatter(value, rows):
@@ -1369,19 +1690,35 @@
             second_gain,
             final_gain,
         ],
-        axis=1,
-    )
-    bias_row = jnp.pad(position_bias.reshape(1, -1), ((0, part - 1), (0, 0)))
-    extra = jnp.concatenate([vectors, bias_row], axis=1)
-    extra = jnp.pad(extra, ((0, 0), (0, LANES - extra.shape[1])))
-    first_part = jnp.concatenate([query_weight, key_weight, value_weight, extra], axis=1)
-    first = lax.all_gather(first_part, "batch", axis=0, tiled=True)
+        axis=0,
+    )
+    bias_part = position_bias.reshape(1, -1)
+    bias_size = bias_part.shape[1]
+    extra = jnp.zeros((16, width), low)
+    extra = lax.dynamic_update_slice(extra, vectors, (0, group * part))
+    extra = lax.dynamic_update_slice(extra, bias_part, (8, group * bias_size))
+    queries, all_keys, all_values, normed_all, gains, first_full = project(
+        tokens, extra, [query_weight, key_weight, value_weight], groups, members
+    )
+    normed = lax.dynamic_slice_in_dim(normed_all, own_first, rows)
+    table = gains[8, : BUCKETS * HEADS].reshape(BUCKETS, HEADS).astype(low)
     second_part = jnp.concatenate(
-        [attention_out, column_blocks(feed_inner, width), feed_outer], axis=0
-    )
-    second = lax.all_gather(second_part, "batch", axis=0, tiled=False)
-    third_part = jnp.concatenate(
         [
+            attention_out[None],
+            column_blocks(feed_inner, width).reshape(blocks, part, width),
+            feed_outer.reshape(blocks, part, width),
+        ],
+        axis=0,
+    )
+    halves = 2 if members == 2 else 1
+    half_share = share // halves
+    half_inner = lax.dynamic_slice_in_dim(
+        second_inner.reshape(part, groups, share), member % halves * half_share, half_share, 2
+    ).reshape(part, groups * half_share)
+    half_outer = lax.dynamic_slice_in_dim(second_outer, member % halves * half_share, half_share)
+    rest_part = jnp.concatenate(
+        [
+            second_part.reshape(-1, width),
             self_value,
             self_out,
             cross_query,
@@ -1389,12 +1726,13 @@
             cross_value,
             cross_out,
             pooler_weight,
-            column_blocks(second_inner, width),
-            second_outer,
+            column_blocks(half_inner, width),
+            half_outer,
         ],
         axis=0,
     )
-    third = lax.all_gather(third_part, "batch", axis=0, tiled=False)
+    rest = lax.all_gather(rest_part, "batch", axis=0, tiled=False)
+    second = rest
 
     def square(gathered, at):
         return gathered[:, at : at + part].reshape(groups * part, width)
@@ -1402,7 +1740,6 @@
     def tall(gathered, at):
         return gathered[:, at : at + share].reshape(groups * share, width)
 
-    gains = first[:, 3 * width : 3 * width + 8].astype(wide).T
     (
         attention_gain_full,
         feed_gain_full,
@@ -1413,20 +1750,7 @@
         second_gain_full,
         final_gain_full,
     ) = [gains[i] for i in range(8)]
-    table = first.reshape(groups, part, -1)[
-        :, 0, 3 * width + 8 : 3 * width + 8 + position_bias.size
-    ].reshape(BUCKETS, HEADS)
-    query_full = first[:, :width]
-    key_value_full = first[:, width : 3 * width]
-
-    all_tokens = in_place_order(seq_exchange(tokens))
     inputs = tokens.astype(wide)
-    normed_all = rms_norm(all_tokens.astype(wide), attention_gain_full).astype(low)
-    normed = rms_norm(inputs, attention_gain_full).astype(low)
-    queries = product(normed, query_full).astype(low)
-    keys_values = product(normed_all, key_value_full).astype(low)
-    all_keys = keys_values[:, :width]
-    all_values = keys_values[:, width:]
     near = offset_biases(table, block_rows(rows), pack, place[3])
     attended, totals = attend(queries, all_keys, all_values, near, place)
     attended_low = attended.astype(low)
@@ -1443,7 +1767,11 @@
         encoded = encoded + product(inner_act[j], outer_full[j])
     context = rms_norm(encoded, encoder_gain_full).astype(low)
 
-    third_blocks = in_blocks(third, [part] * (7 + blocks) + [share])
+    third_blocks = in_blocks(
+        rest,
+        [part] * (1 + blocks) + [share] + [part] * (7 + blocks // halves) + [half_share],
+    )
+    base = (1 + 2 * blocks) * (width // third_blocks.shape[0])
     (
         embedded,
         loss,
@@ -1453,7 +1781,7 @@
         starts,
         decoder_totals,
     ) = decoder_step(
-        context, third_blocks, gains, labels, place, groups, members, seqs
+        context, third_blocks, base, gains, labels, place, groups, members, seqs
     )
     contrastive_loss = loss[0, :1]
     embedded = embedded[:seqs]
@@ -1474,14 +1802,14 @@
     decoder_rows = jnp.pad(decoder_rows, ((0, -count % 16), (0, 0)))
     decoder_rows = lax.all_gather(decoder_rows, "batch", axis=0, tiled=False)
 
-    grad_encoded, grad_encoder_gain = norm_back(encoded, encoder_gain_full, grad_context)
+    grad_encoded, _ = norm_back(encoded, encoder_gain_full, grad_context)
     grad_feed_branch = grad_encoded.astype(low)
     grad_inner_pre = [
         gelu_back(inner_pre[j], back_product(grad_feed_branch, outer_full[j])).astype(low)
         for j in range(blocks)
     ]
     grad_inner_in = sum(back_product(grad_inner_pre[j], inner_full[j]) for j in range(blocks))
-    grad_hidden, grad_feed_gain = norm_back(hidden, feed_gain_full, grad_inner_in)
+    grad_hidden, _ = norm_back(hidden, feed_gain_full, grad_inner_in)
     grad_hidden = grad_hidden + grad_encoded
     grad_attn_branch = grad_hidden.astype(low)
     second_grads = jnp.concatenate(
@@ -1513,14 +1841,10 @@
         normed_all.T,
         second_grads,
     )
-    grad_normed_all = back_product(grad_key_low, key_value_full[:, :width]) + back_product(
-        grad_value_low, key_value_full[:, width:]
-    )
-    grad_normed_own = back_product(grad_query_low, query_full)
-    all_inputs = all_tokens.astype(wide)
-    grad_attention_gain = jnp.sum(
-        grad_normed_all * (all_inputs * rms_factor(all_inputs)), axis=0
-    ) + jnp.sum(grad_normed_own * (inputs * rms_factor(inputs)), axis=0)
+    grad_normed_all = back_product(grad_key_low, first_full[1]) + back_product(
+        grad_value_low, first_full[2]
+    )
+    grad_normed_own = back_product(grad_query_low, first_full[0])
     grad_normed = seq_scatter(grad_normed_all, rows) + grad_normed_own
     grad_inputs, _ = norm_back(inputs, attention_gain_full, grad_normed)
     grad_inputs = grad_inputs + grad_hidden
@@ -1529,15 +1853,12 @@
     last_rows = jnp.concatenate(
         [
             decoder_totals[: HEAD_ROWS + 3],
-            grad_encoder_gain[None],
-            grad_feed_gain[None],
-            grad_attention_gain[None],
             table_row,
         ],
         axis=0,
     )
     last_rows = jnp.pad(last_rows, ((0, -last_rows.shape[0] % 8), (0, 0)))
-    sums, backs = finish(last_rows, third_blocks, starts, gains, groups, members)
+    sums, backs = finish(last_rows, third_blocks, base, starts, gains, groups, members)
     (
         grad_start,
         grad_self_gain,
@@ -1562,12 +1883,18 @@
     act_rows = decoder_rows[:, 2 * seqs : (2 + blocks) * seqs].reshape(
         groups, blocks, seqs, width
     )
-    act_rows = jnp.transpose(act_rows, (0, 2, 1, 3)).reshape(groups * seqs, blocks * width)
+    act_rows = jnp.transpose(act_rows, (0, 2, 1, 3)).reshape(
+        groups * seqs, halves, groups, half_share
+    )
+    act_rows = lax.dynamic_slice_in_dim(act_rows, group, 1, 2).reshape(groups * seqs, share)
     at = (2 + blocks) * seqs
     pooled_rows = every_row(at)
     branch_rows = every_row(at + seqs)
     pre_rows = decoder_rows[:, at + 2 * seqs : at + (2 + blocks) * seqs].reshape(
         groups, blocks, seqs, width
+    )
+    pre_rows = jnp.transpose(pre_rows, (0, 2, 1, 3)).reshape(
+        groups * seqs, halves, groups, half_share
     )
     pre_rows = jnp.transpose(pre_rows, (0, 2, 1, 3)).reshape(groups * seqs, blocks * width)
     at = at + (2 + blocks) * seqs
@@ -1588,32 +1915,45 @@
     ]
     key_totals = mine(sums[:HEADS])
     other_sums = sums[HEAD_ROWS:]
+    def gain_grad(gain, *pairs):
+        total = sum(jnp.sum(weight.astype(wide) * grads, axis=1) for weight, grads in pairs)
+        return total / gain.astype(wide)
+
+    cross_key_sums = jnp.repeat(key_totals.T, HEAD, axis=1) * cross_query_row.astype(low).astype(
+        wide
+    )
+    cross_value_sums = weight_grad(mine(context_rows), att_heads)
     return (
         contrastive_loss,
         embedded,
         grad_inputs,
-        mine(other_sums[5]),
+        gain_grad(
+            attention_gain,
+            (query_weight, query_sums),
+            (key_weight, key_sums),
+            (value_weight, value_sums),
+        ),
         query_sums,
         key_sums,
         value_sums,
         second_sums[0],
-        mine(other_sums[6, : BUCKETS * HEADS], BUCKETS * HEADS // groups).reshape(-1, HEADS),
-        mine(other_sums[4]),
+        mine(other_sums[3, : BUCKETS * HEADS], BUCKETS * HEADS // groups).reshape(-1, HEADS),
+        gain_grad(feed_gain, (feed_inner, inner_sums)),
         inner_sums,
         second_sums[1 + blocks :].reshape(share, width),
-        mine(other_sums[3]),
+        gain_grad(encoder_gain, (cross_key, cross_key_sums), (cross_value, cross_value_sums)),
         mine(grad_start),
         mine(grad_self_gain),
         outer(self_in, grad_self_vals[None]),
         outer(self_vals, grad_self_branch[None]),
         mine(grad_cross_gain),
         outer(cross_in, grad_cross_query_row[None]),
-        jnp.repeat(key_totals.T, HEAD, axis=1) * cross_query_row.astype(low).astype(wide),
-        weight_grad(mine(context_rows), att_heads),
+        cross_key_sums,
+        cross_value_sums,
         weight_grad(mine(cross_rows), branch_rows),
         mine(other_sums[2]),
         weight_grad(mine(second_in_rows), pre_rows),
-        weight_grad(mine(act_rows, share), out_rows),
+        weight_grad(act_rows, out_rows),
         mine(other_sums[1]),
         weight_grad(mine(pooled_rows), grad_pooled_rows),
     )

time: 588 us -> 506 us (0.86)
  waiting for transfers between devices: 152 us -> 24.3 us
  Pallas kernels: 228 us -> 306 us
  local copies, waits for them, and re-layouts: 80.5 us -> 63.6 us
  matrix products: 75.6 us -> 65.5 us
    all_gather x3 -> x1, waiting for transfers between devices: 115 us -> 13 us  [shards(): rest = lax.all_gather(rest_part, 'batch', axis=0, tiled=False)]
    pallas_call x2 -> x3, Pallas kernels: 50.6 us -> 129 us  [the longest x1 74.7 us: project(): pl.pallas_call(functools.partial(first_kernel, groups, members), name='pr...]
    ppermute x1 -> x0, waiting for transfers between devices: 21.2 us -> none  [seq_exchange(): lax.ppermute(value, 'seq', [(i, (i - step) % count) for i in range(count)])]
    unnamed x229 -> x205, local copies, waits for them, and re-layouts: 27.2 us -> 19.5 us
    dot_general x11 -> x9, matrix products: 19.3 us -> 11.9 us  [product(): return jnp.dot(left_side, right_side, preferred_element_type=wide)]
    another operation x8 -> x1, local copies, waits for them, and re-layouts: 6.08 us -> 0.04 us  [shards(): jnp.stack([attention_gain, feed_gain, encoder_gain, start_token, self_gai...]
  transfers between devices with their start and end apart: 6 -> 3, of which waited for: 5 -> 2; matrix products, arithmetic and copies ran while one was open for 14% -> 9% of each run, Pallas kernels for 34% -> 55%
where the time goes in v2:
time: 506 us; the launch traced here: 497 us
  Pallas kernels  306 us (60%)
  matrix products  65.5 us (13%)
  local copies, waits for them, and re-layouts  63.6 us (13%)
  waiting for transfers between devices  24.3 us (5%)
  other arithmetic  19.1 us (4%)
  between operations  15.8 us (3%)
    pallas_call x1, Pallas kernels, attend_back(): pl.pallas_call(functools.partial(attend_back_kernel, groups, members), na...  137 us
    pallas_call x1, Pallas kernels, project(): pl.pallas_call(functools.partial(first_kernel, groups, members), name='pr...  74.7 us
    pallas_call x1, Pallas kernels, attend(): pl.pallas_call(attend_kernel, name='attend', grid=(pairs, rows // size),...  40.9 us
    pallas_call x1, Pallas kernels, decoder_step(): pl.pallas_call(functools.partial(decoder_kernel, base, groups, members, s...  33.9 us
    dot_general x15, matrix products, weight_grad(): lax.dot_general(left_side, right_side, (((0,), (0,)), ((), ())), preferre...  29 us
    dot_general x12, matrix products, back_product(): lax.dot_general(left_side, right_side, (((1,), (1,)), ((), ())), preferre...  24.3 us
    pallas_call x1, Pallas kernels, finish(): pl.pallas_call(functools.partial(finish_kernel, base, groups, members), n...  20.1 us
    unnamed x205, local copies, waits for them, and re-layouts  19.5 us
  transfers between devices with their start and end apart: 3, of which 2 were waited for; matrix products, arithmetic and copies ran while one was open for 9% of the time, Pallas kernels for 55%

profile of v2, /device:TPU:0, one launch (start us, length us, event | category | flops | bytes accessed | tf_op | source)
XLA Modules:
  0.0 497.0 jit_solution(8226479770739999785)
XLA Ops:
  17.4 74.7 %project.1 = (bf16[768,768]{1,0:T(8,128)(2,1)S(1)}, bf16[1536,768]{1,0:T(8,128)(2,1)S(1)}, bf16[1536,768]{1,0:T(8,128)(2,1)}, bf16[1536,768]{1,0:T(8,128)(2,1)},...) custom-call(bf16[768,768]{1,0:T(8,128)(2,1)S(1)} %copy-done.1, bf16[16,768]{1,0:T(8,128)(2,1)S(1)} %dynamic_update_slice.7.extra_ref, ...), custom_call_target="tpu_custom_call" | custom-call | flops 2147483648 | bytes 37748736 | tf_op jit(solution)/shard_map/project/pallas_call | solution.py:365
  93.5 4.7 copy.135
  103.6 2.4 dynamic-slice_bitcast_fusion.own_turned_ref
  106.6 40.9 %attend.1 = (f32[768,768]{1,0:T(8,128)S(1)}, f32[768,128]{1,0:T(8,128)S(1)}) custom-call(s32[4]{0:T(128)S(1)} %pad_add_fusion.place, bf16[768,768]{1,0:T(8,128)(2,1)S(1)} %copy-done.16, bf16[1536,768]{1,0:T(8,128)(2,1)} %copy-done.14, bf16[1536,768]{1,0:T(8,128)(2,1)} %get-tuple-element.53.v_ref, f32[12,1,768]{2,1,0:T(1,128)S(1)} %copy-done.12), custom_call_target="tpu_custom_call" | custom-call | flops 14495514624 | bytes 18874368 | tf_op jit(solution)/shard_map/attend/pallas_call | solution.py:454
  148.2 13.0 %all-gather.5.cloned.1.call-done = bf16[15360,768]{1,0:T(8,128)(2,1)} async-done(((bf16[960,768]{1,0:T(8,128)(2,1)}), bf16[15360,768]{1,0:T(8,128)(2,1)}) %all-gather.5.cloned.1.call-update) | async-done | bytes 23592976 | tf_op jit(solution)/shard_map/all_gather | solution.py:1734
  161.2 2.7 fusion.108
  163.9 4.8 fusion.107
  182.5 33.9 %decoder.1 = (f32[8,768]{1,0:T(8,128)}, f32[8,128]{1,0:T(8,128)}, f32[768,768]{1,0:T(8,128)}, f32[15,8,768]{2,1,0:T(8,128)}, bf16[48,768]{1,0:T(8,128)(2,1)}, /*index=5*/f32[8,768]{1,0:T(8,128)}, f32[24,768]{1,0:T(8,128)}) custom-call(s32[4]{0:T(128)} %copy-done.13, bf16[768,768]{1,0:T(8,128)(2,1)} %multiply_convert_fusion.context_ref, ...), custom_call_target="tpu_custom_call" | custom-call | flops 353894400 | bytes 23592960 | tf_op jit(solution)/shard_map/decoder/pallas_call | solution.py:885
  216.4 2.1 multiply_reduce_fusion.1
  220.8 2.2 fusion.27
  223.0 2.4 convolution_convert_fusion
  225.4 2.2 fusion.13
  227.6 2.6 convolution_convert_fusion.2
  230.2 2.2 fusion.6
  232.5 2.4 convolution_convert_fusion.3
  234.9 2.2 fusion.20
  237.0 2.4 convolution_convert_fusion.1
  239.4 2.1 convolution_convert_fusion.5
  242.7 2.1 convolution_convert_fusion.7
  245.9 2.1 convolution_convert_fusion.6
  249.4 2.2 convolution_convert_fusion.4
  254.4 2.1 convolution_convert_fusion.9.grad_ref
  256.5 2.2 convolution_convert_fusion.8
  267.0 3.9 copy-done.60
  270.9 136.7 %attend_back.1 = (bf16[768,768]{1,0:T(8,128)(2,1)}, bf16[1536,768]{1,0:T(8,128)(2,1)}, bf16[1536,768]{1,0:T(8,128)(2,1)}, f32[6,8,768]{2,1,0:T(8,128)}, f32[6,8,...) custom-call(s32[4]{0:T(128)} %copy-done.13, bf16[768,768]{1,0:T(8,128)(2,1)} %copy-done.15, ...), custom_call_target="tpu_custom_call" | custom-call | flops 36238786560 | bytes 18874368 | tf_op jit(solution)/shard_map/attend_back/pallas_call | solution.py:1398
  410.3 20.1 %finish.1 = (f32[24,768]{1,0:T(8,128)S(1)}, f32[8,768]{1,0:T(8,128)S(1)}) custom-call(f32[24,768]{1,0:T(8,128)S(1)} %pad.18.rows_ref, bf16[16,960,768]{2,1,0:T(8,128)(2,1)} %bitcast.177, f32[8,768]{1,0:T(8,128)S(1)} %copy-done.11, f32[16,768]{1,0:T(8,128)S(1)} %copy-done.4), custom_call_target="tpu_custom_call" | custom-call | flops 1073741824 | bytes 4718592 | tf_op jit(solution)/shard_map/finish/pallas_call | solution.py:1579
  432.5 2.1 fusion.37
  434.6 2.0 convolution_add_fusion
  438.5 2.4 collective-permute-start
  453.4 11.2 %collective-permute-done = bf16[768,768]{1,0:T(8,128)(2,1)} collective-permute-done((bf16[768,768]{1,0:T(8,128)(2,1)}, bf16[768,768]{1,0:T(8,128)(2,1)}, u32[]{:S(2)}, u32[]{:S(2)}) %collective-permute-start) | collective-permute-done | bytes 1179680 | tf_op jit(solution)/shard_map/ppermute | solution.py:1610
  464.6 4.3 fusion.30
  468.9 1.9 fusion.29
  (338 shorter events, 85.9 us)
Async XLA Ops:
  7.2 154.0 %all-gather.5.cloned.1.call-start = ((), (), s32[]{:S(2)}) async-start(), calls=%async_computation | async-start | bytes 25067520 | tf_op jit(solution)/shard_map/all_gather | solution.py:1734
  10.5 6.8 %copy-start.1 = (bf16[768,768]{1,0:T(8,128)(2,1)S(1)}, bf16[768,768]{1,0:T(8,128)(2,1)}, u32[]{:S(2)}) copy-start(bf16[768,768]{1,0:T(8,128)(2,1)} %tokens_ref.1) | copy-start | bytes 3538948
  10.5 6.8 %copy-start.5 = (bf16[48,768]{1,0:T(8,128)(2,1)S(1)}, bf16[48,768]{1,0:T(8,128)(2,1)}, u32[]{:S(2)}) copy-start(bf16[48,768]{1,0:T(8,128)(2,1)} %key_ref.1) | copy-start | bytes 221188
  10.6 6.8 %copy-start.7 = (bf16[48,768]{1,0:T(8,128)(2,1)S(1)}, bf16[48,768]{1,0:T(8,128)(2,1)}, u32[]{:S(2)}) copy-start(bf16[48,768]{1,0:T(8,128)(2,1)} %value_ref.1) | copy-start | bytes 221188
  10.6 6.8 %copy-start.9 = (bf16[48,768]{1,0:T(8,128)(2,1)S(1)}, bf16[48,768]{1,0:T(8,128)(2,1)}, u32[]{:S(2)}) copy-start(bf16[48,768]{1,0:T(8,128)(2,1)} %query_ref.1) | copy-start | bytes 221188
  16.4 454.5 %all-gather.7.cloned.1.call-start = ((), (), s32[]{:S(2)}) async-start(), calls=%async_computation.1 | async-start | bytes 2506752 | tf_op jit(solution)/shard_map/all_gather | solution.py:1803
  93.5 9.4 %copy-start.3 = (f32[16,768]{1,0:T(8,128)}, f32[16,768]{1,0:T(8,128)S(1)}, u32[]{:S(2)}) copy-start(f32[16,768]{1,0:T(8,128)S(1)} %get-tuple-element.54.gains_ref) | copy-start | bytes 147460
  99.2 7.3 %copy-start.12 = (f32[12,1,768]{2,1,0:T(1,128)S(1)}, f32[12,1,768]{2,1,0:T(1,128)}, u32[]{:S(2)}) copy-start(f32[12,1,768]{2,1,0:T(1,128)} %broadcast_in_dim.70.near_ref) | copy-start | bytes 110596
  99.2 7.3 %copy-start.16 = (bf16[768,768]{1,0:T(8,128)(2,1)S(1)}, bf16[768,768]{1,0:T(8,128)(2,1)}, u32[]{:S(2)}) copy-start(bf16[768,768]{1,0:T(8,128)(2,1)} %copy-done.15) | copy-start | bytes 3538948
  101.8 45.6 %copy-start.13 = (s32[4]{0:T(128)}, s32[4]{0:T(128)S(1)}, u32[]{:S(2)}) copy-start(s32[4]{0:T(128)S(1)} %pad_add_fusion.place) | copy-start | bytes 52
  148.2 108.3 %copy-start = (f32[768,768]{1,0:T(8,128)}, f32[768,768]{1,0:T(8,128)S(1)}, u32[]{:S(2)}) copy-start(f32[768,768]{1,0:T(8,128)S(1)} %get-tuple-element.55.attended_ref) | copy-start | bytes 7077892
  163.9 10.8 %copy-start.44 = (bf16[4,192,768]{2,1,0:T(8,128)(2,1)}, bf16[4,192,768]{2,1,0:T(8,128)(2,1)S(1)}, u32[]{:S(2)}) copy-start(bf16[4,192,768]{2,1,0:T(8,128)(2,1)S(1)} %get-tuple-element.99) | copy-start | bytes 3538948
  163.9 12.3 %copy-start.46 = (bf16[4,192,768]{2,1,0:T(8,128)(2,1)}, bf16[4,192,768]{2,1,0:T(8,128)(2,1)S(1)}, u32[]{:S(2)}) copy-start(bf16[4,192,768]{2,1,0:T(8,128)(2,1)S(1)} %get-tuple-element.98) | copy-start | bytes 3538948
  163.9 13.9 %copy-start.42 = (bf16[4,192,768]{2,1,0:T(8,128)(2,1)}, bf16[4,192,768]{2,1,0:T(8,128)(2,1)S(1)}, u32[]{:S(2)}) copy-start(bf16[4,192,768]{2,1,0:T(8,128)(2,1)S(1)} %get-tuple-element.97) | copy-start | bytes 3538948
  163.9 15.4 %copy-start.23 = (bf16[4,192,768]{2,1,0:T(8,128)(2,1)}, bf16[4,192,768]{2,1,0:T(8,128)(2,1)S(1)}, u32[]{:S(2)}) copy-start(bf16[4,192,768]{2,1,0:T(8,128)(2,1)S(1)} %get-tuple-element.96) | copy-start | bytes 3538948
  171.3 8.0 %copy-start.29 = (f32[768,768]{1,0:T(8,128)}, f32[768,768]{1,0:T(8,128)S(1)}, u32[]{:S(2)}) copy-start(f32[768,768]{1,0:T(8,128)S(1)} %fusion.118) | copy-start | bytes 7077892
  270.9 138.7 %copy-start.67 = (s32[768]{0:T(1024)S(1)}, s32[768]{0:T(1024)}, u32[]{:S(2)}) copy-start(s32[768]{0:T(1024)} %fusion.68) | copy-start | bytes 9220
  270.9 138.7 %copy-start.83 = (f32[32]{0:T(128)S(1)}, f32[32]{0:T(128)}, u32[]{:S(2)}) copy-start(f32[32]{0:T(128)} %get-tuple-element.140) | copy-start | bytes 388
  270.9 138.7 %copy-start.84 = (f32[32]{0:T(128)S(1)}, f32[32]{0:T(128)}, u32[]{:S(2)}) copy-start(f32[32]{0:T(128)} %get-tuple-element.141) | copy-start | bytes 388
  270.9 139.3 %copy-start.62 = (f32[24,768]{1,0:T(8,128)S(1)}, f32[24,768]{1,0:T(8,128)}, u32[]{:S(2)}) copy-start(f32[24,768]{1,0:T(8,128)} %get-tuple-element.67) | copy-start | bytes 221188
  270.9 139.3 %copy-start.4 = (f32[16,768]{1,0:T(8,128)S(1)}, f32[16,768]{1,0:T(8,128)}, u32[]{:S(2)}) copy-start(f32[16,768]{1,0:T(8,128)} %copy-done.3) | copy-start | bytes 147460
  410.3 21.3 %copy-start.31 = (f32[9,48,768]{2,1,0:T(8,128)S(1)}, f32[9,48,768]{2,1,0:T(8,128)}, u32[]{:S(2)}) copy-start(f32[9,48,768]{2,1,0:T(8,128)} %get-tuple-element.66) | copy-start | bytes 3981316
  410.3 22.2 %copy-start.85 = (bf16[3,768,768]{2,1,0:T(8,128)(2,1)S(1)}, bf16[3,768,768]{2,1,0:T(8,128)(2,1)}, u32[]{:S(2)}) copy-start(bf16[3,768,768]{2,1,0:T(8,128)(2,1)} %get-tuple-element.62) | copy-start | bytes 10616836
  437.9 6.9 %copy-start.70 = (bf16[48]{0:T(256)(128)(2,1)S(1)}, bf16[48]{0:T(256)(128)(2,1)}, u32[]{:S(2)}) copy-start(bf16[48]{0:T(256)(128)(2,1)} %param.30) | copy-start | bytes 292
  437.9 9.2 %copy-start.66 = (f32[8,768]{1,0:T(8,128)S(1)}, f32[8,768]{1,0:T(8,128)}, u32[]{:S(2)}) copy-start(f32[8,768]{1,0:T(8,128)} %get-tuple-element.57) | copy-start | bytes 73732
  438.5 14.1 %copy-start.28 = (f32[4,6,8,768]{3,2,0,1:T(8,128)}, f32[4,6,8,768]{3,2,0,1:T(8,128)S(1)}, u32[]{:S(2)}) copy-start(f32[4,6,8,768]{3,2,0,1:T(8,128)S(1)} %copy.170) | copy-start | bytes 1769476
  438.5 14.1 %copy-start.58 = (bf16[48,768]{1,0:T(8,128)(2,1)S(1)}, bf16[48,768]{1,0:T(8,128)(2,1)}, u32[]{:S(2)}) copy-start(bf16[48,768]{1,0:T(8,128)(2,1)} %param.46) | copy-start | bytes 221188
  438.5 26.0 %collective-permute-start = (bf16[768,768]{1,0:T(8,128)(2,1)}, bf16[768,768]{1,0:T(8,128)(2,1)}, u32[]{:S(2)}, u32[]{:S(2)}) collective-permute-start(bf16[768,768]{1,0:T(8,128)(2,1)} %dynamic-slice_convert_fusion), channel_id=1, source_target_pairs={{0,1},{1,0},{2,3},{3,2},{4,5},{5,4},{6,7},{7,6},{8,9},{9,8},{10,11... | collective-permute-start | bytes 3538952 | tf_op jit(solution)/shard_map/ppermute | solution.py:1610
  441.6 23.0 %copy-start.2 = (bf16[768,768]{1,0:T(8,128)(2,1)S(1)}, bf16[768,768]{1,0:T(8,128)(2,1)}, u32[]{:S(2)}) copy-start(bf16[768,768]{1,0:T(8,128)(2,1)} %tokens_ref.1) | copy-start | bytes 3538948
  441.6 23.0 %copy-start.68 = (f32[768]{0:T(1024)S(1)}, f32[768]{0:T(1024)}, u32[]{:S(2)}) copy-start(f32[768]{0:T(1024)} %get-tuple-element.77) | copy-start | bytes 9220
  481.0 7.3 %copy-start.55 = (bf16[48,768]{1,0:T(8,128)(2,1)S(1)}, bf16[48,768]{1,0:T(8,128)(2,1)}, u32[]{:S(2)}) copy-start(bf16[48,768]{1,0:T(8,128)(2,1)} %param.47) | copy-start | bytes 221188
  481.0 8.4 %copy-start.72 = (bf16[48]{0:T(256)(128)(2,1)S(1)}, bf16[48]{0:T(256)(128)(2,1)}, u32[]{:S(2)}) copy-start(bf16[48]{0:T(256)(128)(2,1)} %param.39) | copy-start | bytes 292
  (65 other events, 229.4 us)
Sparse Core Ops, SparseCore 0:
  16.5 144.6 all-gather.4
  261.0 45.0 all-gather.6

commit v3 on v2

--- a/solution.py
+++ b/solution.py
@@ -527,7 +527,6 @@
     loss_ref,
     grad_context_ref,
     pieces_ref,
-    mixed_ref,
     starts_ref,
     totals_ref,
     weights,
@@ -536,6 +535,7 @@
     similar_ref,
     halves_sent,
     halves_got,
+    piece_rows,
     weight_sem,
     every_send,
     every_recv,
@@ -680,7 +680,6 @@
         total = total + shared[step, :, width + 1 : width + 2] * scale
         mixed = mixed + shared[step, :, :width] * scale
     mixed = (mixed / total).astype(low)
-    mixed_ref[...] = mixed
     log_total = top + jnp.log(total)
 
     def by_seq(parts):
@@ -850,6 +849,11 @@
     totals_ref[HEAD_ROWS:, :] = first_member * by_seq(
         [jnp.sum(grad_after_cross, axis=0, keepdims=True), grad_final_gain, grad_second_gain]
     )
+    def put(at, values):
+        for i in range(seqs):
+            piece_rows[i, pl.ds(at, 1), :] = values[i : i + 1].astype(wide)
+
+    piece_rows[...] = jnp.zeros_like(piece_rows)
     for i, piece in zip(
         (0, 1, 6, 7, 12, 13, 14),
         (
@@ -862,16 +866,19 @@
             grad_cross_att,
         ),
     ):
-        pieces_ref[i] = piece.astype(wide)
+        put(i, piece)
     if halves == 2:
         half_copy(2, 2, 2 * feeds).wait()
     for first, values, got in ((2, second_act, 2), (8, grad_second_pre, 2 + feeds)):
         for j in range(feeds):
             if halves == 1:
-                pieces_ref[first + j] = values[j].astype(wide)
+                put(first + j, values[j])
             else:
-                pieces_ref[first + feeds * member + j] = values[j].astype(wide)
-                pieces_ref[first + feeds * (1 - member) + j] = halves_got[got + j]
+                put(first + feeds * member + j, values[j])
+                put(first + feeds * (1 - member) + j, halves_got[got + j])
+    for i in range(seqs):
+        piece_rows[i, HEAD_ROWS:, :] = mixed[HEAD_ROWS * i : HEAD_ROWS * (i + 1)].astype(wide)
+    pieces_ref[...] = piece_rows[...].astype(low)
     for i, piece in enumerate([start, self_in, self_vals, after_self, cross_in, cross_query]):
         starts_ref[i : i + 1, :] = piece[:1].astype(wide)
     starts_ref[6:, :] = jnp.zeros((2, width), wide)
@@ -892,13 +899,12 @@
             everything,
             everything,
         ],
-        out_specs=[everything] * 7,
+        out_specs=[everything] * 6,
         out_shape=[
             jax.ShapeDtypeStruct((SEQ_ROWS, width), wide),
             jax.ShapeDtypeStruct((8, LANES), wide),
             jax.ShapeDtypeStruct((rows, width), wide),
-            jax.ShapeDtypeStruct((15, SEQ_ROWS, width), wide),
-            jax.ShapeDtypeStruct((seqs * HEAD_ROWS, width), low),
+            jax.ShapeDtypeStruct((seqs, 2 * HEAD_ROWS, width), low),
             jax.ShapeDtypeStruct((8, width), wide),
             jax.ShapeDtypeStruct((HEAD_ROWS + SEQ_ROWS, width), wide),
         ],
@@ -909,6 +915,7 @@
             pltpu.VMEM((number, number), wide),
             pltpu.VMEM((10, SEQ_ROWS, width), wide),
             pltpu.VMEM((10, SEQ_ROWS, width), wide),
+            pltpu.VMEM((seqs, 2 * HEAD_ROWS, width), wide),
             pltpu.SemaphoreType.DMA((12,)),
             pltpu.SemaphoreType.DMA,
             pltpu.SemaphoreType.DMA,
@@ -924,6 +931,358 @@
             flops=2 * rows * width * 300, bytes_accessed=2 * third.size, transcendentals=0
         ),
     )(place, context, third, gains, labels)
+
+
+def feed_weights(rest_ref, out, inner, outer, sem):
+    count, _, width = rest_ref.shape
+    unit = width // count
+    feeds = inner.shape[0]
+    per = count // feeds
+    copies = [pltpu.make_async_copy(rest_ref.at[:, :unit, :], out, sem.at[0])]
+    for j in range(feeds):
+        first = unit * (1 + j)
+        copies.append(
+            pltpu.make_async_copy(
+                rest_ref.at[:, first : first + unit, :], inner.at[j], sem.at[1 + j]
+            )
+        )
+    first = unit * (1 + feeds)
+    for j in range(feeds):
+        copies.append(
+            pltpu.make_async_copy(
+                rest_ref.at[per * j : per * (j + 1), first : first + feeds * unit, :],
+                outer.at[j],
+                sem.at[1 + feeds + j],
+            )
+        )
+    return copies
+
+
+def feed_buffers(rest, feeds):
+    count, _, width = rest.shape
+    unit = width // count
+    return [
+        pltpu.VMEM((count, unit, width), low),
+        pltpu.VMEM((feeds, count, unit, width), low),
+        pltpu.VMEM((feeds, count // feeds, feeds * unit, width), low),
+        pltpu.SemaphoreType.DMA((1 + 2 * feeds,)),
+    ]
+
+
+def feed_kernel(
+    attended_ref,
+    tokens_ref,
+    rest_ref,
+    gains_ref,
+    hidden_ref,
+    pre_ref,
+    encoded_ref,
+    context_ref,
+    out,
+    inner,
+    outer,
+    sem,
+    inner_in,
+):
+    width = tokens_ref.shape[1]
+    feeds = pre_ref.shape[0]
+    copies = feed_weights(rest_ref, out, inner, outer, sem)
+    for copy in copies:
+        copy.start()
+    copies[0].wait()
+    hidden = tokens_ref[...].astype(wide) + product(
+        attended_ref[...].astype(low), out[...].reshape(width, width)
+    )
+    hidden_ref[...] = hidden
+    inner_in[...] = (hidden * rms_factor(hidden) * gains_ref[1:2, :]).astype(low)
+    encoded_ref[...] = hidden
+    for copy in copies[1:]:
+        copy.wait()
+
+    def step(j, carry):
+        pre = product(inner_in[...], inner[j].reshape(width, width))
+        pre_ref[j] = pre.astype(low)
+        encoded_ref[...] += product(
+            gelu_value(pre).astype(low), outer[j].reshape(width, width)
+        )
+        return carry
+
+    lax.fori_loop(0, feeds, step, 0)
+    encoded = encoded_ref[...]
+    context_ref[...] = (encoded * rms_factor(encoded) * gains_ref[2:3, :]).astype(low)
+
+
+def feed_forward(attended, tokens, rest, gains, feeds):
+    rows, width = tokens.shape
+    whole = pl.BlockSpec(memory_space=pltpu.VMEM)
+    return pl.pallas_call(
+        feed_kernel,
+        name="feed_forward",
+        in_specs=[whole, whole, pl.BlockSpec(memory_space=pl.ANY), whole],
+        out_specs=[whole] * 4,
+        out_shape=[
+            jax.ShapeDtypeStruct((rows, width), wide),
+            jax.ShapeDtypeStruct((feeds, rows, width), low),
+            jax.ShapeDtypeStruct((rows, width), wide),
+            jax.ShapeDtypeStruct((rows, width), low),
+        ],
+        scratch_shapes=feed_buffers(rest, feeds) + [pltpu.VMEM((rows, width), low)],
+        compiler_params=pltpu.CompilerParams(vmem_limit_bytes=50 * 2**20),
+        cost_estimate=pl.CostEstimate(
+            flops=18 * rows * width * width, bytes_accessed=40 * width * width, transcendentals=0
+        ),
+    )(attended, tokens, rest, gains)
+
+
+def feed_back_kernel(
+    base,
+    groups,
+    members,
+    grad_context_ref,
+    encoded_ref,
+    hidden_ref,
+    pre_ref,
+    attended_ref,
+    rest_ref,
+    gains_ref,
+    rows_ref,
+    starts_ref,
+    parts_ref,
+    grad_hidden_ref,
+    grad_attended_ref,
+    sums_ref,
+    backs_ref,
+    out,
+    inner,
+    outer,
+    sem,
+    inner_in,
+    grad_branch,
+    grad_inner_in,
+    outer_grad,
+    inner_grad,
+    grad_sem,
+    weights,
+    sides,
+    weight_sem,
+    send_sem,
+    recv_sem,
+):
+    rows, width = encoded_ref.shape
+    feeds = pre_ref.shape[0]
+    count = rest_ref.shape[0]
+    unit = width // count
+    lines = groups // 4
+    group = lax.axis_index("batch")
+    member = lax.axis_index("seq")
+
+    partners = []
+    for axis, place, number in (("batch", group, groups), ("seq", member, members)):
+        span = 1
+        while span < number:
+            bit = lax.rem(place // span, 2)
+            partners.append({axis: place + span * (1 - 2 * bit)})
+            span *= 2
+    barrier = pltpu.get_barrier_semaphore()
+    for partner in partners:
+        pl.semaphore_signal(barrier, inc=1, device_id=partner, device_id_type=MESH)
+
+    def swap(i):
+        return pltpu.make_async_remote_copy(
+            src_ref=sides.at[2 * i],
+            dst_ref=sides.at[2 * i + 1],
+            send_sem=send_sem.at[i],
+            recv_sem=recv_sem.at[i],
+            device_id=partners[i],
+            device_id_type=MESH,
+        )
+
+    def swapped(i):
+        swap(i).wait()
+        sides[2 * i + 2] = sides[2 * i] + sides[2 * i + 1]
+        if i + 1 < len(partners):
+            swap(i + 1).start()
+
+    copies = feed_weights(rest_ref, out, inner, outer, sem)
+    for copy in copies[1 + feeds :] + copies[1 : 1 + feeds] + copies[:1]:
+        copy.start()
+    start_copies = [
+        pltpu.make_async_copy(
+            rest_ref.at[:, base + unit * i : base + unit * (i + 1), :],
+            weights.at[i],
+            weight_sem.at[i],
+        )
+        for i in range(4)
+    ]
+    for copy in start_copies:
+        copy.start()
+    sides[0] = rows_ref[...]
+    hidden = hidden_ref[...]
+    inner_in[...] = (hidden * rms_factor(hidden) * gains_ref[1:2, :]).astype(low)
+    grad_encoded, _ = rms_back(encoded_ref[...], gains_ref[2:3, :], grad_context_ref[...])
+    grad_hidden_ref[...] = grad_encoded
+    grad_branch[...] = grad_encoded.astype(low)
+    grad_inner_in[...] = jnp.zeros_like(grad_inner_in)
+    pl.semaphore_wait(barrier, len(partners))
+    swap(0).start()
+    for copy in copies[1:]:
+        copy.wait()
+
+    def outer_put(j, slot):
+        per = lines // feeds
+        return pltpu.make_async_copy(
+            outer_grad.at[slot],
+            parts_ref.at[pl.ds(j * per, per), :, :, 1 + feeds :],
+            grad_sem.at[0, slot],
+        )
+
+    def inner_put(j, slot):
+        return pltpu.make_async_copy(
+            inner_grad.at[slot], parts_ref.at[:, :, :, 1 + j], grad_sem.at[1, slot]
+        )
+
+    def step(j, carry):
+        slot = lax.rem(j, 2)
+        pre = pre_ref[j].astype(wide)
+        grad_act = back_product(grad_branch[...], outer[j].reshape(width, width))
+        grad_pre = (gelu_slope(pre) * grad_act).astype(low)
+        grad_inner_in[...] += back_product(grad_pre, inner[j].reshape(width, width))
+        act = gelu_value(pre).astype(low)
+
+        @pl.when(j >= 2)
+        def _():
+            outer_put(j - 2, slot).wait()
+            inner_put(j - 2, slot).wait()
+
+        outer_grad[slot] = (
+            weight_grad(act, grad_branch[...]).reshape(outer_grad.shape[1:]).astype(low)
+        )
+        outer_put(j, slot).start()
+        inner_grad[slot] = (
+            weight_grad(inner_in[...], grad_pre).reshape(inner_grad.shape[1:]).astype(low)
+        )
+        inner_put(j, slot).start()
+        for i in range(min(feeds, len(partners))):
+
+            @pl.when(j == i)
+            def _():
+                swapped(i)
+
+        return carry
+
+    lax.fori_loop(0, feeds, step, 0)
+    grad_hidden, _ = rms_back(hidden_ref[...], gains_ref[1:2, :], grad_inner_in[...])
+    grad_hidden = grad_hidden + grad_hidden_ref[...]
+    grad_hidden_ref[...] = grad_hidden
+    grad_branch[...] = grad_hidden.astype(low)
+    copies[0].wait()
+    grad_attended_ref[...] = back_product(
+        grad_branch[...], out[...].reshape(width, width)
+    ).astype(low)
+    for j in range(feeds - 2, feeds):
+        outer_put(j, j % 2).wait()
+        inner_put(j, j % 2).wait()
+    inner_grad[0] = (
+        weight_grad(attended_ref[...].astype(low), grad_branch[...])
+        .reshape(inner_grad.shape[1:])
+        .astype(low)
+    )
+    out_put = pltpu.make_async_copy(
+        inner_grad.at[0], parts_ref.at[:, :, :, 0], grad_sem.at[1, 0]
+    )
+    out_put.start()
+
+    for i in range(feeds, len(partners)):
+        swapped(i)
+    sums = sides[2 * len(partners)]
+    sums_ref[...] = sums
+    for copy in start_copies:
+        copy.wait()
+
+    def weight(i):
+        return weights[i].reshape(width, width)
+
+    head_row = lax.broadcasted_iota(jnp.int32, (HEAD_ROWS, width), 0)
+    head_mask = head_row == lax.broadcasted_iota(jnp.int32, (HEAD_ROWS, width), 1) // HEAD
+    spread = product(sums[:HEAD_ROWS].astype(low), weight(3))
+    grad_cross_query = jnp.sum(jnp.where(head_mask, spread, 0.0), axis=0, keepdims=True)
+    grad_cross_query = grad_cross_query.astype(low)
+
+    def widened(row):
+        return jnp.broadcast_to(row.astype(wide), (SEQ_ROWS, width))
+
+    start = widened(starts_ref[0:1, :])
+    after_self = widened(starts_ref[3:4, :])
+    grad_rows = back_product(widened(grad_cross_query).astype(low), weight(2))
+    grad_after_self, _ = rms_back(after_self, gains_ref[5:6, :], grad_rows)
+    cross_gain = grad_rows * after_self * rms_factor(after_self)
+    grad_after_self = grad_after_self + widened(sums[HEAD_ROWS : HEAD_ROWS + 1])
+    grad_self_branch = grad_after_self.astype(low)
+    grad_self_vals = back_product(grad_self_branch, weight(1)).astype(low)
+    grad_rows = back_product(grad_self_vals, weight(0))
+    grad_start, _ = rms_back(start, gains_ref[4:5, :], grad_rows)
+    self_gain = grad_rows * start * rms_factor(start)
+    for i, row in enumerate(
+        (
+            grad_start + grad_after_self,
+            self_gain,
+            cross_gain,
+            grad_cross_query,
+            grad_self_branch,
+            grad_self_vals,
+        )
+    ):
+        backs_ref[i : i + 1, :] = row[:1].astype(wide)
+    backs_ref[6:, :] = jnp.zeros((2, width), wide)
+    out_put.wait()
+
+
+def feed_back(
+    grad_context, encoded, hidden, pre, attended, rest, base, gains, sum_rows, starts, groups, members, part
+):
+    rows, width = encoded.shape
+    feeds = pre.shape[0]
+    lines = groups // 4
+    count = rest.shape[0]
+    many = sum_rows.shape[0]
+    partners = (groups.bit_length() - 1) + (members.bit_length() - 1)
+    whole = pl.BlockSpec(memory_space=pltpu.VMEM)
+    anywhere = pl.BlockSpec(memory_space=pl.ANY)
+    return pl.pallas_call(
+        functools.partial(feed_back_kernel, base, groups, members),
+        name="feed_back",
+        in_specs=[whole] * 5 + [anywhere] + [whole] * 3,
+        out_specs=[anywhere] + [whole] * 4,
+        out_shape=[
+            jax.ShapeDtypeStruct((lines, 2, 2, 1 + 2 * feeds, part, width), low),
+            jax.ShapeDtypeStruct((rows, width), wide),
+            jax.ShapeDtypeStruct((rows, width), low),
+            jax.ShapeDtypeStruct((many, width), wide),
+            jax.ShapeDtypeStruct((8, width), wide),
+        ],
+        scratch_shapes=feed_buffers(rest, feeds)
+        + [
+            pltpu.VMEM((rows, width), low),
+            pltpu.VMEM((rows, width), low),
+            pltpu.VMEM((rows, width), wide),
+            pltpu.VMEM((2, lines // feeds, 2, 2, feeds, part, width), low),
+            pltpu.VMEM((2, lines, 2, 2, part, width), low),
+            pltpu.SemaphoreType.DMA((2, 2)),
+            pltpu.VMEM((4, count, width // count, width), low),
+            pltpu.VMEM((2 * partners + 1, many, width), wide),
+            pltpu.SemaphoreType.DMA((4,)),
+            pltpu.SemaphoreType.DMA((partners,)),
+            pltpu.SemaphoreType.DMA((partners,)),
+        ],
+        compiler_params=pltpu.CompilerParams(
+            collective_id=2, has_side_effects=True, vmem_limit_bytes=60 * 2**20
+        ),
+        cost_estimate=pl.CostEstimate(
+            flops=36 * rows * width * width, bytes_accessed=80 * width * width, transcendentals=0
+        ),
+    )(
+        grad_context, encoded, hidden, pre, attended, rest, gains, sum_rows, starts
+    )
 
 
 class Summing:
@@ -1141,10 +1500,13 @@
     grad_q_ref,
     grad_k_ref,
     grad_v_ref,
-    band_ref,
-    far_ref,
-    feed_sums_ref,
-    pair_sums_ref,
+    table_ref,
+    out_sums_ref,
+    inner_sums_ref,
+    outer_sums_ref,
+    query_sums_ref,
+    key_sums_ref,
+    value_sums_ref,
     bias,
     key_side,
     value_side,
@@ -1158,6 +1520,15 @@
     fetched,
     held,
     fetch_sem,
+    bands,
+    kept,
+    sent,
+    got,
+    keep_send,
+    keep_recv,
+    tables,
+    table_send,
+    table_recv,
     *buffers,
 ):
     pair = pl.program_id(0)
@@ -1175,15 +1546,11 @@
     shift = lax.rem(summing.member * rows_here, LANES) if size % LANES else 0
     barrier = pltpu.get_barrier_semaphore()
     feed_chunks = 2 * parts_ref.shape[3]
+    feeds = (parts_ref.shape[3] - 1) // 2
     half_width = fetched.shape[-1]
     part = fetched.shape[-2]
     lines = groups // 4
     delays = stage_delays(lines)
-
-    @pl.when(now == 0)
-    def _():
-        summing.greet(barrier)
-        summing.greeted(barrier)
 
     def feed_part(chunk, core):
         return parts_ref.at[
@@ -1211,8 +1578,22 @@
             summing.to_members(chunk, held)
         else:
             total = summing.result(chunk)
+            piece = chunk // 2
             column = pl.multiple_of(lax.rem(chunk, 2) * half_width, LANES)
-            feed_sums_ref[chunk // 2, :, pl.ds(column, half_width)] = total
+
+            @pl.when(piece == 0)
+            def _():
+                out_sums_ref[:, pl.ds(column, half_width)] = total
+
+            @pl.when((piece > 0) & (piece <= feeds))
+            def _():
+                at = pl.multiple_of((piece - 1) * 2 * half_width + column, LANES)
+                inner_sums_ref[:, pl.ds(at, half_width)] = total
+
+            @pl.when(piece > feeds)
+            def _():
+                at = pl.multiple_of((piece - 1 - feeds) * part, 8)
+                outer_sums_ref[pl.ds(at, part), pl.ds(column, half_width)] = total
 
     def pair_stage(stage, which):
         chunk = feed_chunks + which
@@ -1229,7 +1610,71 @@
         elif stage == lines + 1:
             summing.to_members(chunk, held)
         else:
-            pair_sums_ref[which] = summing.result(chunk)
+            total = summing.result(chunk)
+            span = pl.ds(pl.multiple_of(which * LANES, LANES), LANES)
+            for i, sums_ref in enumerate((query_sums_ref, key_sums_ref, value_sums_ref)):
+                sums_ref[:, span] = total[:, LANES * i : LANES * (i + 1)]
+
+    def keep_copy(which, step):
+        return summing.copy(
+            sent.at[which, step - 1],
+            got.at[which, step - 1],
+            keep_send.at[which, step - 1],
+            keep_recv.at[which, step - 1],
+            {"seq": lax.rem(summing.member + step, members)},
+        )
+
+    def keep_result(which):
+        total = [kept[lax.rem(which, 2), i] for i in range(2)]
+        for step in range(1, members):
+            keep_copy(which, step).wait()
+            total = [total[i] + got[which, step - 1, i].astype(wide) for i in range(2)]
+        span = pl.ds(pl.multiple_of(which * LANES, LANES), LANES)
+        grad_k_ref[:, span] = total[0].astype(low)
+        grad_v_ref[:, span] = total[1].astype(low)
+
+    partners = []
+    for axis, spot, number in (
+        ("batch", summing.group, groups),
+        ("seq", summing.member, members),
+    ):
+        reach_out = 1
+        while reach_out < number:
+            bit = lax.rem(spot // reach_out, 2)
+            partners.append({axis: spot + reach_out * (1 - 2 * bit)})
+            reach_out *= 2
+
+    def swap(i):
+        return summing.copy(
+            tables.at[2 * i],
+            tables.at[2 * i + 1],
+            table_send.at[i],
+            table_recv.at[i],
+            partners[i],
+        )
+
+    def swapped(i):
+        swap(i).wait()
+        tables[2 * i + 2] = tables[2 * i] + tables[2 * i + 1]
+        if i + 1 < len(partners):
+            swap(i + 1).start()
+
+    @pl.when(now == 0)
+    def _():
+        peers = summing.neighbours()
+        for i in range(len(partners)):
+            peers.append((None, partners[i]))
+        for condition, device in peers:
+            if condition is None:
+                pl.semaphore_signal(barrier, inc=1, device_id=device, device_id_type=MESH)
+            else:
+
+                @pl.when(condition)
+                def _():
+                    pl.semaphore_signal(barrier, inc=1, device_id=device, device_id_type=MESH)
+
+        edges = (summing.z > 0).astype(jnp.int32) + (summing.z < lines - 1).astype(jnp.int32)
+        pl.semaphore_wait(barrier, 2 + members - 1 + edges + len(partners))
 
     stages = 3 + lines
     starts = [0] + delays
@@ -1248,6 +1693,11 @@
             @pl.when((late >= 0) & (lax.rem(late + 64 * blocks, blocks) == 0) & (late < total_steps))
             def _():
                 pair_stage(stage, late // blocks)
+
+    @pl.when(now == 0)
+    def _():
+        tables[0] = jnp.zeros_like(tables[0])
+        bands[...] = jnp.zeros_like(bands)
 
     @pl.when(block == 0)
     def _():
@@ -1328,8 +1778,19 @@
     def _():
         grad_key = grad_k_sum[:, :LANES].astype(low)
         grad_value = grad_v_sum[...].astype(low)
-        grad_k_ref[...] = grad_key
-        grad_v_ref[...] = grad_value
+
+        @pl.when(pair > 0)
+        def _():
+            keep_result(pair - 1)
+
+        for step in range(1, members):
+            other = pl.multiple_of(lax.rem(summing.member + step, members) * rows_here, 64)
+            sent[pair, step - 1, 0] = grad_k_sum[pl.ds(other, rows_here), :LANES].astype(low)
+            sent[pair, step - 1, 1] = grad_v_sum[pl.ds(other, rows_here), :].astype(low)
+            keep_copy(pair, step).start()
+        mine_rows = pl.ds(pl.multiple_of(summing.member * rows_here, 64), rows_here)
+        kept[lax.rem(pair, 2), 0] = grad_k_sum[mine_rows, :LANES]
+        kept[lax.rem(pair, 2), 1] = grad_v_sum[mine_rows, :]
         for i, gradient in enumerate(
             (
                 product(own_turned_ref[...], grad_q_sum[...]),
@@ -1346,30 +1807,57 @@
         sums = grad_k_sum[:, LANES:]
         below = jnp.sum(jnp.where(key < begin - LANES, sums, 0.0), axis=0, keepdims=True)
         above = jnp.sum(jnp.where(key >= begin + reach, sums, 0.0), axis=0, keepdims=True)
-        far_ref[0] = jnp.concatenate([below, above, jnp.zeros((6, LANES), wide)], axis=0)
-        columns = band_ref.shape[2]
+        columns = bands.shape[1]
         mirror = (
             lax.broadcasted_iota(jnp.int32, (size, columns), 0)
             + lax.broadcasted_iota(jnp.int32, (size, columns), 1)
             == size - 1
         ).astype(wide)
+        row_lane = lax.broadcasted_iota(jnp.int32, (1, LANES), 1)
         for half in range(2):
             flipped = jnp.dot(
                 band_sum[half], mirror, precision=highest, preferred_element_type=wide
             )
             turned = pltpu.roll(flipped, 0, 1, stride=1, stride_axis=0)
-            band_ref[0, half : half + 1, :] = jnp.sum(turned, axis=0, keepdims=True)
-        band_ref[0, 2:, :] = jnp.zeros((6, columns), wide)
+            head = pl.ds(2 * pair + half, 1)
+            bands[head, :] = jnp.sum(turned, axis=0, keepdims=True)
+            own_lanes = row_lane // 8 == half
+            low_sum = jnp.sum(jnp.where(own_lanes, below, 0.0), axis=1, keepdims=True)
+            high_sum = jnp.sum(jnp.where(own_lanes, above, 0.0), axis=1, keepdims=True)
+            tables[0, head, :] = jnp.where(row_lane == 15, low_sum, 0.0) + jnp.where(
+                row_lane == 31, high_sum, 0.0
+            )
 
     run_stages(now)
 
     @pl.when(now == total_steps - 1)
     def _():
+        columns = bands.shape[1]
+        offset = (
+            lax.broadcasted_iota(jnp.int32, (columns, LANES), 0) - (size - 1) - LANES - shift
+        )
+        onehot = (
+            bucket_of(offset) == lax.broadcasted_iota(jnp.int32, (columns, LANES), 1)
+        ).astype(wide)
+        tables[0] += jnp.dot(
+            bands[...], onehot, precision=highest, preferred_element_type=wide
+        )
+        swap(0).start()
+
         def drain(step, carry):
             run_stages(step)
+            for i in range(len(partners)):
+
+                @pl.when(step == total_steps + i)
+                def _():
+                    swapped(i)
+
             return carry
 
-        lax.fori_loop(total_steps, total_steps + starts[-1] + 1, drain, 0)
+        final = max(starts[-1] + 1, len(partners))
+        lax.fori_loop(total_steps, total_steps + final, drain, 0)
+        keep_result(pairs - 1)
+        table_ref[...] = tables[2 * len(partners)]
 
 
 def attend_back(
@@ -1395,7 +1883,9 @@
         return (0, p)
 
     whole = pl.BlockSpec(memory_space=pltpu.VMEM)
-    grad_q, grad_k, grad_v, band_sums, far_sums, feed_sums, pair_sums = pl.pallas_call(
+    partners = (groups.bit_length() - 1) + (members.bit_length() - 1)
+    feeds = (pieces - 1) // 2
+    return pl.pallas_call(
         functools.partial(attend_back_kernel, groups, members),
         name="attend_back",
         grid=(pairs, rows // size),
@@ -1414,21 +1904,19 @@
         ],
         out_specs=[
             pl.BlockSpec((size, LANES), own),
-            pl.BlockSpec((pack, LANES), every),
-            pl.BlockSpec((pack, LANES), every),
-            pl.BlockSpec((1, 8, band), lambda p, i: (p, 0, 0)),
-            pl.BlockSpec((1, 8, LANES), lambda p, i: (p, 0, 0)),
-            whole,
-            whole,
-        ],
+        ]
+        + [whole] * 9,
         out_shape=[
             jax.ShapeDtypeStruct((rows, width), low),
-            jax.ShapeDtypeStruct((pack, width), low),
-            jax.ShapeDtypeStruct((pack, width), low),
-            jax.ShapeDtypeStruct((pairs, 8, band), wide),
-            jax.ShapeDtypeStruct((pairs, 8, LANES), wide),
-            jax.ShapeDtypeStruct((pieces, part, width), wide),
-            jax.ShapeDtypeStruct((pairs, part, half_width), wide),
+            jax.ShapeDtypeStruct((rows, width), low),
+            jax.ShapeDtypeStruct((rows, width), low),
+            jax.ShapeDtypeStruct((16, LANES), wide),
+            jax.ShapeDtypeStruct((part, width), wide),
+            jax.ShapeDtypeStruct((part, feeds * width), wide),
+            jax.ShapeDtypeStruct((feeds * part, width), wide),
+            jax.ShapeDtypeStruct((part, width), wide),
+            jax.ShapeDtypeStruct((part, width), wide),
+            jax.ShapeDtypeStruct((part, width), wide),
         ],
         scratch_shapes=[
             pltpu.VMEM((2, columns, size), wide),
@@ -1444,6 +1932,15 @@
             pltpu.VMEM((4, groups // 4, 2, part, half_width), low),
             pltpu.VMEM((part, half_width), wide),
             pltpu.SemaphoreType.DMA((4,)),
+            pltpu.VMEM((16, band), wide),
+            pltpu.VMEM((2, 2, rows, LANES), wide),
+            pltpu.VMEM((pairs, max(members - 1, 1), 2, rows, LANES), low),
+            pltpu.VMEM((pairs, max(members - 1, 1), 2, rows, LANES), low),
+            pltpu.SemaphoreType.DMA((pairs, max(members - 1, 1))),
+            pltpu.SemaphoreType.DMA((pairs, max(members - 1, 1))),
+            pltpu.VMEM((2 * partners + 1, 16, LANES), wide),
+            pltpu.SemaphoreType.DMA((partners,)),
+            pltpu.SemaphoreType.DMA((partners,)),
         ]
         + summing_scratch(groups, members, chunks, part, half_width),
         compiler_params=pltpu.CompilerParams(
@@ -1465,152 +1962,201 @@
         all_turned,
         parts,
     )
-    offsets = jnp.arange(band, dtype=jnp.int32) - (size - 1) - LANES - place[3]
-    buckets = jnp.arange(BUCKETS, dtype=jnp.int32)
-    onehot = (bucket_of(offsets)[:, None] == buckets[None, :]).astype(wide)
-    near_grad = jnp.dot(
-        band_sums[:, :2].reshape(HEADS, band), onehot, precision=highest, preferred_element_type=wide
-    )
-    far_grad = jnp.sum(far_sums[:, :2, :16].reshape(pairs, 2, 2, 8), axis=3)
-    far_grad = jnp.transpose(far_grad, (0, 2, 1)).reshape(HEADS, 2)
-    grad_table = near_grad + far_grad[:, :1] * (buckets == 15) + far_grad[:, 1:] * (buckets == 31)
-    return grad_q, grad_k, grad_v, grad_table.T, feed_sums, pair_sums
-
-
-def finish_kernel(
-    base,
+
+
+def last_kernel(
     groups,
-    members,
+    seqs,
+    halves,
+    grad_q_ref,
+    grad_k_ref,
+    grad_v_ref,
+    first_ref,
+    tokens_ref,
+    grad_hidden_ref,
+    gains_ref,
     rows_ref,
-    third_ref,
+    sums_ref,
     starts_ref,
-    gains_ref,
-    sums_ref,
     backs_ref,
-    weights,
-    parts,
-    weight_sem,
-    send_sem,
-    recv_sem,
+    query_ref,
+    key_ref,
+    value_ref,
+    inner_ref,
+    cross_key_ref,
+    cross_value_ref,
+    query_sums_ref,
+    key_sums_ref,
+    value_sums_ref,
+    inner_sums_ref,
+    grad_tokens_ref,
+    vectors_ref,
+    grad_self_value_ref,
+    grad_self_out_ref,
+    grad_cross_query_ref,
+    grad_cross_key_ref,
+    grad_cross_value_ref,
+    grad_cross_out_ref,
+    grad_second_inner_ref,
+    grad_second_outer_ref,
+    grad_pooler_ref,
+    pieces,
 ):
-    count, _, width = third_ref.shape
-    unit = width // count
+    rows, width = tokens_ref.shape
+    part = query_ref.shape[0]
+    feeds = inner_ref.shape[1] // width
+    number = groups * seqs
+    every = 2 * HEAD_ROWS
     group = lax.axis_index("batch")
-    member = lax.axis_index("seq")
-    partners = []
-    for axis, place, number in (("batch", group, groups), ("seq", member, members)):
-        span = 1
-        while span < number:
-            bit = lax.rem(place // span, 2)
-            partners.append({axis: place + span * (1 - 2 * bit)})
-            span *= 2
-    barrier = pltpu.get_barrier_semaphore()
-    for partner in partners:
-        pl.semaphore_signal(barrier, inc=1, device_id=partner, device_id_type=MESH)
-    copies = [
-        pltpu.make_async_copy(
-            third_ref.at[:, base + unit * i : base + unit * (i + 1), :], weights.at[i], weight_sem.at[i]
-        )
-        for i in range(4)
-    ]
-    for copy in copies:
-        copy.start()
-    parts[0] = rows_ref[...]
-    pl.semaphore_wait(barrier, len(partners))
-    for i, partner in enumerate(partners):
-        copy = pltpu.make_async_remote_copy(
-            src_ref=parts.at[2 * i],
-            dst_ref=parts.at[2 * i + 1],
-            send_sem=send_sem.at[i],
-            recv_sem=recv_sem.at[i],
-            device_id=partner,
-            device_id_type=MESH,
-        )
-        copy.start()
-        copy.wait()
-        parts[2 * i + 2] = parts[2 * i] + parts[2 * i + 1]
-    sums = parts[2 * len(partners)]
-    sums_ref[...] = sums
-    for copy in copies:
-        copy.wait()
-
-    def weight(i):
-        return weights[i].reshape(width, width)
-
+    grad_normed = (
+        back_product(grad_q_ref[...], first_ref[0])
+        + back_product(grad_k_ref[...], first_ref[1])
+        + back_product(grad_v_ref[...], first_ref[2])
+    )
+    grad_tokens, _ = rms_back(tokens_ref[...].astype(wide), gains_ref[:1, :], grad_normed)
+    grad_tokens_ref[...] = grad_tokens + grad_hidden_ref[...]
+
+    def chooser(count, first):
+        row = lax.broadcasted_iota(jnp.int32, (count, width), 0)
+        column = lax.broadcasted_iota(jnp.int32, (count, width), 1)
+        return column == first + row
+
+    chosen = chooser(part, group * part)
+    choose = chosen.astype(wide).astype(low)
+    tiles = width // LANES
+    for i in range(tiles):
+        pieces[i] = (
+            rows_ref[:, :, LANES * i : LANES * (i + 1)].reshape(number * every, LANES).astype(wide)
+        )
+
+    def piece(at):
+        return jnp.concatenate(
+            [pieces[i, pl.ds(at, number, stride=every), :] for i in range(tiles)], axis=1
+        ).astype(low)
+
+    def own(values, which=None):
+        which = choose if which is None else which
+        return lax.dot_general(
+            which, values, (((1,), (1,)), ((), ())), preferred_element_type=wide
+        ).astype(low)
+
+    def pair(left, right):
+        return product(left, right)
+
+    grad_cross_out_ref[...] = pair(own(piece(0)), piece(7))
+    second_in = own(piece(1))
+    grad_second_inner = [pair(second_in, piece(8 + j)) for j in range(feeds)]
+    share = grad_second_outer_ref.shape[0]
+    half = share // halves
+    per = width // half
+    grad_out = piece(12)
+    for i in range(halves):
+        chunk = group // per
+        at = lax.rem(group, per) * half
+        which = chooser(half, at).astype(wide).astype(low)
+        found = jnp.zeros((half, number), wide)
+        for j in range(feeds // halves):
+            here = own(piece(2 + feeds // halves * i + j), which).astype(wide)
+            found = jnp.where(chunk == j, here, found)
+        grad_second_outer_ref[half * i : half * (i + 1), :] = pair(found.astype(low), grad_out)
+    for j in range(feeds):
+        grad_second_inner_ref[:, width * j : width * (j + 1)] = grad_second_inner[j]
+    grad_pooler_ref[...] = pair(own(piece(6)), piece(13))
+
+    mixed = rows_ref[:, HEAD_ROWS:, :].reshape(number * HEAD_ROWS, width)
+    repeat = (
+        lax.broadcasted_iota(jnp.int32, (number * HEAD_ROWS, number), 0) // HEAD_ROWS
+        == lax.broadcasted_iota(jnp.int32, (number * HEAD_ROWS, number), 1)
+    )
+    heads = product(repeat.astype(wide).astype(low), piece(14))
+    head = lax.broadcasted_iota(jnp.int32, heads.shape, 0) % HEAD_ROWS
+    head_column = lax.broadcasted_iota(jnp.int32, heads.shape, 1) // HEAD
+    heads = jnp.where(head == head_column, heads, 0.0).astype(low)
+    grad_cross_value = pair(own(mixed), heads)
+    grad_cross_value_ref[...] = grad_cross_value
+
+    def exact(left, right):
+        return lax.dot_general(
+            left,
+            right,
+            (((1,), (1,)), ((), ())),
+            precision=highest,
+            preferred_element_type=wide,
+        )
+
+    chosen = chosen.astype(wide)
+    key_rows = exact(chosen, sums_ref[:HEAD_ROWS, :])
     head_row = lax.broadcasted_iota(jnp.int32, (HEAD_ROWS, width), 0)
     head_mask = head_row == lax.broadcasted_iota(jnp.int32, (HEAD_ROWS, width), 1) // HEAD
-    spread = product(sums[:HEAD_ROWS].astype(low), weight(3))
-    grad_cross_query = jnp.sum(jnp.where(head_mask, spread, 0.0), axis=0, keepdims=True)
-    grad_cross_query = grad_cross_query.astype(low)
-
-    def widened(row):
-        return jnp.broadcast_to(row.astype(wide), (SEQ_ROWS, width))
-
-    start = widened(starts_ref[0:1, :])
-    after_self = widened(starts_ref[3:4, :])
-    grad_rows = back_product(widened(grad_cross_query).astype(low), weight(2))
-    grad_after_self, _ = rms_back(after_self, gains_ref[5:6, :], grad_rows)
-    cross_gain = grad_rows * after_self * rms_factor(after_self)
-    grad_after_self = grad_after_self + widened(sums[HEAD_ROWS : HEAD_ROWS + 1])
-    grad_branch = grad_after_self.astype(low)
-    grad_self_vals = back_product(grad_branch, weight(1)).astype(low)
-    grad_rows = back_product(grad_self_vals, weight(0))
-    grad_start, _ = rms_back(start, gains_ref[4:5, :], grad_rows)
-    self_gain = grad_rows * start * rms_factor(start)
+    query_row = starts_ref[5:6, :].astype(low).astype(wide)
+    query_heads = jnp.where(head_mask, jnp.broadcast_to(query_row, (HEAD_ROWS, width)), 0.0)
+    grad_cross_key = jnp.dot(
+        key_rows, query_heads, precision=highest, preferred_element_type=wide
+    )
+    grad_cross_key_ref[...] = grad_cross_key
+    starts = exact(chosen, starts_ref[...])
+    grad_self_value_ref[...] = starts[:, 1:2] * backs_ref[5:6, :]
+    grad_self_out_ref[...] = starts[:, 2:3] * backs_ref[4:5, :]
+    grad_cross_query_ref[...] = starts[:, 4:5] * backs_ref[3:4, :]
+
+    def gain_sum(weight, grads):
+        ones = jnp.ones((8, grads.shape[1]), wide)
+        return exact(ones, weight.astype(wide) * grads)[:1]
+
+    attention = (
+        gain_sum(query_ref[...], query_sums_ref[...])
+        + gain_sum(key_ref[...], key_sums_ref[...])
+        + gain_sum(value_ref[...], value_sums_ref[...])
+    )
+    feed = gain_sum(inner_ref[...], inner_sums_ref[...])
+    encoder = gain_sum(cross_key_ref[...], grad_cross_key) + gain_sum(
+        cross_value_ref[...], grad_cross_value
+    )
+    gains = exact(gains_ref[:8, :], chosen)
+    backs = exact(backs_ref[...], chosen)
+    others = exact(sums_ref[HEAD_ROWS:, :], chosen)
     for i, row in enumerate(
         (
-            grad_start + grad_after_self,
-            self_gain,
-            cross_gain,
-            grad_cross_query,
-            grad_branch,
-            grad_self_vals,
+            attention / gains[0:1],
+            feed / gains[1:2],
+            encoder / gains[2:3],
+            backs[0:1],
+            backs[1:2],
+            backs[2:3],
+            others[2:3],
+            others[1:2],
         )
     ):
-        backs_ref[i : i + 1, :] = row[:1].astype(wide)
-    backs_ref[6:, :] = jnp.zeros((2, width), wide)
-
-
-def finish(rows, third, base, starts, gains, groups, members):
-    many, width = rows.shape
-    partners = (groups.bit_length() - 1) + (members.bit_length() - 1)
-    count = third.shape[0]
+        vectors_ref[i] = row
+
+
+def last_step(groups, seqs, halves, tokens, part, share, feeds, *arrays):
+    rows, width = tokens.shape
     whole = pl.BlockSpec(memory_space=pltpu.VMEM)
+    square = jax.ShapeDtypeStruct((part, width), wide)
     return pl.pallas_call(
-        functools.partial(finish_kernel, base, groups, members),
-        name="finish",
-        in_specs=[whole, pl.BlockSpec(memory_space=pl.ANY), whole, whole],
-        out_specs=[whole, whole],
+        functools.partial(last_kernel, groups, seqs, halves),
+        name="last",
+        in_specs=[whole] * len(arrays),
+        out_specs=[whole] * 11,
         out_shape=[
-            jax.ShapeDtypeStruct((many, width), wide),
-            jax.ShapeDtypeStruct((8, width), wide),
+            jax.ShapeDtypeStruct((rows, width), wide),
+            jax.ShapeDtypeStruct((8, 1, part), wide),
+            square,
+            square,
+            square,
+            square,
+            square,
+            square,
+            jax.ShapeDtypeStruct((part, feeds * width), wide),
+            jax.ShapeDtypeStruct((share, width), wide),
+            square,
         ],
         scratch_shapes=[
-            pltpu.VMEM((4, count, width // count, width), low),
-            pltpu.VMEM((2 * partners + 1, many, width), wide),
-            pltpu.SemaphoreType.DMA((4,)),
-            pltpu.SemaphoreType.DMA((partners,)),
-            pltpu.SemaphoreType.DMA((partners,)),
+            pltpu.VMEM((width // LANES, groups * seqs * 2 * HEAD_ROWS, LANES), wide)
         ],
-        compiler_params=pltpu.CompilerParams(
-            collective_id=2, has_side_effects=True, vmem_limit_bytes=32 * 2**20
-        ),
-        cost_estimate=pl.CostEstimate(
-            flops=2**30, bytes_accessed=8 * width * width, transcendentals=0
-        ),
-    )(rows, third, starts, gains)
-
-
-def seq_scatter(value, rows):
-    count = lax.axis_size("seq")
-    me = lax.axis_index("seq")
-    total = lax.dynamic_slice_in_dim(value, me * rows, rows)
-    for step in range(1, count):
-        other = lax.dynamic_slice_in_dim(value, (me + step) % count * rows, rows)
-        total = total + lax.ppermute(
-            other.astype(low), "seq", [(i, (i + step) % count) for i in range(count)]
-        ).astype(wide)
-    return total
+        compiler_params=pltpu.CompilerParams(vmem_limit_bytes=50 * 2**20),
+    )(*arrays)
 
 
 def in_blocks(gathered, sizes):
@@ -1700,7 +2246,6 @@
     queries, all_keys, all_values, normed_all, gains, first_full = project(
         tokens, extra, [query_weight, key_weight, value_weight], groups, members
     )
-    normed = lax.dynamic_slice_in_dim(normed_all, own_first, rows)
     table = gains[8, : BUCKETS * HEADS].reshape(BUCKETS, HEADS).astype(low)
     second_part = jnp.concatenate(
         [
@@ -1732,103 +2277,55 @@
         axis=0,
     )
     rest = lax.all_gather(rest_part, "batch", axis=0, tiled=False)
-    second = rest
-
-    def square(gathered, at):
-        return gathered[:, at : at + part].reshape(groups * part, width)
-
-    def tall(gathered, at):
-        return gathered[:, at : at + share].reshape(groups * share, width)
-
-    (
-        attention_gain_full,
-        feed_gain_full,
-        encoder_gain_full,
-        start_full,
-        self_gain_full,
-        cross_gain_full,
-        second_gain_full,
-        final_gain_full,
-    ) = [gains[i] for i in range(8)]
-    inputs = tokens.astype(wide)
+
     near = offset_biases(table, block_rows(rows), pack, place[3])
     attended, totals = attend(queries, all_keys, all_values, near, place)
-    attended_low = attended.astype(low)
-    out_full = square(second, 0)
-    hidden = inputs + product(attended_low, out_full)
-
-    inner_in = rms_norm(hidden, feed_gain_full).astype(low)
-    inner_full = [square(second, part * (1 + j)) for j in range(blocks)]
-    outer_full = tall(second, part * (1 + blocks)).reshape(blocks, -1, width)
-    inner_pre = [product(inner_in, inner_full[j]) for j in range(blocks)]
-    inner_act = [jax.nn.gelu(inner_pre[j]).astype(low) for j in range(blocks)]
-    encoded = hidden
-    for j in range(blocks):
-        encoded = encoded + product(inner_act[j], outer_full[j])
-    context = rms_norm(encoded, encoder_gain_full).astype(low)
-
-    third_blocks = in_blocks(
+    rest_blocks = in_blocks(
         rest,
         [part] * (1 + blocks) + [share] + [part] * (7 + blocks // halves) + [half_share],
     )
-    base = (1 + 2 * blocks) * (width // third_blocks.shape[0])
-    (
-        embedded,
-        loss,
-        grad_context,
-        pieces,
-        mixed,
-        starts,
-        decoder_totals,
-    ) = decoder_step(
-        context, third_blocks, base, gains, labels, place, groups, members, seqs
+    base = (1 + 2 * blocks) * (width // rest_blocks.shape[0])
+    hidden, inner_pre, encoded, context = feed_forward(
+        attended, tokens, rest_blocks, gains, blocks
+    )
+
+    embedded, loss, grad_context, decoder_rows, starts, decoder_totals = decoder_step(
+        context, rest_blocks, base, gains, labels, place, groups, members, seqs
     )
     contrastive_loss = loss[0, :1]
     embedded = embedded[:seqs]
-    decoder_rows = jnp.concatenate(
-        [
-            pieces[:, :seqs].astype(low).reshape(-1, width),
-            mixed.reshape(seqs, HEAD_ROWS, width)[:, :HEADS].reshape(-1, width),
-        ],
-        axis=0,
-    )
-    start_row, self_in, self_vals, after_self, cross_in, cross_query_row = [
-        starts[i : i + 1] for i in range(6)
-    ]
-    head_of = jnp.arange(width, dtype=jnp.int32) // HEAD
-    head_mask = head_of[None, :] == jnp.arange(HEADS, dtype=jnp.int32)[:, None]
-
-    count = decoder_rows.shape[0]
-    decoder_rows = jnp.pad(decoder_rows, ((0, -count % 16), (0, 0)))
-    decoder_rows = lax.all_gather(decoder_rows, "batch", axis=0, tiled=False)
-
-    grad_encoded, _ = norm_back(encoded, encoder_gain_full, grad_context)
-    grad_feed_branch = grad_encoded.astype(low)
-    grad_inner_pre = [
-        gelu_back(inner_pre[j], back_product(grad_feed_branch, outer_full[j])).astype(low)
-        for j in range(blocks)
-    ]
-    grad_inner_in = sum(back_product(grad_inner_pre[j], inner_full[j]) for j in range(blocks))
-    grad_hidden, _ = norm_back(hidden, feed_gain_full, grad_inner_in)
-    grad_hidden = grad_hidden + grad_encoded
-    grad_attn_branch = grad_hidden.astype(low)
-    second_grads = jnp.concatenate(
-        [weight_grad(attended_low, grad_attn_branch).astype(low).reshape(groups, 1, part, width)]
-        + [
-            weight_grad(inner_in, grad_inner_pre[j]).astype(low).reshape(groups, 1, part, width)
-            for j in range(blocks)
-        ]
-        + [
-            jnp.concatenate(
-                [weight_grad(inner_act[j], grad_feed_branch).astype(low) for j in range(blocks)],
-                axis=0,
-            ).reshape(groups, blocks, part, width)
-        ],
-        axis=1,
-    ).reshape(groups // 4, 2, 2, 1 + 2 * blocks, part, width)
-
-    grad_attended = back_product(grad_attn_branch, out_full).astype(low)
-    grad_query_low, grad_key_low, grad_value_low, grad_table, second_sums, first_sums = attend_back(
+    decoder_rows = lax.all_gather(
+        decoder_rows.reshape(seqs * 2 * HEAD_ROWS, width), "batch", axis=0, tiled=False
+    )
+
+    second_grads, grad_hidden, grad_attended, sums, backs = feed_back(
+        grad_context,
+        encoded,
+        hidden,
+        inner_pre,
+        attended,
+        rest_blocks,
+        base,
+        gains,
+        decoder_totals,
+        starts,
+        groups,
+        members,
+        part,
+    )
+    normed = lax.dynamic_slice_in_dim(normed_all, own_first, rows)
+    (
+        grad_query_rows,
+        grad_key_rows,
+        grad_value_rows,
+        table_sums,
+        out_sums,
+        inner_sums,
+        outer_sums,
+        query_sums,
+        key_sums,
+        value_sums,
+    ) = attend_back(
         queries,
         all_keys,
         all_values,
@@ -1841,121 +2338,83 @@
         normed_all.T,
         second_grads,
     )
-    grad_normed_all = back_product(grad_key_low, first_full[1]) + back_product(
-        grad_value_low, first_full[2]
-    )
-    grad_normed_own = back_product(grad_query_low, first_full[0])
-    grad_normed = seq_scatter(grad_normed_all, rows) + grad_normed_own
-    grad_inputs, _ = norm_back(inputs, attention_gain_full, grad_normed)
-    grad_inputs = grad_inputs + grad_hidden
-
-    table_row = jnp.pad(grad_table.reshape(1, -1), ((0, 0), (0, width - grad_table.size)))
-    last_rows = jnp.concatenate(
-        [
-            decoder_totals[: HEAD_ROWS + 3],
-            table_row,
-        ],
-        axis=0,
-    )
-    last_rows = jnp.pad(last_rows, ((0, -last_rows.shape[0] % 8), (0, 0)))
-    sums, backs = finish(last_rows, third_blocks, base, starts, gains, groups, members)
     (
-        grad_start,
-        grad_self_gain,
-        grad_cross_gain,
-        grad_cross_query_row,
-        grad_self_branch,
-        grad_self_vals,
-    ) = [backs[i] for i in range(6)]
-
-    def mine(values, size=part):
-        return lax.dynamic_slice_in_dim(values, group * size, size, values.ndim - 1)
-
-    def outer(left_side, right_side):
-        return mine(left_side).astype(wide).T * right_side.astype(wide)
-
-    def every_row(at, size=seqs):
-        return decoder_rows[:, at : at + size].reshape(groups * size, width)
-
-    at = 0
-    cross_rows = every_row(0)
-    second_in_rows = every_row(seqs)
-    act_rows = decoder_rows[:, 2 * seqs : (2 + blocks) * seqs].reshape(
-        groups, blocks, seqs, width
-    )
-    act_rows = jnp.transpose(act_rows, (0, 2, 1, 3)).reshape(
-        groups * seqs, halves, groups, half_share
-    )
-    act_rows = lax.dynamic_slice_in_dim(act_rows, group, 1, 2).reshape(groups * seqs, share)
-    at = (2 + blocks) * seqs
-    pooled_rows = every_row(at)
-    branch_rows = every_row(at + seqs)
-    pre_rows = decoder_rows[:, at + 2 * seqs : at + (2 + blocks) * seqs].reshape(
-        groups, blocks, seqs, width
-    )
-    pre_rows = jnp.transpose(pre_rows, (0, 2, 1, 3)).reshape(
-        groups * seqs, halves, groups, half_share
-    )
-    pre_rows = jnp.transpose(pre_rows, (0, 2, 1, 3)).reshape(groups * seqs, blocks * width)
-    at = at + (2 + blocks) * seqs
-    out_rows = every_row(at)
-    grad_pooled_rows = every_row(at + seqs)
-    att_rows = every_row(at + 2 * seqs)
-    context_rows = every_row(at + 3 * seqs, seqs * HEADS)
-    att_heads = jnp.where(
-        head_mask[None], att_rows[:, None, :], jnp.zeros((), low)
-    ).reshape(-1, width)
-
-    inner_sums = jnp.transpose(second_sums[1 : 1 + blocks], (1, 0, 2)).reshape(
-        part, blocks * width
-    )
-    query_sums, key_sums, value_sums = [
-        jnp.transpose(first_sums[:, :, LANES * i : LANES * (i + 1)], (1, 0, 2)).reshape(part, width)
-        for i in range(3)
-    ]
-    key_totals = mine(sums[:HEADS])
-    other_sums = sums[HEAD_ROWS:]
-    def gain_grad(gain, *pairs):
-        total = sum(jnp.sum(weight.astype(wide) * grads, axis=1) for weight, grads in pairs)
-        return total / gain.astype(wide)
-
-    cross_key_sums = jnp.repeat(key_totals.T, HEAD, axis=1) * cross_query_row.astype(low).astype(
-        wide
-    )
-    cross_value_sums = weight_grad(mine(context_rows), att_heads)
+        grad_tokens,
+        vectors,
+        grad_self_value,
+        grad_self_out,
+        grad_cross_query,
+        grad_cross_key,
+        grad_cross_value,
+        grad_cross_out,
+        grad_second_inner,
+        grad_second_outer,
+        grad_pooler,
+    ) = last_step(
+        groups,
+        seqs,
+        halves,
+        tokens,
+        part,
+        share,
+        blocks,
+        grad_query_rows,
+        grad_key_rows,
+        grad_value_rows,
+        first_full,
+        tokens,
+        grad_hidden,
+        gains,
+        decoder_rows.reshape(groups * seqs, 2 * HEAD_ROWS, width),
+        sums,
+        starts,
+        backs,
+        query_weight,
+        key_weight,
+        value_weight,
+        feed_inner,
+        cross_key,
+        cross_value,
+        query_sums,
+        key_sums,
+        value_sums,
+        inner_sums,
+    )
+    half_share = share // halves
+    grad_second_inner = jnp.transpose(
+        grad_second_inner.reshape(part, halves, groups, half_share), (0, 2, 1, 3)
+    ).reshape(part, blocks * width)
+    vectors = vectors.reshape(8, part)
+    own_buckets = BUCKETS // groups
+    grad_table = lax.dynamic_slice_in_dim(table_sums, group * own_buckets, own_buckets, 1)[:HEADS].T
     return (
         contrastive_loss,
         embedded,
-        grad_inputs,
-        gain_grad(
-            attention_gain,
-            (query_weight, query_sums),
-            (key_weight, key_sums),
-            (value_weight, value_sums),
-        ),
+        grad_tokens,
+        vectors[0],
         query_sums,
         key_sums,
         value_sums,
-        second_sums[0],
-        mine(other_sums[3, : BUCKETS * HEADS], BUCKETS * HEADS // groups).reshape(-1, HEADS),
-        gain_grad(feed_gain, (feed_inner, inner_sums)),
+        out_sums,
+        grad_table,
+        vectors[1],
         inner_sums,
-        second_sums[1 + blocks :].reshape(share, width),
-        gain_grad(encoder_gain, (cross_key, cross_key_sums), (cross_value, cross_value_sums)),
-        mine(grad_start),
-        mine(grad_self_gain),
-        outer(self_in, grad_self_vals[None]),
-        outer(self_vals, grad_self_branch[None]),
-        mine(grad_cross_gain),
-        outer(cross_in, grad_cross_query_row[None]),
-        cross_key_sums,
-        cross_value_sums,
-        weight_grad(mine(cross_rows), branch_rows),
-        mine(other_sums[2]),
-        weight_grad(mine(second_in_rows), pre_rows),
-        weight_grad(act_rows, out_rows),
-        mine(other_sums[1]),
-        weight_grad(mine(pooled_rows), grad_pooled_rows),
+        outer_sums,
+        vectors[2],
+        vectors[3],
+        vectors[4],
+        grad_self_value,
+        grad_self_out,
+        vectors[5],
+        grad_cross_query,
+        grad_cross_key,
+        grad_cross_value,
+        grad_cross_out,
+        vectors[6],
+        grad_second_inner,
+        grad_second_outer,
+        vectors[7],
+        grad_pooler,
     )
 
 

time: 506 us -> 434 us (0.86); the launches traced: 497 us -> 431 us
  matrix products: 65.5 us -> 0.17 us
  Pallas kernels: 306 us -> 363 us
  local copies, waits for them, and re-layouts: 63.6 us -> 35 us
  other arithmetic: 19.1 us -> 2.65 us
  waiting for transfers between devices: 24.3 us -> 14.6 us
    pallas_call x1 -> x3, Pallas kernels: 20.1 us -> 75.8 us  [the longest x1 45.7 us: feed_back(): pl.pallas_call(functools.partial(feed_back_kernel, base, groups, members)...]
    dot_general x22 -> x0, matrix products: 36.5 us -> none  [the longest x12 24.3 us: back_product(): lax.dot_general(left_side, right_side, (((1,), (1,)), ((), ())), preferre...]
    dot_general x15 -> x1, matrix products: 29 us -> 0.17 us  [weight_grad(): lax.dot_general(left_side, right_side, (((0,), (0,)), ((), ())), preferre...]
    slice x14 -> x0, local copies, waits for them, and re-layouts: 16.4 us -> none  [the longest x1 4.76 us: square(): return gathered[:, at:at + part].reshape(groups * part, width)]
    ppermute x1 -> x0, waiting for transfers between devices: 11.2 us -> none  [seq_scatter(): lax.ppermute(other.astype(low), 'seq', [(i, (i + step) % count) for i in...]
    reduce_sum x7 -> x0, other arithmetic: 5.52 us -> none  [the longest x5 3.3 us: gain_grad(): jnp.sum(weight.astype(wide) * grads, axis=1)]
    unnamed x205 -> x110, local copies, waits for them, and re-layouts: 19.5 us -> 16.9 us
  transfers between devices with their start and end apart: 3 -> 2, of which waited for: 2 -> 1; matrix products, arithmetic and copies ran while one was open for 9% -> 3% of each run, Pallas kernels for 55% -> 70%
where the time goes in v3:
time: 434 us; the launch traced here: 431 us
  Pallas kernels  363 us (84%)
  local copies, waits for them, and re-layouts  35 us (8%)
  between operations  15 us (3%)
  waiting for transfers between devices  14.6 us (3%)
    pallas_call x1, Pallas kernels, attend_back(): pl.pallas_call(functools.partial(attend_back_kernel, groups, members), na...  138 us
    pallas_call x1, Pallas kernels, project(): pl.pallas_call(functools.partial(first_kernel, groups, members), name='pr...  75.3 us
    pallas_call x1, Pallas kernels, feed_back(): pl.pallas_call(functools.partial(feed_back_kernel, base, groups, members)...  45.7 us
    pallas_call x1, Pallas kernels, attend(): pl.pallas_call(attend_kernel, name='attend', grid=(pairs, rows // size),...  40.6 us
    pallas_call x1, Pallas kernels, decoder_step(): pl.pallas_call(functools.partial(decoder_kernel, base, groups, members, s...  33.6 us
    unnamed x110, local copies, waits for them, and re-layouts  16.9 us
    pallas_call x1, Pallas kernels, feed_forward(): pl.pallas_call(feed_kernel, name='feed_forward', in_specs=[whole, whole,...  16.8 us
    all_gather x1, waiting for transfers between devices, shards(): rest = lax.all_gather(rest_part, 'batch', axis=0, tiled=False)  14.6 us
  transfers between devices with their start and end apart: 2, of which 1 were waited for; matrix products, arithmetic and copies ran while one was open for 3% of the time, Pallas kernels for 70%

profile of v3, /device:TPU:0, one launch (start us, length us, event | category | flops | bytes accessed | tf_op | source)
XLA Modules:
  0.0 430.7 jit_solution(10386184018036251078)
XLA Ops:
  7.3 1.0 copy.78
  8.3 1.1 pad_maximum_fusion
  10.8 1.0 constant_dynamic-update-slice_fusion.1
  11.8 0.9 dynamic-slice_dynamic-update-slice_fusion
  12.7 1.1 copy-done.28
  14.8 75.3 %project.1 = (bf16[768,768]{1,0:T(8,128)(2,1)S(1)}, bf16[1536,768]{1,0:T(8,128)(2,1)S(1)}, bf16[1536,768]{1,0:T(8,128)(2,1)}, bf16[1536,768]{1,0:T(8,128)(2,1)},...) custom-call(bf16[768,768]{1,0:T(8,128)(2,1)S(1)} %copy-done.2, bf16[16,768]{1,0:T(8,128)(2,1)S(1)} %dynamic_update_slice.7.extra_ref, ...), custom_call_target="tpu_custom_call" | custom-call | flops 2147483648 | bytes 37748736 | tf_op jit(solution)/shard_map/project/pallas_call | solution.py:365
  90.2 1.4 copy-done.25
  92.0 4.4 %copy.72 = bf16[1536,768]{0,1:T(8,128)(2,1)} copy(bf16[1536,768]{1,0:T(8,128)(2,1)} %get-tuple-element.87) | data formatting | bytes 4718592 | tf_op jit(solution)/shard_map/project/pallas_call | solution.py:365
  97.6 1.4 pad_add_fusion.place
  98.9 2.4 dynamic-slice_bitcast_fusion.own_turned_ref
  101.4 40.6 %attend.1 = (f32[768,768]{1,0:T(8,128)S(1)}, f32[768,128]{1,0:T(8,128)S(1)}) custom-call(s32[4]{0:T(128)S(1)} %pad_add_fusion.place, bf16[768,768]{1,0:T(8,128)(2,1)S(1)} %get-tuple-element.71.q_ref, bf16[1536,768]{1,0:T(8,128)(2,1)} %copy-done.25, bf16[1536,768]{1,0:T(8,128)(2,1)} %get-tuple-element.73.v_ref, f32[12,1,768]{2,1,0:T(1,128)S(1)} %broadcast_in_dim.22.near_ref), custom_call_target="tpu_custom_call" | custom-call | flops 14495514624 | bytes 18874368 | tf_op jit(solution)/shard_map/attend/pallas_call | solution.py:454
  142.0 1.4 copy-done.24
  143.4 0.7 copy-done.27
  144.1 14.6 %all-gather.6.cloned.1.call-done = bf16[15360,768]{1,0:T(8,128)(2,1)} async-done(((bf16[960,768]{1,0:T(8,128)(2,1)}), bf16[15360,768]{1,0:T(8,128)(2,1)}) %all-gather.6.cloned.1.call-update) | async-done | bytes 23592976 | tf_op jit(solution)/shard_map/all_gather | solution.py:2279
  158.7 16.8 %feed_forward.1 = (f32[768,768]{1,0:T(8,128)}, bf16[4,768,768]{2,1,0:T(8,128)(2,1)}, f32[768,768]{1,0:T(8,128)}, bf16[768,768]{1,0:T(8,128)(2,1)S(1)}) custom-call(f32[768,768]{1,0:T(8,128)} %copy-done.24, bf16[768,768]{1,0:T(8,128)(2,1)S(1)} %copy-done.2, bf16[16,960,768]{2,1,0:T(8,128)(2,1)} %bitcast.55, f32[16,768]{1,0:T(8,128)S(1)} %get-tuple-element.74.gains_ref), custom_call_target="tpu_custom_call" | custom-call | flops 8153726976 | bytes 23592960 | tf_op jit(solution)/shard_map/feed_forward/pallas_call | solution.py:1018
  175.5 1.0 copy-done.4
  176.5 33.6 %decoder.1 = (f32[8,768]{1,0:T(8,128)}, f32[8,128]{1,0:T(8,128)}, f32[768,768]{1,0:T(8,128)}, bf16[3,32,768]{2,1,0:T(8,128)(2,1)}, f32[8,768]{1,0:T(8,128)}, /*index=5*/f32[24,768]{1,0:T(8,128)}) custom-call(s32[4]{0:T(128)} %copy-done.23, bf16[768,768]{1,0:T(8,128)(2,1)} %copy-done.4, bf16[16,960,768]{2,1,0:T(8,128)(2,1)} %bitcast.56, ...), custom_call_target="tpu_custom_call" | custom-call | flops 353894400 | bytes 23592960 | tf_op jit(solution)/shard_map/decoder/pallas_call | solution.py:892
  210.1 1.2 slice.62
  211.3 1.3 slice.63
  212.7 45.7 %feed_back.1 = (bf16[4,2,2,9,48,768]{5,4,3,2,1,0:T(8,128)(2,1)}, f32[768,768]{1,0:T(8,128)}, bf16[768,768]{1,0:T(8,128)(2,1)}, f32[24,768]{1,0:T(8,128)}, f32[8,768]{1,0:T(8,128)}) custom-call(f32[768,768]{1,0:T(8,128)} %get-tuple-element.79.grad_context_ref, f32[768,768]{1,0:T(8,128)} %get-tuple-element.80.encoded_ref, ...), custom_call_target="tpu_custom_call" | custom-call | flops 16307453952 | bytes 47185920 | tf_op jit(solution)/shard_map/feed_back/pallas_call | solution.py:1251
  258.4 137.8 %attend_back.1 = (bf16[768,768]{1,0:T(8,128)(2,1)}, bf16[768,768]{1,0:T(8,128)(2,1)}, bf16[768,768]{1,0:T(8,128)(2,1)}, f32[16,128]{1,0:T(8,128)}, f32[48,768]{1...) custom-call(s32[4]{0:T(128)} %copy-done.23, ...), custom_call_target="tpu_custom_call" | custom-call | flops 36238786560 | bytes 18874368 | tf_op jit(solution)/shard_map/attend_back/pallas_call | solution.py:1888
  396.2 0.8 dynamic-slice_bitcast_fusion.1
  397.7 1.1 copy-done
  398.7 1.3 copy-done.3
  400.0 0.9 copy-done.6
  400.9 0.9 copy-done.8
  401.8 0.9 copy-done.10
  402.7 13.4 %last.1 = (f32[768,768]{1,0:T(8,128)}, f32[8,1,48]{2,1,0:T(1,128)S(1)}, f32[48,768]{1,0:T(8,128)}, f32[48,768]{1,0:T(8,128)}, f32[48,768]{1,0:T(8,128)}, /*index...) custom-call(bf16[768,768]{1,0:T(8,128)(2,1)S(1)} %copy-done.3, ...), custom_call_target="tpu_custom_call" | custom-call | tf_op jit(solution)/shard_map/last/pallas_call | solution.py:2137
  417.4 1.9 reshape.147
  419.3 0.7 copy.96
  422.0 0.8 copy.100
  422.8 0.8 copy.101
  (122 shorter events, 7.6 us)
Async XLA Ops:
  7.2 151.5 %all-gather.6.cloned.1.call-start = ((), (), s32[]{:S(2)}) async-start(), calls=%async_computation.1 | async-start | bytes 25067520 | tf_op jit(solution)/shard_map/all_gather | solution.py:2279
  10.5 3.4 copy-start.44
  10.5 3.6 copy-start.45
  10.5 3.7 copy-start.36
  10.6 3.6 copy-start.37
  10.6 3.6 copy-start.38
  10.6 3.6 copy-start.39
  10.6 3.6 copy-start.40
  10.6 3.6 copy-start.41
  10.6 3.6 copy-start.42
  10.6 3.6 copy-start.43
  10.6 4.2 copy-start.2
  10.6 4.2 copy-start.16
  10.7 4.2 copy-start.17
  10.7 4.2 copy-start.18
  13.9 383.8 %all-gather.4.cloned.1.call-start = ((), (), s32[]{:S(2)}) async-start(), calls=%async_computation | async-start | bytes 2506752 | tf_op jit(solution)/shard_map/all_gather | solution.py:2297
  91.6 9.8 %copy-start.26 = (bf16[768,768]{1,0:T(8,128)(2,1)}, bf16[768,768]{1,0:T(8,128)(2,1)S(1)}, u32[]{:S(2)}) copy-start(bf16[768,768]{1,0:T(8,128)(2,1)S(1)} %get-tuple-element.71.q_ref) | copy-start | bytes 3538948
  91.6 67.1 %copy-start.14 = (f32[16,768]{1,0:T(8,128)}, f32[16,768]{1,0:T(8,128)S(1)}, u32[]{:S(2)}) copy-start(f32[16,768]{1,0:T(8,128)S(1)} %get-tuple-element.74.gains_ref) | copy-start | bytes 147460
  91.9 9.4 %copy-start.20 = (f32[12,1,768]{2,1,0:T(1,128)}, f32[12,1,768]{2,1,0:T(1,128)S(1)}, u32[]{:S(2)}) copy-start(f32[12,1,768]{2,1,0:T(1,128)S(1)} %broadcast_in_dim.22.near_ref) | copy-start | bytes 110596
  92.0 4.4 %copy-start.46 = (s32[48]{0:T(128)S(1)}, s32[48]{0:T(128)}, u32[]{:S(2)}) copy-start(s32[48]{0:T(128)} %param.29) | copy-start | bytes 580
  98.9 43.1 %copy-start.23 = (s32[4]{0:T(128)}, s32[4]{0:T(128)S(1)}, u32[]{:S(2)}) copy-start(s32[4]{0:T(128)S(1)} %pad_add_fusion.place) | copy-start | bytes 52
  258.3 139.3 %copy-start.5 = (bf16[48,3072]{1,0:T(8,128)(2,1)S(1)}, bf16[48,3072]{1,0:T(8,128)(2,1)}, u32[]{:S(2)}) copy-start(bf16[48,3072]{1,0:T(8,128)(2,1)} %inner_ref.1) | copy-start | bytes 884740
  258.3 139.3 %copy-start.15 = (f32[16,768]{1,0:T(8,128)S(1)}, f32[16,768]{1,0:T(8,128)}, u32[]{:S(2)}) copy-start(f32[16,768]{1,0:T(8,128)} %copy-done.14) | copy-start | bytes 147460
  258.4 139.3 %copy-start.19 = (f32[24,768]{1,0:T(8,128)S(1)}, f32[24,768]{1,0:T(8,128)}, u32[]{:S(2)}) copy-start(f32[24,768]{1,0:T(8,128)} %get-tuple-element.95.sums_ref) | copy-start | bytes 221188
  258.4 139.3 %copy-start.21 = (f32[8,768]{1,0:T(8,128)S(1)}, f32[8,768]{1,0:T(8,128)}, u32[]{:S(2)}) copy-start(f32[8,768]{1,0:T(8,128)} %get-tuple-element.84.starts_ref) | copy-start | bytes 73732
  258.4 139.3 %copy-start.22 = (f32[8,768]{1,0:T(8,128)S(1)}, f32[8,768]{1,0:T(8,128)}, u32[]{:S(2)}) copy-start(f32[8,768]{1,0:T(8,128)} %get-tuple-element.96.backs_ref) | copy-start | bytes 73732
  417.0 2.4 copy-start.11
  417.0 3.0 copy-start.9
  417.0 3.7 copy-start.7
  417.4 3.9 copy-start.31
  417.4 4.6 %copy-start.1 = (f32[48,3072]{1,0:T(8,128)S(1)}, f32[48,3072]{1,0:T(8,128)}, u32[]{:S(2)}) copy-start(f32[48,3072]{1,0:T(8,128)} %get-tuple-element.270.inner_sums_ref) | copy-start | bytes 1769476
  419.3 3.5 copy-start.29
  (17 other events, 19.2 us)
Sparse Core Ops, SparseCore 0:
  14.0 144.6 all-gather.5
  212.8 43.5 all-gather.3

commit v4 on v3

--- a/solution.py
+++ b/solution.py
@@ -391,50 +391,65 @@
     )(tokens, extra, *parts)
 
 
+FAR_LANE = 3
+
+
+def key_lanes(places, lane, ends, near, begins, reach):
+    blocks = len(begins)
+    values = jnp.where((segment_of(places, ends) == lane) & (lane < 3), 1.0, 0.0)
+    for half in range(2):
+        row = near[half]
+        for i, begin in enumerate(begins):
+            far = jnp.where(
+                places < begin - LANES,
+                row[:, :1],
+                jnp.where(places >= begin + reach, row[:, -1:], 0.0),
+            )
+            values = jnp.where(lane == FAR_LANE + half * blocks + i, far, values)
+    return values.astype(low)
+
+
 def attend_kernel(
-    place, q_ref, k_ref, v_ref, near_ref, attended_ref, total_ref, bias, key_side, value_side
+    place, q_ref, k_ref, v_ref, near_ref, attended_ref, total_ref, key_side, value_side, scores_ref
 ):
     pair = pl.program_id(0)
-    block = pl.program_id(1)
     pack = k_ref.shape[0]
-    size = q_ref.shape[0]
-    middle, reach, lead, width = table_sizes(size, pack)
+    rows = q_ref.shape[0]
+    size = block_rows(rows)
+    blocks = rows // size
+    _, reach, lead, _ = table_sizes(size, pack)
     ends = (place[0], place[1])
-    first = place[2] + block * size
     shift = place[3]
-
-    @pl.when(block == 0)
-    def _():
-        places = lax.broadcasted_iota(jnp.int32, (pack, LANES), 0)
-        lane = lax.broadcasted_iota(jnp.int32, (pack, LANES), 1)
-        key_side[:, :LANES] = k_ref[...]
-        key_side[:, LANES:] = (segment_of(places, ends) == lane).astype(wide).astype(low)
-        value_side[:, :LANES] = v_ref[...]
-        value_side[:, LANES:] = jnp.ones((pack, LANES), low)
-        for half in range(2):
-            row = near_ref[half]
-            before = middle - LANES
-            after = middle + reach
-            bias[half, :, before:after] = turned_biases(row, size, lead)
-            if before > 0:
-                bias[half, :, :before] = jnp.broadcast_to(row[:, :1], (size, before))
-            if after < width:
-                bias[half, :, after:] = jnp.broadcast_to(row[:, -1:], (size, width - after))
-
-    lane = lax.broadcasted_iota(jnp.int32, (size, LANES), 1)
-    rows = first + lax.broadcasted_iota(jnp.int32, (size, LANES), 0)
-    apart = jnp.where((segment_of(rows, ends) != lane) & (lane < 3), -far_apart, 0.0).astype(low)
-    own = pl.ds(pl.multiple_of(block * size, 64), size)
-    start = pl.multiple_of(middle - (first - shift), LANES)
+    begins = [place[2] - shift + size * i for i in range(blocks)]
+    near = [near_ref[half] for half in range(2)]
+    places = lax.broadcasted_iota(jnp.int32, (pack, LANES), 0)
+    lane = lax.broadcasted_iota(jnp.int32, (pack, LANES), 1)
+    key_side[:, :LANES] = k_ref[...]
+    key_side[:, LANES:] = key_lanes(places, lane, ends, near, begins, reach)
+    value_side[:, :LANES] = v_ref[...]
+    value_side[:, LANES:] = jnp.ones((pack, LANES), low)
+
+    lane = lax.broadcasted_iota(jnp.int32, (rows, LANES), 1)
+    row = lax.broadcasted_iota(jnp.int32, (rows, LANES), 0)
+    apart = jnp.where(
+        (segment_of(place[2] + row, ends) != lane) & (lane < 3), -far_apart, 0.0
+    )
     queries = q_ref[...]
     outputs = []
-    totals = total_ref[own, :]
+    totals = total_ref[...]
     for half in range(2):
         mine = (lane >= HEAD) if half else (lane < HEAD)
+        side = jnp.where(lane == FAR_LANE + half * blocks + row // size, 1.0, apart).astype(low)
         query_side = jnp.concatenate(
-            [jnp.where(mine, queries, jnp.zeros_like(queries)), apart], axis=1
-        )
-        scores = back_product(query_side, key_side[...]) + bias[half, :, pl.ds(start, pack)]
+            [jnp.where(mine, queries, jnp.zeros_like(queries)), side], axis=1
+        )
+        scores_ref[half, :, LANES : LANES + pack] = back_product(query_side, key_side[...])
+        band = turned_biases(near[half], size, lead)
+        for i in range(blocks):
+            span = slice(size * i, size * (i + 1))
+            columns = pl.ds(pl.multiple_of(begins[i], LANES), LANES + reach)
+            scores_ref[half, span, columns] += band
+        scores = scores_ref[half, :, LANES : LANES + pack]
         top = jnp.max(scores, axis=1, keepdims=True)
         weights = jnp.exp(scores - top).astype(low)
         output = product(weights, value_side[...])
@@ -442,40 +457,40 @@
         outputs.append(output[:, :LANES] / total)
         totals = jnp.where(lane == 2 * pair + half, top + jnp.log(total), totals)
     attended_ref[...] = jnp.where(lane < HEAD, outputs[0], outputs[1])
-    total_ref[own, :] = totals
+    total_ref[...] = totals
 
 
 def attend(queries, all_keys, all_values, near, place):
     rows, width = queries.shape
     pack = all_keys.shape[0]
     size = block_rows(rows)
-    _, _, _, columns = table_sizes(size, pack)
+    _, reach, _, _ = table_sizes(size, pack)
     pairs = width // LANES
     return pl.pallas_call(
         attend_kernel,
         name="attend",
-        grid=(pairs, rows // size),
+        grid=(pairs,),
         in_specs=[
             pl.BlockSpec(memory_space=pltpu.SMEM),
-            pl.BlockSpec((size, LANES), lambda p, i: (i, p)),
-            pl.BlockSpec((pack, LANES), lambda p, i: (0, p)),
-            pl.BlockSpec((pack, LANES), lambda p, i: (0, p)),
-            pl.BlockSpec((2, 1, near.shape[2]), lambda p, i: (p, 0, 0)),
+            pl.BlockSpec((rows, LANES), lambda p: (0, p)),
+            pl.BlockSpec((pack, LANES), lambda p: (0, p)),
+            pl.BlockSpec((pack, LANES), lambda p: (0, p)),
+            pl.BlockSpec((2, 1, near.shape[2]), lambda p: (p, 0, 0)),
         ],
         out_specs=[
-            pl.BlockSpec((size, LANES), lambda p, i: (i, p)),
-            pl.BlockSpec((rows, LANES), lambda p, i: (0, 0)),
+            pl.BlockSpec((rows, LANES), lambda p: (0, p)),
+            pl.BlockSpec((rows, LANES), lambda p: (0, 0)),
         ],
         out_shape=[
             jax.ShapeDtypeStruct((rows, width), wide),
             jax.ShapeDtypeStruct((rows, LANES), wide),
         ],
         scratch_shapes=[
-            pltpu.VMEM((2, size, columns), wide),
             pltpu.VMEM((pack, 2 * LANES), low),
             pltpu.VMEM((pack, 2 * LANES), low),
+            pltpu.VMEM((2, rows, LANES + pack + reach), wide),
         ],
-        compiler_params=pltpu.CompilerParams(vmem_limit_bytes=48 * 2**20),
+        compiler_params=pltpu.CompilerParams(vmem_limit_bytes=56 * 2**20),
         cost_estimate=pl.CostEstimate(
             flops=8 * rows * pack * width * 2, bytes_accessed=16 * pack * width, transcendentals=0
         ),
@@ -933,6 +948,201 @@
     )(place, context, third, gains, labels)
 
 
+class Summing:
+    def __init__(self, groups, members, buffers):
+        self.groups = groups
+        self.members = members
+        self.lines = groups // 4
+        self.group = lax.axis_index("batch")
+        self.member = lax.axis_index("seq")
+        self.z = self.group // 4
+        self.y = lax.rem(self.group // 2, 2)
+        self.core = lax.rem(self.group, 2)
+        (
+            self.chip,
+            self.pairs,
+            self.line,
+            self.shares,
+            self.chip_send,
+            self.chip_recv,
+            self.pair_send,
+            self.pair_recv,
+            self.line_send,
+            self.line_recv,
+            self.share_send,
+            self.share_recv,
+        ) = buffers
+        self.stages = 3 + self.lines
+
+    def batch_id(self, offset):
+        return {"batch": self.group + offset}
+
+    def neighbours(self):
+        found = [
+            (None, self.batch_id(1 - 2 * self.core)),
+            (None, self.batch_id(2 - 4 * self.y)),
+            (self.z > 0, self.batch_id(-4)),
+            (self.z < self.lines - 1, self.batch_id(4)),
+        ]
+        for step in range(1, self.members):
+            found.append((None, {"seq": lax.rem(self.member + step, self.members)}))
+        return found
+
+    def greet(self, barrier):
+        for condition, device in self.neighbours():
+            if condition is None:
+                pl.semaphore_signal(barrier, inc=1, device_id=device, device_id_type=MESH)
+            else:
+
+                @pl.when(condition)
+                def _():
+                    pl.semaphore_signal(barrier, inc=1, device_id=device, device_id_type=MESH)
+
+    def greeted(self, barrier):
+        ends = (self.z > 0).astype(jnp.int32) + (self.z < self.lines - 1).astype(jnp.int32)
+        pl.semaphore_wait(barrier, 2 + self.members - 1 + ends)
+
+    def copy(self, source, target, send, recv, device):
+        return pltpu.make_async_remote_copy(
+            src_ref=source,
+            dst_ref=target,
+            send_sem=send,
+            recv_sem=recv,
+            device_id=device,
+            device_id_type=MESH,
+        )
+
+    def chip_copy(self, chunk, source):
+        return self.copy(
+            source,
+            self.chip.at[chunk],
+            self.chip_send.at[chunk],
+            self.chip_recv.at[chunk],
+            self.batch_id(1 - 2 * self.core),
+        )
+
+    def pair_copy(self, chunk):
+        return self.copy(
+            self.chip.at[chunk, :, 1 - self.y],
+            self.pairs.at[chunk],
+            self.pair_send.at[chunk],
+            self.pair_recv.at[chunk],
+            self.batch_id(2 - 4 * self.y),
+        )
+
+    def line_copy(self, chunk, way, first, last, source):
+        return self.copy(
+            source.at[chunk, pl.ds(first, last - first)]
+            if source is self.pairs
+            else source.at[chunk, way, pl.ds(first, last - first)],
+            self.line.at[chunk, way, pl.ds(first, last - first)],
+            self.line_send.at[chunk, way],
+            self.line_recv.at[chunk, way],
+            self.batch_id(-4 if way else 4),
+        )
+
+    def share_copy(self, chunk, step):
+        return self.copy(
+            self.shares.at[chunk, self.member],
+            self.shares.at[chunk, self.member],
+            self.share_send.at[chunk, step - 1],
+            self.share_recv.at[chunk, step - 1],
+            {"seq": lax.rem(self.member + step, self.members)},
+        )
+
+    def start(self, chunk, source):
+        self.chip_copy(chunk, source).start()
+
+    def to_pair(self, chunk, source, own):
+        self.chip_copy(chunk, source).wait()
+        self.chip[chunk] = self.chip[chunk] + own
+        self.pair_copy(chunk).start()
+
+    def to_line(self, chunk, step):
+        lines = self.lines
+        if step == 0:
+            self.pair_copy(chunk).wait()
+            self.pairs[chunk] = self.pairs[chunk] + self.chip[chunk, :, self.y]
+        for way in range(2):
+            at = lines - 1 - step if way else step
+            first, last = (0, at) if way else (at + 1, lines)
+
+            @pl.when(self.z == at)
+            def _():
+                if step > 0:
+                    kept = (0, at + 1) if way else (at, lines)
+                    self.line_copy(chunk, way, kept[0], kept[1], self.line).wait_recv()
+                    span = pl.ds(first, last - first)
+                    self.line[chunk, way, span] = (
+                        self.line[chunk, way, span] + self.pairs[chunk, span]
+                    )
+                self.line_copy(
+                    chunk, way, first, last, self.line if step > 0 else self.pairs
+                ).start()
+
+    def to_members(self, chunk, held):
+        lines = self.lines
+        for way in range(2):
+            end = 0 if way else lines - 1
+
+            @pl.when(self.z == end)
+            def _():
+                kept = (0, 1) if way else (lines - 1, lines)
+                self.line_copy(chunk, way, kept[0], kept[1], self.line).wait_recv()
+
+            for step in range(lines - 1):
+                at = lines - 1 - step if way else step
+                first, last = (0, at) if way else (at + 1, lines)
+
+                @pl.when(self.z == at)
+                def _():
+                    self.line_copy(chunk, way, first, last, self.line).wait_send()
+
+        held[...] = self.pairs[chunk, self.z].astype(wide)
+
+        @pl.when(self.z > 0)
+        def _():
+            held[...] += self.line[chunk, 0, self.z].astype(wide)
+
+        @pl.when(self.z < lines - 1)
+        def _():
+            held[...] += self.line[chunk, 1, self.z].astype(wide)
+
+        self.shares[chunk, self.member] = held[...].astype(low)
+        for step in range(1, self.members):
+            self.share_copy(chunk, step).start()
+
+    def result(self, chunk):
+        for step in range(1, self.members):
+            self.share_copy(chunk, step).wait()
+        total = self.shares[chunk, 0].astype(wide)
+        for member in range(1, self.members):
+            total = total + self.shares[chunk, member].astype(wide)
+        return total
+
+
+def summing_scratch(groups, members, chunks, rows, columns):
+    lines = groups // 4
+    return [
+        pltpu.VMEM((chunks, lines, 2, rows, columns), low),
+        pltpu.VMEM((chunks, lines, rows, columns), low),
+        pltpu.VMEM((chunks, 2, lines, rows, columns), low),
+        pltpu.VMEM((chunks, members, rows, columns), low),
+        pltpu.SemaphoreType.DMA((chunks,)),
+        pltpu.SemaphoreType.DMA((chunks,)),
+        pltpu.SemaphoreType.DMA((chunks,)),
+        pltpu.SemaphoreType.DMA((chunks,)),
+        pltpu.SemaphoreType.DMA((chunks, 2)),
+        pltpu.SemaphoreType.DMA((chunks, 2)),
+        pltpu.SemaphoreType.DMA((chunks, max(members - 1, 1))),
+        pltpu.SemaphoreType.DMA((chunks, max(members - 1, 1))),
+    ]
+
+
+def stage_delays(lines):
+    return [1, 4] + [6 + 2 * step for step in range(lines - 2)] + [2 * lines + 2, 2 * lines + 6]
+
+
 def feed_weights(rest_ref, out, inner, outer, sem):
     count, _, width = rest_ref.shape
     unit = width // count
@@ -956,6 +1166,15 @@
             )
         )
     return copies
+
+
+def feed_arrival(rest_ref, inner, outer, sem, j):
+    feeds = inner.shape[0]
+    unit = inner.shape[2]
+    pltpu.make_async_copy(rest_ref.at[:, :unit, :], inner.at[j], sem.at[1 + j]).wait()
+    pltpu.make_async_copy(
+        rest_ref.at[: outer.shape[1], : outer.shape[2], :], outer.at[j], sem.at[1 + feeds + j]
+    ).wait()
 
 
 def feed_buffers(rest, feeds):
@@ -987,8 +1206,10 @@
     width = tokens_ref.shape[1]
     feeds = pre_ref.shape[0]
     copies = feed_weights(rest_ref, out, inner, outer, sem)
-    for copy in copies:
-        copy.start()
+    copies[0].start()
+    for j in range(feeds):
+        copies[1 + j].start()
+        copies[1 + feeds + j].start()
     copies[0].wait()
     hidden = tokens_ref[...].astype(wide) + product(
         attended_ref[...].astype(low), out[...].reshape(width, width)
@@ -996,10 +1217,9 @@
     hidden_ref[...] = hidden
     inner_in[...] = (hidden * rms_factor(hidden) * gains_ref[1:2, :]).astype(low)
     encoded_ref[...] = hidden
-    for copy in copies[1:]:
-        copy.wait()
 
     def step(j, carry):
+        feed_arrival(rest_ref, inner, outer, sem, j)
         pre = product(inner_in[...], inner[j].reshape(width, width))
         pre_ref[j] = pre.astype(low)
         encoded_ref[...] += product(
@@ -1104,8 +1324,10 @@
             swap(i + 1).start()
 
     copies = feed_weights(rest_ref, out, inner, outer, sem)
-    for copy in copies[1 + feeds :] + copies[1 : 1 + feeds] + copies[:1]:
-        copy.start()
+    for j in range(feeds):
+        copies[1 + feeds + j].start()
+        copies[1 + j].start()
+    copies[0].start()
     start_copies = [
         pltpu.make_async_copy(
             rest_ref.at[:, base + unit * i : base + unit * (i + 1), :],
@@ -1125,8 +1347,6 @@
     grad_inner_in[...] = jnp.zeros_like(grad_inner_in)
     pl.semaphore_wait(barrier, len(partners))
     swap(0).start()
-    for copy in copies[1:]:
-        copy.wait()
 
     def outer_put(j, slot):
         per = lines // feeds
@@ -1143,6 +1363,7 @@
 
     def step(j, carry):
         slot = lax.rem(j, 2)
+        feed_arrival(rest_ref, inner, outer, sem, j)
         pre = pre_ref[j].astype(wide)
         grad_act = back_product(grad_branch[...], outer[j].reshape(width, width))
         grad_pre = (gelu_slope(pre) * grad_act).astype(low)
@@ -1283,204 +1504,6 @@
     )(
         grad_context, encoded, hidden, pre, attended, rest, gains, sum_rows, starts
     )
-
-
-class Summing:
-    def __init__(self, groups, members, buffers):
-        self.groups = groups
-        self.members = members
-        self.lines = groups // 4
-        self.group = lax.axis_index("batch")
-        self.member = lax.axis_index("seq")
-        self.z = self.group // 4
-        self.y = lax.rem(self.group // 2, 2)
-        self.core = lax.rem(self.group, 2)
-        (
-            self.chip,
-            self.pairs,
-            self.line,
-            self.shares,
-            self.chip_send,
-            self.chip_recv,
-            self.pair_send,
-            self.pair_recv,
-            self.line_send,
-            self.line_recv,
-            self.share_send,
-            self.share_recv,
-        ) = buffers
-        self.stages = 3 + self.lines
-
-    def batch_id(self, offset):
-        return {"batch": self.group + offset}
-
-    def neighbours(self):
-        found = [
-            (None, self.batch_id(1 - 2 * self.core)),
-            (None, self.batch_id(2 - 4 * self.y)),
-            (self.z > 0, self.batch_id(-4)),
-            (self.z < self.lines - 1, self.batch_id(4)),
-        ]
-        for step in range(1, self.members):
-            found.append((None, {"seq": lax.rem(self.member + step, self.members)}))
-        return found
-
-    def greet(self, barrier):
-        for condition, device in self.neighbours():
-            if condition is None:
-                pl.semaphore_signal(barrier, inc=1, device_id=device, device_id_type=MESH)
-            else:
-
-                @pl.when(condition)
-                def _():
-                    pl.semaphore_signal(barrier, inc=1, device_id=device, device_id_type=MESH)
-
-    def greeted(self, barrier):
-        ends = (self.z > 0).astype(jnp.int32) + (self.z < self.lines - 1).astype(jnp.int32)
-        pl.semaphore_wait(barrier, 2 + self.members - 1 + ends)
-
-    def copy(self, source, target, send, recv, device):
-        return pltpu.make_async_remote_copy(
-            src_ref=source,
-            dst_ref=target,
-            send_sem=send,
-            recv_sem=recv,
-            device_id=device,
-            device_id_type=MESH,
-        )
-
-    def chip_copy(self, chunk, source):
-        return self.copy(
-            source,
-            self.chip.at[chunk],
-            self.chip_send.at[chunk],
-            self.chip_recv.at[chunk],
-            self.batch_id(1 - 2 * self.core),
-        )
-
-    def pair_copy(self, chunk):
-        return self.copy(
-            self.chip.at[chunk, :, 1 - self.y],
-            self.pairs.at[chunk],
-            self.pair_send.at[chunk],
-            self.pair_recv.at[chunk],
-            self.batch_id(2 - 4 * self.y),
-        )
-
-    def line_copy(self, chunk, way, first, last, source):
-        return self.copy(
-            source.at[chunk, pl.ds(first, last - first)]
-            if source is self.pairs
-            else source.at[chunk, way, pl.ds(first, last - first)],
-            self.line.at[chunk, way, pl.ds(first, last - first)],
-            self.line_send.at[chunk, way],
-            self.line_recv.at[chunk, way],
-            self.batch_id(-4 if way else 4),
-        )
-
-    def share_copy(self, chunk, step):
-        return self.copy(
-            self.shares.at[chunk, self.member],
-            self.shares.at[chunk, self.member],
-            self.share_send.at[chunk, step - 1],
-            self.share_recv.at[chunk, step - 1],
-            {"seq": lax.rem(self.member + step, self.members)},
-        )
-
-    def start(self, chunk, source):
-        self.chip_copy(chunk, source).start()
-
-    def to_pair(self, chunk, source, own):
-        self.chip_copy(chunk, source).wait()
-        self.chip[chunk] = (self.chip[chunk].astype(wide) + own.astype(wide)).astype(low)
-        self.pair_copy(chunk).start()
-
-    def to_line(self, chunk, step):
-        lines = self.lines
-        if step == 0:
-            self.pair_copy(chunk).wait()
-            self.pairs[chunk] = (
-                self.pairs[chunk].astype(wide) + self.chip[chunk, :, self.y].astype(wide)
-            ).astype(low)
-        for way in range(2):
-            at = lines - 1 - step if way else step
-            first, last = (0, at) if way else (at + 1, lines)
-
-            @pl.when(self.z == at)
-            def _():
-                if step > 0:
-                    kept = (0, at + 1) if way else (at, lines)
-                    self.line_copy(chunk, way, kept[0], kept[1], self.line).wait_recv()
-                    span = pl.ds(first, last - first)
-                    self.line[chunk, way, span] = (
-                        self.line[chunk, way, span].astype(wide)
-                        + self.pairs[chunk, span].astype(wide)
-                    ).astype(low)
-                self.line_copy(
-                    chunk, way, first, last, self.line if step > 0 else self.pairs
-                ).start()
-
-    def to_members(self, chunk, held):
-        lines = self.lines
-        for way in range(2):
-            end = 0 if way else lines - 1
-
-            @pl.when(self.z == end)
-            def _():
-                kept = (0, 1) if way else (lines - 1, lines)
-                self.line_copy(chunk, way, kept[0], kept[1], self.line).wait_recv()
-
-            for step in range(lines - 1):
-                at = lines - 1 - step if way else step
-                first, last = (0, at) if way else (at + 1, lines)
-
-                @pl.when(self.z == at)
-                def _():
-                    self.line_copy(chunk, way, first, last, self.line).wait_send()
-
-        held[...] = self.pairs[chunk, self.z].astype(wide)
-
-        @pl.when(self.z > 0)
-        def _():
-            held[...] += self.line[chunk, 0, self.z].astype(wide)
-
-        @pl.when(self.z < lines - 1)
-        def _():
-            held[...] += self.line[chunk, 1, self.z].astype(wide)
-
-        self.shares[chunk, self.member] = held[...].astype(low)
-        for step in range(1, self.members):
-            self.share_copy(chunk, step).start()
-
-    def result(self, chunk):
-        for step in range(1, self.members):
-            self.share_copy(chunk, step).wait()
-        total = self.shares[chunk, 0].astype(wide)
-        for member in range(1, self.members):
-            total = total + self.shares[chunk, member].astype(wide)
-        return total
-
-
-def summing_scratch(groups, members, chunks, rows, columns):
-    lines = groups // 4
-    return [
-        pltpu.VMEM((chunks, lines, 2, rows, columns), low),
-        pltpu.VMEM((chunks, lines, rows, columns), low),
-        pltpu.VMEM((chunks, 2, lines, rows, columns), low),
-        pltpu.VMEM((chunks, members, rows, columns), low),
-        pltpu.SemaphoreType.DMA((chunks,)),
-        pltpu.SemaphoreType.DMA((chunks,)),
-        pltpu.SemaphoreType.DMA((chunks,)),
-        pltpu.SemaphoreType.DMA((chunks,)),
-        pltpu.SemaphoreType.DMA((chunks, 2)),
-        pltpu.SemaphoreType.DMA((chunks, 2)),
-        pltpu.SemaphoreType.DMA((chunks, max(members - 1, 1))),
-        pltpu.SemaphoreType.DMA((chunks, max(members - 1, 1))),
-    ]
-
-
-def stage_delays(lines):
-    return [1, 3] + [4 + step for step in range(lines - 2)] + [lines + 2, lines + 3]
 
 
 def attend_back_kernel(
@@ -1713,11 +1736,13 @@
             row = near_ref[half]
             before = middle - LANES
             after = middle + reach
-            bias[half, before:after, :] = turned_biases(row, size, lead).T
+            bias[half, before:after, :] = turned_biases(row, size, lead).T.astype(low)
             if before > 0:
-                bias[half, :before, :] = jnp.broadcast_to(row[:, :1], (before, size))
+                bias[half, :before, :] = jnp.broadcast_to(row[:, :1], (before, size)).astype(low)
             if after < width:
-                bias[half, after:, :] = jnp.broadcast_to(row[:, -1:], (width - after, size))
+                bias[half, after:, :] = jnp.broadcast_to(
+                    row[:, -1:], (width - after, size)
+                ).astype(low)
         grad_scores[...] = jnp.zeros_like(grad_scores)
         grad_k_sum[...] = jnp.zeros_like(grad_k_sum)
         grad_v_sum[...] = jnp.zeros_like(grad_v_sum)
@@ -1759,7 +1784,8 @@
             [grad_part, (-in_parts(row_term, 3 * half)).astype(low)], axis=1
         )
         weights = jnp.exp(
-            back_product(key_side[...], query_side) + bias[half, pl.ds(start, pack), :]
+            back_product(key_side[...], query_side)
+            + bias[half, pl.ds(start, pack), :].astype(wide)
         )
         grad_block = (weights * back_product(value_side[...], grad_side)).astype(low)
         grad_scores[LANES : LANES + pack, :] = grad_block
@@ -1809,16 +1835,22 @@
         above = jnp.sum(jnp.where(key >= begin + reach, sums, 0.0), axis=0, keepdims=True)
         columns = bands.shape[1]
         mirror = (
-            lax.broadcasted_iota(jnp.int32, (size, columns), 0)
-            + lax.broadcasted_iota(jnp.int32, (size, columns), 1)
+            lax.broadcasted_iota(jnp.int32, (size, size), 0)
+            + lax.broadcasted_iota(jnp.int32, (size, size), 1)
             == size - 1
-        ).astype(wide)
+        ).astype(wide).astype(low)
         row_lane = lax.broadcasted_iota(jnp.int32, (1, LANES), 1)
         for half in range(2):
-            flipped = jnp.dot(
-                band_sum[half], mirror, precision=highest, preferred_element_type=wide
+            rest = band_sum[half]
+            flipped = jnp.zeros_like(rest)
+            for _ in range(3):
+                head_part = rest.astype(low)
+                flipped = flipped + product(head_part, mirror)
+                rest = rest - head_part.astype(wide)
+            padded = jnp.concatenate(
+                [flipped, jnp.zeros((rest.shape[0], columns - size), wide)], axis=1
             )
-            turned = pltpu.roll(flipped, 0, 1, stride=1, stride_axis=0)
+            turned = pltpu.roll(padded, 0, 1, stride=1, stride_axis=0)
             head = pl.ds(2 * pair + half, 1)
             bands[head, :] = jnp.sum(turned, axis=0, keepdims=True)
             own_lanes = row_lane // 8 == half
@@ -1919,7 +1951,7 @@
             jax.ShapeDtypeStruct((part, width), wide),
         ],
         scratch_shapes=[
-            pltpu.VMEM((2, columns, size), wide),
+            pltpu.VMEM((2, columns, size), low),
             pltpu.VMEM((pack, 2 * LANES), low),
             pltpu.VMEM((pack, 2 * LANES), low),
             pltpu.VMEM((LANES, pack), low),
@@ -1968,14 +2000,14 @@
     groups,
     seqs,
     halves,
-    grad_q_ref,
-    grad_k_ref,
-    grad_v_ref,
-    first_ref,
+    grad_q_any,
+    grad_k_any,
+    grad_v_any,
+    first_any,
+    grad_hidden_any,
+    rows_any,
     tokens_ref,
-    grad_hidden_ref,
     gains_ref,
-    rows_ref,
     sums_ref,
     starts_ref,
     backs_ref,
@@ -1989,6 +2021,8 @@
     key_sums_ref,
     value_sums_ref,
     inner_sums_ref,
+    out_sums_ref,
+    outer_sums_ref,
     grad_tokens_ref,
     vectors_ref,
     grad_self_value_ref,
@@ -2000,7 +2034,20 @@
     grad_second_inner_ref,
     grad_second_outer_ref,
     grad_pooler_ref,
+    query_out,
+    key_out,
+    value_out,
+    inner_out,
+    attention_out,
+    outer_out,
     pieces,
+    grad_q_ref,
+    grad_k_ref,
+    grad_v_ref,
+    first_ref,
+    grad_hidden_ref,
+    rows_ref,
+    copy_sem,
 ):
     rows, width = tokens_ref.shape
     part = query_ref.shape[0]
@@ -2008,13 +2055,31 @@
     number = groups * seqs
     every = 2 * HEAD_ROWS
     group = lax.axis_index("batch")
-    grad_normed = (
-        back_product(grad_q_ref[...], first_ref[0])
-        + back_product(grad_k_ref[...], first_ref[1])
-        + back_product(grad_v_ref[...], first_ref[2])
-    )
-    grad_tokens, _ = rms_back(tokens_ref[...].astype(wide), gains_ref[:1, :], grad_normed)
-    grad_tokens_ref[...] = grad_tokens + grad_hidden_ref[...]
+    copies = [
+        pltpu.make_async_copy(source, target, copy_sem.at[i])
+        for i, (source, target) in enumerate(
+            (
+                (rows_any, rows_ref),
+                (grad_q_any, grad_q_ref),
+                (grad_k_any, grad_k_ref),
+                (grad_v_any, grad_v_ref),
+                (first_any, first_ref),
+                (grad_hidden_any, grad_hidden_ref),
+            )
+        )
+    ]
+    for copy in copies:
+        copy.start()
+    for source, target in (
+        (query_sums_ref, query_out),
+        (key_sums_ref, key_out),
+        (value_sums_ref, value_out),
+        (inner_sums_ref, inner_out),
+        (out_sums_ref, attention_out),
+        (outer_sums_ref, outer_out),
+    ):
+        target[...] = source[...]
+    copies[0].wait()
 
     def chooser(count, first):
         row = lax.broadcasted_iota(jnp.int32, (count, width), 0)
@@ -2129,6 +2194,16 @@
     ):
         vectors_ref[i] = row
 
+    for copy in copies[1:]:
+        copy.wait()
+    grad_normed = (
+        back_product(grad_q_ref[...], first_ref[0])
+        + back_product(grad_k_ref[...], first_ref[1])
+        + back_product(grad_v_ref[...], first_ref[2])
+    )
+    grad_tokens, _ = rms_back(tokens_ref[...].astype(wide), gains_ref[:1, :], grad_normed)
+    grad_tokens_ref[...] = grad_tokens + grad_hidden_ref[...]
+
 
 def last_step(groups, seqs, halves, tokens, part, share, feeds, *arrays):
     rows, width = tokens.shape
@@ -2137,8 +2212,8 @@
     return pl.pallas_call(
         functools.partial(last_kernel, groups, seqs, halves),
         name="last",
-        in_specs=[whole] * len(arrays),
-        out_specs=[whole] * 11,
+        in_specs=[pl.BlockSpec(memory_space=pltpu.HBM)] * 6 + [whole] * (len(arrays) - 6),
+        out_specs=[whole] * 17,
         out_shape=[
             jax.ShapeDtypeStruct((rows, width), wide),
             jax.ShapeDtypeStruct((8, 1, part), wide),
@@ -2151,9 +2226,22 @@
             jax.ShapeDtypeStruct((part, feeds * width), wide),
             jax.ShapeDtypeStruct((share, width), wide),
             square,
+            square,
+            square,
+            square,
+            jax.ShapeDtypeStruct((part, feeds * width), wide),
+            square,
+            jax.ShapeDtypeStruct((share, width), wide),
         ],
         scratch_shapes=[
-            pltpu.VMEM((width // LANES, groups * seqs * 2 * HEAD_ROWS, LANES), wide)
+            pltpu.VMEM((width // LANES, groups * seqs * 2 * HEAD_ROWS, LANES), wide),
+            pltpu.VMEM((rows, width), low),
+            pltpu.VMEM((rows, width), low),
+            pltpu.VMEM((rows, width), low),
+            pltpu.VMEM((3, width, width), low),
+            pltpu.VMEM((rows, width), wide),
+            pltpu.VMEM((groups * seqs, 2 * HEAD_ROWS, width), low),
+            pltpu.SemaphoreType.DMA((6,)),
         ],
         compiler_params=pltpu.CompilerParams(vmem_limit_bytes=50 * 2**20),
     )(*arrays)
@@ -2350,6 +2438,12 @@
         grad_second_inner,
         grad_second_outer,
         grad_pooler,
+        query_sums,
+        key_sums,
+        value_sums,
+        inner_sums,
+        out_sums,
+        outer_sums,
     ) = last_step(
         groups,
         seqs,
@@ -2362,10 +2456,10 @@
         grad_key_rows,
         grad_value_rows,
         first_full,
+        grad_hidden,
+        decoder_rows.reshape(groups * seqs, 2 * HEAD_ROWS, width),
         tokens,
-        grad_hidden,
         gains,
-        decoder_rows.reshape(groups * seqs, 2 * HEAD_ROWS, width),
         sums,
         starts,
         backs,
@@ -2379,6 +2473,8 @@
         key_sums,
         value_sums,
         inner_sums,
+        out_sums,
+        outer_sums,
     )
     half_share = share // halves
     grad_second_inner = jnp.transpose(

time: 434 us -> 401 us (0.924)
  Pallas kernels: 363 us -> 330 us
  local copies, waits for them, and re-layouts: 35 us -> 28.7 us
  waiting for transfers between devices: 14.6 us -> 19.8 us
    pallas_call x1, Pallas kernels: 138 us -> 116 us  [attend_back(): pl.pallas_call(functools.partial(attend_back_kernel, groups, members), na...]
    unnamed x110 -> x86, local copies, waits for them, and re-layouts: 16.9 us -> 10.2 us
    pallas_call x1, Pallas kernels: 40.6 us -> 34.5 us  [attend(): pl.pallas_call(attend_kernel, name='attend', grid=(pairs,), in_specs=[pl....]
    all_gather x1, waiting for transfers between devices: 14.6 us -> 19.8 us  [shards(): rest = lax.all_gather(rest_part, 'batch', axis=0, tiled=False)]
  transfers between devices with their start and end apart: 2 -> 2, of which waited for: 1 -> 1; matrix products, arithmetic and copies ran while one was open for 3% -> 4% of each run, Pallas kernels for 70% -> 67%
where the time goes in v4:
time: 401 us; the launch traced here: 398 us
  Pallas kernels  330 us (82%)
  local copies, waits for them, and re-layouts  28.7 us (7%)
  waiting for transfers between devices  19.8 us (5%)
  between operations  15 us (4%)
    pallas_call x1, Pallas kernels, attend_back(): pl.pallas_call(functools.partial(attend_back_kernel, groups, members), na...  116 us
    pallas_call x1, Pallas kernels, project(): pl.pallas_call(functools.partial(first_kernel, groups, members), name='pr...  76 us
    pallas_call x1, Pallas kernels, feed_back(): pl.pallas_call(functools.partial(feed_back_kernel, base, groups, members)...  42 us
    pallas_call x1, Pallas kernels, attend(): pl.pallas_call(attend_kernel, name='attend', grid=(pairs,), in_specs=[pl....  34.5 us
    pallas_call x1, Pallas kernels, decoder_step(): pl.pallas_call(functools.partial(decoder_kernel, base, groups, members, s...  33.6 us
    all_gather x1, waiting for transfers between devices, shards(): rest = lax.all_gather(rest_part, 'batch', axis=0, tiled=False)  19.8 us
    pallas_call x1, Pallas kernels, feed_forward(): pl.pallas_call(feed_kernel, name='feed_forward', in_specs=[whole, whole,...  15.5 us
    pallas_call x1, Pallas kernels, last_step(): pl.pallas_call(functools.partial(last_kernel, groups, seqs, halves), name...  13 us
  transfers between devices with their start and end apart: 2, of which 1 were waited for; matrix products, arithmetic and copies ran while one was open for 4% of the time, Pallas kernels for 67%

profile of v4, /device:TPU:0, one launch (start us, length us, event | category | flops | bytes accessed | tf_op | source)
XLA Modules:
  0.0 398.1 jit_solution(6026792028571686615)
XLA Ops:
  7.3 1.0 copy.78
  8.3 1.1 pad_maximum_fusion
  10.9 1.1 copy-done.21
  12.1 0.8 reduce-window.4
  12.9 0.7 reshape.139
  14.3 76.0 %project.1 = (bf16[768,768]{1,0:T(8,128)(2,1)S(1)}, bf16[1536,768]{1,0:T(8,128)(2,1)S(1)}, bf16[1536,768]{1,0:T(8,128)(2,1)}, bf16[1536,768]{1,0:T(8,128)(2,1)},...) custom-call(bf16[768,768]{1,0:T(8,128)(2,1)S(1)} %copy-done, bf16[16,768]{1,0:T(8,128)(2,1)S(1)} %dynamic_update_slice.7.extra_ref, ...), custom_call_target="tpu_custom_call" | custom-call | flops 2147483648 | bytes 37748736 | tf_op jit(solution)/shard_map/project/pallas_call | solution.py:365
  90.3 1.4 copy-done.19
  92.0 0.7 broadcast_in_dim.22.near_ref
  92.7 4.4 %copy.72 = bf16[1536,768]{0,1:T(8,128)(2,1)} copy(bf16[1536,768]{1,0:T(8,128)(2,1)} %get-tuple-element.93) | data formatting | bytes 4718592 | tf_op jit(solution)/shard_map/project/pallas_call | solution.py:365
  97.1 0.6 pad.4.target_ref
  97.7 0.6 fusion.13
  98.3 1.9 pad_add_fusion.place
  100.2 2.4 dynamic-slice_bitcast_fusion.own_turned_ref
  102.6 34.5 %attend.1 = (f32[768,768]{1,0:T(8,128)}, f32[768,128]{1,0:T(8,128)}) custom-call(s32[4]{0:T(128)} %pad_add_fusion.place, bf16[768,768]{1,0:T(8,128)(2,1)} %copy-done.20, bf16[1536,768]{1,0:T(8,128)(2,1)} %copy-done.19, bf16[1536,768]{1,0:T(8,128)(2,1)} %get-tuple-element.79.v_ref, f32[12,1,768]{2,1,0:T(1,128)} %broadcast_in_dim.22.near_ref), custom_call_target="tpu_custom_call" | custom-call | flops 14495514624 | bytes 18874368 | tf_op jit(solution)/shard_map/attend/pallas_call | solution.py:469
  137.1 19.8 %all-gather.6.cloned.1.call-done = bf16[15360,768]{1,0:T(8,128)(2,1)} async-done(((bf16[960,768]{1,0:T(8,128)(2,1)}), bf16[15360,768]{1,0:T(8,128)(2,1)}) %all-gather.6.cloned.1.call-update) | async-done | bytes 23592976 | tf_op jit(solution)/shard_map/all_gather | solution.py:2367
  156.9 15.5 %feed_forward.1 = (f32[768,768]{1,0:T(8,128)}, bf16[4,768,768]{2,1,0:T(8,128)(2,1)}, f32[768,768]{1,0:T(8,128)}, bf16[768,768]{1,0:T(8,128)(2,1)S(1)}) custom-call(f32[768,768]{1,0:T(8,128)} %get-tuple-element.81.attended_ref, bf16[768,768]{1,0:T(8,128)(2,1)S(1)} %copy-done, bf16[16,960,768]{2,1,0:T(8,128)(2,1)} %bitcast.55, ...), custom_call_target="tpu_custom_call" | custom-call | flops 8153726976 | bytes 23592960 | tf_op jit(solution)/shard_map/feed_forward/pallas_call | solution.py:1238
  172.4 1.0 copy-done.1
  173.4 33.6 %decoder.1 = (f32[8,768]{1,0:T(8,128)}, f32[8,128]{1,0:T(8,128)}, f32[768,768]{1,0:T(8,128)}, bf16[3,32,768]{2,1,0:T(8,128)(2,1)}, f32[8,768]{1,0:T(8,128)}, /*index=5*/f32[24,768]{1,0:T(8,128)}) custom-call(s32[4]{0:T(128)} %pad_add_fusion.place, bf16[768,768]{1,0:T(8,128)(2,1)} %copy-done.1, bf16[16,960,768]{2,1,0:T(8,128)(2,1)} %bitcast.56, ...), custom_call_target="tpu_custom_call" | custom-call | flops 353894400 | bytes 23592960 | tf_op jit(solution)/shard_map/decoder/pallas_call | solution.py:907
  207.0 1.2 slice.62
  208.2 1.3 slice.63
  209.6 42.0 %feed_back.1 = (bf16[4,2,2,9,48,768]{5,4,3,2,1,0:T(8,128)(2,1)}, f32[768,768]{1,0:T(8,128)}, bf16[768,768]{1,0:T(8,128)(2,1)}, f32[24,768]{1,0:T(8,128)}, f32[8,768]{1,0:T(8,128)}) custom-call(f32[768,768]{1,0:T(8,128)} %get-tuple-element.85.grad_context_ref, f32[768,768]{1,0:T(8,128)} %get-tuple-element.86.encoded_ref, ...), custom_call_target="tpu_custom_call" | custom-call | flops 16307453952 | bytes 47185920 | tf_op jit(solution)/shard_map/feed_back/pallas_call | solution.py:1472
  251.7 115.9 %attend_back.1 = (bf16[768,768]{1,0:T(8,128)(2,1)}, bf16[768,768]{1,0:T(8,128)(2,1)}, bf16[768,768]{1,0:T(8,128)(2,1)}, f32[16,128]{1,0:T(8,128)}, f32[48,768]{1...) custom-call(s32[4]{0:T(128)} %pad_add_fusion.place, ...), custom_call_target="tpu_custom_call" | custom-call | flops 36238786560 | bytes 18874368 | tf_op jit(solution)/shard_map/attend_back/pallas_call | solution.py:1920
  367.6 0.8 dynamic-slice_bitcast_fusion.1
  368.3 0.6 copy.75
  369.0 1.1 copy-done.3
  370.1 1.1 copy-done.4
  371.2 0.9 copy-done.9
  372.1 0.9 copy-done.10
  373.0 0.9 copy-done.11
  373.9 0.9 copy-done.12
  374.8 13.0 %last.1 = (f32[768,768]{1,0:T(8,128)}, f32[8,1,48]{2,1,0:T(1,128)S(1)}, f32[48,768]{1,0:T(8,128)}, f32[48,768]{1,0:T(8,128)}, f32[48,768]{1,0:T(8,128)}, /*index...) custom-call(bf16[768,768]{1,0:T(8,128)(2,1)} %get-tuple-element.95.g, ...), custom_call_target="tpu_custom_call" | custom-call | tf_op jit(solution)/shard_map/last/pallas_call | solution.py:2212
  389.0 1.9 reshape.147
  (98 shorter events, 3.5 us)
Async XLA Ops:
  7.2 149.7 %all-gather.6.cloned.1.call-start = ((), (), s32[]{:S(2)}) async-start(), calls=%async_computation.1 | async-start | bytes 25067520 | tf_op jit(solution)/shard_map/all_gather | solution.py:2367
  8.2 1.2 copy-start.22
  9.3 1.1 copy-start.24
  9.4 1.1 copy-start.25
  9.4 1.2 copy-start.26
  9.4 1.3 copy-start.5
  9.5 1.3 copy-start.6
  9.5 1.3 copy-start.27
  9.5 1.3 copy-start.28
  9.5 1.3 copy-start.23
  10.5 3.1 copy-start.29
  10.6 3.1 copy-start.30
  10.6 3.1 copy-start.31
  10.6 3.1 copy-start.32
  10.6 3.7 copy-start
  10.6 3.7 copy-start.13
  10.6 3.7 copy-start.14
  10.6 3.7 copy-start.15
  10.7 3.0 copy-start.33
  10.7 3.0 copy-start.34
  10.7 3.0 copy-start.35
  10.7 3.0 copy-start.36
  12.0 357.0 %all-gather.4.cloned.1.call-start = ((), (), s32[]{:S(2)}) async-start(), calls=%async_computation | async-start | bytes 2506752 | tf_op jit(solution)/shard_map/all_gather | solution.py:2385
  90.3 1.4 copy-start.19
  91.7 5.4 %copy-start.20 = (bf16[768,768]{1,0:T(8,128)(2,1)}, bf16[768,768]{1,0:T(8,128)(2,1)S(1)}, u32[]{:S(2)}) copy-start(bf16[768,768]{1,0:T(8,128)(2,1)S(1)} %get-tuple-element.77.q_ref) | copy-start | bytes 3538948
  91.7 65.2 %copy-start.7 = (f32[16,768]{1,0:T(8,128)}, f32[16,768]{1,0:T(8,128)S(1)}, u32[]{:S(2)}) copy-start(f32[16,768]{1,0:T(8,128)S(1)} %get-tuple-element.80.gains_ref) | copy-start | bytes 147460
  92.7 4.4 %copy-start.37 = (s32[48]{0:T(128)S(1)}, s32[48]{0:T(128)}, u32[]{:S(2)}) copy-start(s32[48]{0:T(128)} %param.29) | copy-start | bytes 580
  251.6 117.4 %copy-start.2 = (bf16[48,3072]{1,0:T(8,128)(2,1)S(1)}, bf16[48,3072]{1,0:T(8,128)(2,1)}, u32[]{:S(2)}) copy-start(bf16[48,3072]{1,0:T(8,128)(2,1)} %inner_ref.1) | copy-start | bytes 884740
  251.6 117.4 %copy-start.8 = (f32[16,768]{1,0:T(8,128)S(1)}, f32[16,768]{1,0:T(8,128)}, u32[]{:S(2)}) copy-start(f32[16,768]{1,0:T(8,128)} %copy-done.7) | copy-start | bytes 147460
  251.6 117.4 %copy-start.16 = (f32[24,768]{1,0:T(8,128)S(1)}, f32[24,768]{1,0:T(8,128)}, u32[]{:S(2)}) copy-start(f32[24,768]{1,0:T(8,128)} %get-tuple-element.101.sums_ref) | copy-start | bytes 221188
  251.6 117.4 %copy-start.17 = (f32[8,768]{1,0:T(8,128)S(1)}, f32[8,768]{1,0:T(8,128)}, u32[]{:S(2)}) copy-start(f32[8,768]{1,0:T(8,128)} %get-tuple-element.90.starts_ref) | copy-start | bytes 73732
  251.6 117.4 %copy-start.18 = (f32[8,768]{1,0:T(8,128)S(1)}, f32[8,768]{1,0:T(8,128)}, u32[]{:S(2)}) copy-start(f32[8,768]{1,0:T(8,128)} %get-tuple-element.102.backs_ref) | copy-start | bytes 73732
  (8 other events, 7.9 us)
Sparse Core Ops, SparseCore 0:
  12.1 144.6 all-gather.5
  209.7 43.3 all-gather.3

commit v5 on v4

--- a/solution.py
+++ b/solution.py
@@ -546,6 +546,7 @@
     totals_ref,
     weights,
     everyone,
+    unpacked,
     shared,
     similar_ref,
     halves_sent,
@@ -735,7 +736,9 @@
     embedded = pooled * size
     embedded_ref[...] = embedded
 
-    everyone[0] = embedded
+    tiles = width // LANES
+    for i in range(tiles):
+        everyone[0, 4 * i : 4 * (i + 1), :] = embedded[:4, LANES * i : LANES * (i + 1)]
     sends = []
     for step in range(1, groups):
         sends.append(
@@ -759,7 +762,10 @@
     )
     arrival.wait_recv()
     arrival.wait_send()
-    all_rows = everyone[...].reshape(groups * SEQ_ROWS, width)
+    unpacked[...] = jnp.zeros_like(unpacked)
+    for i in range(tiles):
+        unpacked[:, :4, LANES * i : LANES * (i + 1)] = everyone[:, 4 * i : 4 * (i + 1), :]
+    all_rows = unpacked[...].reshape(groups * SEQ_ROWS, width)
     number = groups * SEQ_ROWS
     row = lax.broadcasted_iota(jnp.int32, (number, number), 0)
     column = lax.broadcasted_iota(jnp.int32, (number, number), 1)
@@ -925,6 +931,7 @@
         ],
         scratch_shapes=[
             pltpu.VMEM((third.shape[0], third.shape[1] - base, width), low),
+            pltpu.VMEM((groups, 4 * width // LANES, LANES), wide),
             pltpu.VMEM((groups, SEQ_ROWS, width), wide),
             pltpu.VMEM((members, seqs * HEAD_ROWS, width + LANES), wide),
             pltpu.VMEM((number, number), wide),
@@ -1340,7 +1347,7 @@
         copy.start()
     sides[0] = rows_ref[...]
     hidden = hidden_ref[...]
-    inner_in[...] = (hidden * rms_factor(hidden) * gains_ref[1:2, :]).astype(low)
+    inner_in[...] = (hidden * rms_factor(hidden) * gains_ref[1:2, :]).astype(low).T
     grad_encoded, _ = rms_back(encoded_ref[...], gains_ref[2:3, :], grad_context_ref[...])
     grad_hidden_ref[...] = grad_encoded
     grad_branch[...] = grad_encoded.astype(low)
@@ -1380,7 +1387,7 @@
         )
         outer_put(j, slot).start()
         inner_grad[slot] = (
-            weight_grad(inner_in[...], grad_pre).reshape(inner_grad.shape[1:]).astype(low)
+            product(inner_in[...], grad_pre).reshape(inner_grad.shape[1:]).astype(low)
         )
         inner_put(j, slot).start()
         for i in range(min(feeds, len(partners))):
@@ -1483,7 +1490,7 @@
         ],
         scratch_shapes=feed_buffers(rest, feeds)
         + [
-            pltpu.VMEM((rows, width), low),
+            pltpu.VMEM((width, rows), low),
             pltpu.VMEM((rows, width), low),
             pltpu.VMEM((rows, width), wide),
             pltpu.VMEM((2, lines // feeds, 2, 2, feeds, part, width), low),
@@ -2006,6 +2013,12 @@
     first_any,
     grad_hidden_any,
     rows_any,
+    query_any,
+    key_any,
+    value_any,
+    inner_any,
+    attention_any,
+    outer_any,
     tokens_ref,
     gains_ref,
     sums_ref,
@@ -2017,12 +2030,6 @@
     inner_ref,
     cross_key_ref,
     cross_value_ref,
-    query_sums_ref,
-    key_sums_ref,
-    value_sums_ref,
-    inner_sums_ref,
-    out_sums_ref,
-    outer_sums_ref,
     grad_tokens_ref,
     vectors_ref,
     grad_self_value_ref,
@@ -2034,12 +2041,12 @@
     grad_second_inner_ref,
     grad_second_outer_ref,
     grad_pooler_ref,
-    query_out,
-    key_out,
-    value_out,
-    inner_out,
-    attention_out,
-    outer_out,
+    query_sums_ref,
+    key_sums_ref,
+    value_sums_ref,
+    inner_sums_ref,
+    attention_sums_ref,
+    outer_sums_ref,
     pieces,
     grad_q_ref,
     grad_k_ref,
@@ -2065,20 +2072,17 @@
                 (grad_v_any, grad_v_ref),
                 (first_any, first_ref),
                 (grad_hidden_any, grad_hidden_ref),
+                (query_any, query_sums_ref),
+                (key_any, key_sums_ref),
+                (value_any, value_sums_ref),
+                (inner_any, inner_sums_ref),
+                (attention_any, attention_sums_ref),
+                (outer_any, outer_sums_ref),
             )
         )
     ]
     for copy in copies:
         copy.start()
-    for source, target in (
-        (query_sums_ref, query_out),
-        (key_sums_ref, key_out),
-        (value_sums_ref, value_out),
-        (inner_sums_ref, inner_out),
-        (out_sums_ref, attention_out),
-        (outer_sums_ref, outer_out),
-    ):
-        target[...] = source[...]
     copies[0].wait()
 
     def chooser(count, first):
@@ -2168,6 +2172,8 @@
         ones = jnp.ones((8, grads.shape[1]), wide)
         return exact(ones, weight.astype(wide) * grads)[:1]
 
+    for copy in copies[1:]:
+        copy.wait()
     attention = (
         gain_sum(query_ref[...], query_sums_ref[...])
         + gain_sum(key_ref[...], key_sums_ref[...])
@@ -2194,8 +2200,6 @@
     ):
         vectors_ref[i] = row
 
-    for copy in copies[1:]:
-        copy.wait()
     grad_normed = (
         back_product(grad_q_ref[...], first_ref[0])
         + back_product(grad_k_ref[...], first_ref[1])
@@ -2212,7 +2216,8 @@
     return pl.pallas_call(
         functools.partial(last_kernel, groups, seqs, halves),
         name="last",
-        in_specs=[pl.BlockSpec(memory_space=pltpu.HBM)] * 6 + [whole] * (len(arrays) - 6),
+        in_specs=[pl.BlockSpec(memory_space=pltpu.HBM)] * 12
+        + [whole] * (len(arrays) - 12),
         out_specs=[whole] * 17,
         out_shape=[
             jax.ShapeDtypeStruct((rows, width), wide),
@@ -2241,9 +2246,9 @@
             pltpu.VMEM((3, width, width), low),
             pltpu.VMEM((rows, width), wide),
             pltpu.VMEM((groups * seqs, 2 * HEAD_ROWS, width), low),
-            pltpu.SemaphoreType.DMA((6,)),
+            pltpu.SemaphoreType.DMA((12,)),
         ],
-        compiler_params=pltpu.CompilerParams(vmem_limit_bytes=50 * 2**20),
+        compiler_params=pltpu.CompilerParams(vmem_limit_bytes=62 * 2**20),
     )(*arrays)
 
 
@@ -2458,6 +2463,12 @@
         first_full,
         grad_hidden,
         decoder_rows.reshape(groups * seqs, 2 * HEAD_ROWS, width),
+        query_sums,
+        key_sums,
+        value_sums,
+        inner_sums,
+        out_sums,
+        outer_sums,
         tokens,
         gains,
         sums,
@@ -2469,12 +2480,6 @@
         feed_inner,
         cross_key,
         cross_value,
-        query_sums,
-        key_sums,
-        value_sums,
-        inner_sums,
-        out_sums,
-        outer_sums,
     )
     half_share = share // halves
     grad_second_inner = jnp.transpose(

time: 401 us -> 395 us (0.985)
    unnamed x86 -> x64, local copies, waits for them, and re-layouts: 10.2 us -> 4.45 us
  transfers between devices with their start and end apart: 2 -> 2, of which waited for: 1 -> 1; matrix products, arithmetic and copies ran while one was open for 4% -> 4% of each run, Pallas kernels for 67% -> 68%
where the time goes in v5:
time: 395 us; the launch traced here: 392 us
  Pallas kernels  328 us (83%)
  local copies, waits for them, and re-layouts  24.8 us (6%)
  waiting for transfers between devices  19.9 us (5%)
  between operations  14.9 us (4%)
    pallas_call x1, Pallas kernels, attend_back(): pl.pallas_call(functools.partial(attend_back_kernel, groups, members), na...  116 us
    pallas_call x1, Pallas kernels, project(): pl.pallas_call(functools.partial(first_kernel, groups, members), name='pr...  76 us
    pallas_call x1, Pallas kernels, feed_back(): pl.pallas_call(functools.partial(feed_back_kernel, base, groups, members)...  39.9 us
    pallas_call x1, Pallas kernels, attend(): pl.pallas_call(attend_kernel, name='attend', grid=(pairs,), in_specs=[pl....  34.3 us
    pallas_call x1, Pallas kernels, decoder_step(): pl.pallas_call(functools.partial(decoder_kernel, base, groups, members, s...  32.8 us
    all_gather x1, waiting for transfers between devices, shards(): rest = lax.all_gather(rest_part, 'batch', axis=0, tiled=False)  19.9 us
    pallas_call x1, Pallas kernels, feed_forward(): pl.pallas_call(feed_kernel, name='feed_forward', in_specs=[whole, whole,...  15.4 us
    pallas_call x1, Pallas kernels, last_step(): pl.pallas_call(functools.partial(last_kernel, groups, seqs, halves), name...  13.4 us
  transfers between devices with their start and end apart: 2, of which 1 were waited for; matrix products, arithmetic and copies ran while one was open for 4% of the time, Pallas kernels for 68%

profile of v5, /device:TPU:0, one launch (start us, length us, event | category | flops | bytes accessed | tf_op | source)
XLA Modules:
  0.0 391.6 jit_solution(7342457018956375562)
XLA Ops:
  7.3 1.0 copy.78
  8.3 1.1 pad_maximum_fusion
  9.5 0.5 reshape.143
  10.1 0.3 reshape_reshape.3
  10.9 1.1 copy-done.8
  12.1 0.8 reduce-window.4
  12.9 0.7 reshape.139
  13.7 0.3 dynamic_update_slice.6
  14.3 76.0 %project.1 = (bf16[768,768]{1,0:T(8,128)(2,1)S(1)}, bf16[1536,768]{1,0:T(8,128)(2,1)S(1)}, bf16[1536,768]{1,0:T(8,128)(2,1)}, bf16[1536,768]{1,0:T(8,128)(2,1)},...) custom-call(bf16[768,768]{1,0:T(8,128)(2,1)S(1)} %copy-done, bf16[16,768]{1,0:T(8,128)(2,1)S(1)} %dynamic_update_slice.7.extra_ref, ...), custom_call_target="tpu_custom_call" | custom-call | flops 2147483648 | bytes 37748736 | tf_op jit(solution)/shard_map/project/pallas_call | solution.py:365
  90.3 1.4 copy-done.6
  92.0 0.7 broadcast_in_dim.22.near_ref
  92.7 4.4 %copy.72 = bf16[1536,768]{0,1:T(8,128)(2,1)} copy(bf16[1536,768]{1,0:T(8,128)(2,1)} %get-tuple-element.93) | data formatting | bytes 4718592 | tf_op jit(solution)/shard_map/project/pallas_call | solution.py:365
  97.1 0.6 pad.4.target_ref
  97.7 0.6 fusion.13
  98.3 1.9 pad_add_fusion.place
  100.2 2.5 dynamic-slice_bitcast_fusion.own_turned_ref
  102.7 34.3 %attend.1 = (f32[768,768]{1,0:T(8,128)}, f32[768,128]{1,0:T(8,128)}) custom-call(s32[4]{0:T(128)} %pad_add_fusion.place, bf16[768,768]{1,0:T(8,128)(2,1)} %copy-done.7, bf16[1536,768]{1,0:T(8,128)(2,1)} %copy-done.6, bf16[1536,768]{1,0:T(8,128)(2,1)} %get-tuple-element.79.v_ref, f32[12,1,768]{2,1,0:T(1,128)} %broadcast_in_dim.22.near_ref), custom_call_target="tpu_custom_call" | custom-call | flops 14495514624 | bytes 18874368 | tf_op jit(solution)/shard_map/attend/pallas_call | solution.py:469
  137.0 19.9 %all-gather.6.cloned.1.call-done = bf16[15360,768]{1,0:T(8,128)(2,1)} async-done(((bf16[960,768]{1,0:T(8,128)(2,1)}), bf16[15360,768]{1,0:T(8,128)(2,1)}) %all-gather.6.cloned.1.call-update) | async-done | bytes 23592976 | tf_op jit(solution)/shard_map/all_gather | solution.py:2372
  156.8 15.4 %feed_forward.1 = (f32[768,768]{1,0:T(8,128)}, bf16[4,768,768]{2,1,0:T(8,128)(2,1)}, f32[768,768]{1,0:T(8,128)}, bf16[768,768]{1,0:T(8,128)(2,1)S(1)}) custom-call(f32[768,768]{1,0:T(8,128)} %get-tuple-element.81.attended_ref, bf16[768,768]{1,0:T(8,128)(2,1)S(1)} %copy-done, bf16[16,960,768]{2,1,0:T(8,128)(2,1)} %bitcast.54, ...), custom_call_target="tpu_custom_call" | custom-call | flops 8153726976 | bytes 23592960 | tf_op jit(solution)/shard_map/feed_forward/pallas_call | solution.py:1245
  172.2 1.0 copy-done.1
  173.3 32.8 %decoder.1 = (f32[8,768]{1,0:T(8,128)}, f32[8,128]{1,0:T(8,128)}, f32[768,768]{1,0:T(8,128)}, bf16[3,32,768]{2,1,0:T(8,128)(2,1)}, f32[8,768]{1,0:T(8,128)}, /*index=5*/f32[24,768]{1,0:T(8,128)}) custom-call(s32[4]{0:T(128)} %pad_add_fusion.place, bf16[768,768]{1,0:T(8,128)(2,1)} %copy-done.1, bf16[16,960,768]{2,1,0:T(8,128)(2,1)} %bitcast.55, ...), custom_call_target="tpu_custom_call" | custom-call | flops 353894400 | bytes 23592960 | tf_op jit(solution)/shard_map/decoder/pallas_call | solution.py:913
  206.1 1.2 slice.62
  207.3 1.3 slice.63
  208.6 39.9 %feed_back.1 = (bf16[4,2,2,9,48,768]{5,4,3,2,1,0:T(8,128)(2,1)}, f32[768,768]{1,0:T(8,128)}, bf16[768,768]{1,0:T(8,128)(2,1)}, f32[24,768]{1,0:T(8,128)}, f32[8,768]{1,0:T(8,128)}) custom-call(f32[768,768]{1,0:T(8,128)} %get-tuple-element.85.grad_context_ref, f32[768,768]{1,0:T(8,128)} %get-tuple-element.86.encoded_ref, ...), custom_call_target="tpu_custom_call" | custom-call | flops 16307453952 | bytes 47185920 | tf_op jit(solution)/shard_map/feed_back/pallas_call | solution.py:1479
  248.5 116.2 %attend_back.1 = (bf16[768,768]{1,0:T(8,128)(2,1)}, bf16[768,768]{1,0:T(8,128)(2,1)}, bf16[768,768]{1,0:T(8,128)(2,1)}, f32[16,128]{1,0:T(8,128)}, f32[48,768]{1...) custom-call(s32[4]{0:T(128)} %pad_add_fusion.place, ...), custom_call_target="tpu_custom_call" | custom-call | flops 36238786560 | bytes 18874368 | tf_op jit(solution)/shard_map/attend_back/pallas_call | solution.py:1927
  364.8 0.8 dynamic-slice_bitcast_fusion.1
  365.5 0.6 copy.75
  366.2 13.4 %last.1 = (f32[768,768]{1,0:T(8,128)}, f32[8,1,48]{2,1,0:T(1,128)}, f32[48,768]{1,0:T(8,128)}, f32[48,768]{1,0:T(8,128)}, f32[48,768]{1,0:T(8,128)}, /*index=5*/...) custom-call(bf16[768,768]{1,0:T(8,128)(2,1)} %get-tuple-element.95.g, ...), custom_call_target="tpu_custom_call" | custom-call | tf_op jit(solution)/shard_map/last/pallas_call | solution.py:2216
  379.6 1.2 slice_bitcast_fusion
  380.8 1.4 reshape.146
  382.2 0.4 copy.74
  382.6 1.9 reshape.147
  (76 shorter events, 1.1 us)
Async XLA Ops:
  7.2 149.6 %all-gather.6.cloned.1.call-start = ((), (), s32[]{:S(2)}) async-start(), calls=%async_computation.1 | async-start | bytes 25067520 | tf_op jit(solution)/shard_map/all_gather | solution.py:2372
  8.2 1.2 copy-start.11
  9.3 1.1 copy-start.13
  9.4 1.1 copy-start.14
  9.4 1.2 copy-start.15
  9.4 1.3 copy-start.9
  9.5 1.3 copy-start.10
  9.5 1.3 copy-start.16
  9.5 1.3 copy-start.17
  9.5 1.3 copy-start.12
  10.5 3.1 copy-start.18
  10.5 3.1 copy-start.19
  10.6 3.1 copy-start.20
  10.6 3.1 copy-start.21
  10.6 3.7 copy-start
  10.6 3.7 copy-start.3
  10.6 3.7 copy-start.4
  10.6 3.7 copy-start.5
  10.7 3.0 copy-start.22
  10.7 3.0 copy-start.23
  10.7 3.0 copy-start.24
  10.7 3.0 copy-start.25
  10.9 1.1 copy-start.8
  12.0 354.2 %all-gather.4.cloned.1.call-start = ((), (), s32[]{:S(2)}) async-start(), calls=%async_computation | async-start | bytes 2506752 | tf_op jit(solution)/shard_map/all_gather | solution.py:2390
  90.3 1.4 copy-start.6
  91.7 5.4 %copy-start.7 = (bf16[768,768]{1,0:T(8,128)(2,1)}, bf16[768,768]{1,0:T(8,128)(2,1)S(1)}, u32[]{:S(2)}) copy-start(bf16[768,768]{1,0:T(8,128)(2,1)S(1)} %get-tuple-element.77.q_ref) | copy-start | bytes 3538948
  91.7 65.2 %copy-start.2 = (f32[16,768]{1,0:T(8,128)}, f32[16,768]{1,0:T(8,128)S(1)}, u32[]{:S(2)}) copy-start(f32[16,768]{1,0:T(8,128)S(1)} %get-tuple-element.80.gains_ref) | copy-start | bytes 147460
  92.7 4.4 %copy-start.26 = (s32[48]{0:T(128)S(1)}, s32[48]{0:T(128)}, u32[]{:S(2)}) copy-start(s32[48]{0:T(128)} %param.29) | copy-start | bytes 580
  172.2 1.0 copy-start.1
Sparse Core Ops, SparseCore 0:
  12.1 144.6 all-gather.5
  208.8 41.1 all-gather.3

commit v6 on v5

--- a/solution.py
+++ b/solution.py
@@ -2030,6 +2030,9 @@
     inner_ref,
     cross_key_ref,
     cross_value_ref,
+    embedded_ref,
+    loss_ref,
+    table_ref,
     grad_tokens_ref,
     vectors_ref,
     grad_self_value_ref,
@@ -2047,6 +2050,9 @@
     inner_sums_ref,
     attention_sums_ref,
     outer_sums_ref,
+    embedded_out,
+    loss_out,
+    table_out,
     pieces,
     grad_q_ref,
     grad_k_ref,
@@ -2083,6 +2089,19 @@
     ]
     for copy in copies:
         copy.start()
+    embedded_out[...] = embedded_ref[:seqs, :]
+    loss_out[...] = loss_ref[:1, :1]
+    buckets = table_out.shape[0]
+    bucket_row = lax.broadcasted_iota(jnp.int32, (8, LANES), 0)
+    bucket_column = lax.broadcasted_iota(jnp.int32, (8, LANES), 1)
+    own_buckets = (bucket_column == group * buckets + bucket_row).astype(wide)
+    table_out[...] = lax.dot_general(
+        own_buckets,
+        table_ref[...],
+        (((1,), (1,)), ((), ())),
+        precision=highest,
+        preferred_element_type=wide,
+    )[:buckets, :HEADS]
     copies[0].wait()
 
     def chooser(count, first):
@@ -2218,7 +2237,7 @@
         name="last",
         in_specs=[pl.BlockSpec(memory_space=pltpu.HBM)] * 12
         + [whole] * (len(arrays) - 12),
-        out_specs=[whole] * 17,
+        out_specs=[whole] * 20,
         out_shape=[
             jax.ShapeDtypeStruct((rows, width), wide),
             jax.ShapeDtypeStruct((8, 1, part), wide),
@@ -2237,6 +2256,9 @@
             jax.ShapeDtypeStruct((part, feeds * width), wide),
             square,
             jax.ShapeDtypeStruct((share, width), wide),
+            jax.ShapeDtypeStruct((seqs, width), wide),
+            jax.ShapeDtypeStruct((1, 1), wide),
+            jax.ShapeDtypeStruct((BUCKETS // groups, HEADS), wide),
         ],
         scratch_shapes=[
             pltpu.VMEM((width // LANES, groups * seqs * 2 * HEAD_ROWS, LANES), wide),
@@ -2385,8 +2407,6 @@
     embedded, loss, grad_context, decoder_rows, starts, decoder_totals = decoder_step(
         context, rest_blocks, base, gains, labels, place, groups, members, seqs
     )
-    contrastive_loss = loss[0, :1]
-    embedded = embedded[:seqs]
     decoder_rows = lax.all_gather(
         decoder_rows.reshape(seqs * 2 * HEAD_ROWS, width), "batch", axis=0, tiled=False
     )
@@ -2449,6 +2469,9 @@
         inner_sums,
         out_sums,
         outer_sums,
+        embedded,
+        loss,
+        grad_table,
     ) = last_step(
         groups,
         seqs,
@@ -2480,16 +2503,17 @@
         feed_inner,
         cross_key,
         cross_value,
+        embedded,
+        loss,
+        table_sums,
     )
     half_share = share // halves
     grad_second_inner = jnp.transpose(
         grad_second_inner.reshape(part, halves, groups, half_share), (0, 2, 1, 3)
     ).reshape(part, blocks * width)
     vectors = vectors.reshape(8, part)
-    own_buckets = BUCKETS // groups
-    grad_table = lax.dynamic_slice_in_dim(table_sums, group * own_buckets, own_buckets, 1)[:HEADS].T
     return (
-        contrastive_loss,
+        loss.reshape(1),
         embedded,
         grad_tokens,
         vectors[0],

time: 395 us -> 390 us (0.987)
  local copies, waits for them, and re-layouts: 24.8 us -> 20 us
  transfers between devices with their start and end apart: 2 -> 2, of which waited for: 1 -> 1; matrix products, arithmetic and copies ran while one was open for 4% -> 3% of each run, Pallas kernels for 68% -> 69%
where the time goes in v6:
time: 390 us; the launch traced here: 387 us
  Pallas kernels  328 us (84%)
  waiting for transfers between devices  21.9 us (6%)
  local copies, waits for them, and re-layouts  20 us (5%)
  between operations  15 us (4%)
    pallas_call x1, Pallas kernels, attend_back(): pl.pallas_call(functools.partial(attend_back_kernel, groups, members), na...  116 us
    pallas_call x1, Pallas kernels, project(): pl.pallas_call(functools.partial(first_kernel, groups, members), name='pr...  75.3 us
    pallas_call x1, Pallas kernels, feed_back(): pl.pallas_call(functools.partial(feed_back_kernel, base, groups, members)...  39.9 us
    pallas_call x1, Pallas kernels, attend(): pl.pallas_call(attend_kernel, name='attend', grid=(pairs,), in_specs=[pl....  34.4 us
    pallas_call x1, Pallas kernels, decoder_step(): pl.pallas_call(functools.partial(decoder_kernel, base, groups, members, s...  32.8 us
    all_gather x1, waiting for transfers between devices, shards(): rest = lax.all_gather(rest_part, 'batch', axis=0, tiled=False)  21.9 us
    pallas_call x1, Pallas kernels, feed_forward(): pl.pallas_call(feed_kernel, name='feed_forward', in_specs=[whole, whole,...  15.4 us
    pallas_call x1, Pallas kernels, last_step(): pl.pallas_call(functools.partial(last_kernel, groups, seqs, halves), name...  13.5 us
  transfers between devices with their start and end apart: 2, of which 1 were waited for; matrix products, arithmetic and copies ran while one was open for 3% of the time, Pallas kernels for 69%

profile of v6, /device:TPU:0, one launch (start us, length us, event | category | flops | bytes accessed | tf_op | source)
XLA Modules:
  0.0 386.8 jit_solution(8408652505950412032)
XLA Ops:
  7.3 1.5 reshape.146
  8.8 0.1 constant_dynamic-slice_fusion
  8.9 0.3 reshape_reshape.3
  9.4 0.1 pad_maximum_fusion
  9.6 0.6 copy-done.14
  10.6 1.1 copy-done.8
  11.8 0.1 reshape.142
  12.0 0.3 dynamic_update_slice.6
  12.3 0.2 dynamic_update_slice.7.extra_ref
  12.5 75.3 %project.1 = (bf16[768,768]{1,0:T(8,128)(2,1)S(1)}, bf16[1536,768]{1,0:T(8,128)(2,1)S(1)}, bf16[1536,768]{1,0:T(8,128)(2,1)}, bf16[1536,768]{1,0:T(8,128)(2,1)},...) custom-call(bf16[768,768]{1,0:T(8,128)(2,1)S(1)} %copy-done, bf16[16,768]{1,0:T(8,128)(2,1)S(1)} %dynamic_update_slice.7.extra_ref, ...), custom_call_target="tpu_custom_call" | custom-call | flops 2147483648 | bytes 37748736 | tf_op jit(solution)/shard_map/project/pallas_call | solution.py:365
  87.9 1.4 copy-done.6
  89.3 0.1 convert_element_type.59
  89.4 0.2 fusion
  89.6 0.7 broadcast_in_dim.22.near_ref
  90.3 0.2 reduce-window.4
  90.5 4.3 %copy.69 = bf16[1536,768]{0,1:T(8,128)(2,1)} copy(bf16[1536,768]{1,0:T(8,128)(2,1)} %get-tuple-element.94) | data formatting | bytes 4718592 | tf_op jit(solution)/shard_map/project/pallas_call | solution.py:365
  94.8 0.6 pad.4.target_ref
  95.4 0.6 fusion.13
  96.0 1.9 pad_add_fusion.place
  97.9 2.4 dynamic-slice_bitcast_fusion.own_turned_ref
  100.3 34.4 %attend.1 = (f32[768,768]{1,0:T(8,128)}, f32[768,128]{1,0:T(8,128)}) custom-call(s32[4]{0:T(128)} %pad_add_fusion.place, bf16[768,768]{1,0:T(8,128)(2,1)} %copy-done.7, bf16[1536,768]{1,0:T(8,128)(2,1)} %copy-done.6, bf16[1536,768]{1,0:T(8,128)(2,1)} %get-tuple-element.82.v_ref, f32[12,1,768]{2,1,0:T(1,128)} %broadcast_in_dim.22.near_ref), custom_call_target="tpu_custom_call" | custom-call | flops 14495514624 | bytes 18874368 | tf_op jit(solution)/shard_map/attend/pallas_call | solution.py:469
  134.7 21.9 %all-gather.6.cloned.1.call-done = bf16[15360,768]{1,0:T(8,128)(2,1)} async-done(((bf16[960,768]{1,0:T(8,128)(2,1)}), bf16[15360,768]{1,0:T(8,128)(2,1)}) %all-gather.6.cloned.1.call-update) | async-done | bytes 23592976 | tf_op jit(solution)/shard_map/all_gather | solution.py:2394
  156.6 15.4 %feed_forward.1 = (f32[768,768]{1,0:T(8,128)}, bf16[4,768,768]{2,1,0:T(8,128)(2,1)}, f32[768,768]{1,0:T(8,128)}, bf16[768,768]{1,0:T(8,128)(2,1)S(1)}) custom-call(f32[768,768]{1,0:T(8,128)} %get-tuple-element.84.attended_ref, bf16[768,768]{1,0:T(8,128)(2,1)S(1)} %copy-done, bf16[16,960,768]{2,1,0:T(8,128)(2,1)} %bitcast.52, ...), custom_call_target="tpu_custom_call" | custom-call | flops 8153726976 | bytes 23592960 | tf_op jit(solution)/shard_map/feed_forward/pallas_call | solution.py:1245
  171.9 1.0 copy-done.1
  173.0 32.8 %decoder.1 = (f32[8,768]{1,0:T(8,128)}, f32[8,128]{1,0:T(8,128)}, f32[768,768]{1,0:T(8,128)}, bf16[3,32,768]{2,1,0:T(8,128)(2,1)}, f32[8,768]{1,0:T(8,128)}, /*index=5*/f32[24,768]{1,0:T(8,128)}) custom-call(s32[4]{0:T(128)} %pad_add_fusion.place, bf16[768,768]{1,0:T(8,128)(2,1)} %copy-done.1, bf16[16,960,768]{2,1,0:T(8,128)(2,1)} %bitcast.53, ...), custom_call_target="tpu_custom_call" | custom-call | flops 353894400 | bytes 23592960 | tf_op jit(solution)/shard_map/decoder/pallas_call | solution.py:913
  205.8 39.9 %feed_back.1 = (bf16[4,2,2,9,48,768]{5,4,3,2,1,0:T(8,128)(2,1)}, f32[768,768]{1,0:T(8,128)}, bf16[768,768]{1,0:T(8,128)(2,1)}, f32[24,768]{1,0:T(8,128)}, f32[8,768]{1,0:T(8,128)}) custom-call(f32[768,768]{1,0:T(8,128)} %get-tuple-element.86.grad_context_ref, f32[768,768]{1,0:T(8,128)} %get-tuple-element.87.encoded_ref, ...), custom_call_target="tpu_custom_call" | custom-call | flops 16307453952 | bytes 47185920 | tf_op jit(solution)/shard_map/feed_back/pallas_call | solution.py:1479
  245.7 116.2 %attend_back.1 = (bf16[768,768]{1,0:T(8,128)(2,1)}, bf16[768,768]{1,0:T(8,128)(2,1)}, bf16[768,768]{1,0:T(8,128)(2,1)}, f32[16,128]{1,0:T(8,128)}, f32[48,768]{1...) custom-call(s32[4]{0:T(128)} %pad_add_fusion.place, ...), custom_call_target="tpu_custom_call" | custom-call | flops 36238786560 | bytes 18874368 | tf_op jit(solution)/shard_map/attend_back/pallas_call | solution.py:1927
  361.9 13.5 %last.1 = (f32[768,768]{1,0:T(8,128)}, f32[8,1,48]{2,1,0:T(1,128)}, f32[48,768]{1,0:T(8,128)}, f32[48,768]{1,0:T(8,128)}, f32[48,768]{1,0:T(8,128)}, /*index=5*/...) custom-call(bf16[768,768]{1,0:T(8,128)(2,1)} %get-tuple-element.96.g, ...), custom_call_target="tpu_custom_call" | custom-call | tf_op jit(solution)/shard_map/last/pallas_call | solution.py:2235
  375.5 1.4 reshape.150
  376.9 0.4 copy.71
  377.3 1.9 reshape.151
  379.2 0.5 slice_bitcast_fusion
  (82 shorter events, 0.6 us)
Async XLA Ops:
  7.2 2.1 copy-start.9
  7.2 2.1 copy-start.19
  7.2 2.1 copy-start.12
  7.2 149.3 %all-gather.6.cloned.1.call-start = ((), (), s32[]{:S(2)}) async-start(), calls=%async_computation.1 | async-start | bytes 25067520 | tf_op jit(solution)/shard_map/all_gather | solution.py:2394
  9.4 1.0 copy-start.16
  9.4 1.0 copy-start.10
  9.4 1.1 copy-start.11
  9.4 1.1 copy-start.17
  9.4 1.1 copy-start.18
  9.5 1.1 copy-start.13
  10.2 1.5 copy-start.29
  10.2 1.6 copy-start.21
  10.2 1.6 copy-start.22
  10.3 1.6 copy-start.23
  10.3 1.6 copy-start.24
  10.3 1.6 copy-start.25
  10.3 1.6 copy-start.26
  10.3 1.6 copy-start.27
  10.3 1.6 copy-start.28
  10.4 2.1 copy-start
  10.4 2.1 copy-start.3
  10.4 2.1 copy-start.4
  10.4 2.1 copy-start.5
  10.6 1.1 copy-start.8
  11.7 350.2 %all-gather.4.cloned.1.call-start = ((), (), s32[]{:S(2)}) async-start(), calls=%async_computation | async-start | bytes 2506752 | tf_op jit(solution)/shard_map/all_gather | solution.py:2410
  12.5 77.8 %copy-start.30 = (s32[1,3]{1,0:T(1,128)S(1)}, s32[1,3]{1,0:T(1,128)}, u32[]{:S(2)}) copy-start(s32[1,3]{1,0:T(1,128)} %param.28) | copy-start | bytes 40
  87.9 1.4 copy-start.6
  89.3 5.5 %copy-start.7 = (bf16[768,768]{1,0:T(8,128)(2,1)}, bf16[768,768]{1,0:T(8,128)(2,1)S(1)}, u32[]{:S(2)}) copy-start(bf16[768,768]{1,0:T(8,128)(2,1)S(1)} %get-tuple-element.80.q_ref) | copy-start | bytes 3538948
  89.3 67.3 %copy-start.2 = (f32[16,768]{1,0:T(8,128)}, f32[16,768]{1,0:T(8,128)S(1)}, u32[]{:S(2)}) copy-start(f32[16,768]{1,0:T(8,128)S(1)} %get-tuple-element.83.gains_ref) | copy-start | bytes 147460
  90.5 4.3 %copy-start.31 = (s32[48]{0:T(128)S(1)}, s32[48]{0:T(128)}, u32[]{:S(2)}) copy-start(s32[48]{0:T(128)} %param.29) | copy-start | bytes 580
  171.9 1.0 copy-start.1
  376.9 2.3 copy-start.20
  (2 other events, 1.8 us)
Sparse Core Ops, SparseCore 0:
  11.8 144.6 all-gather.5
  205.9 41.1 all-gather.3
